TPU v7x, 32 devices: a whole 2x2x4 slice. The times are simulated.
32 devices in a mesh: grp: 2 (over y), sec: 4 (over z), op: 2 (over x), rep: 2 (over core).
Axes of the slice: x: 2, y: 2, z: 4, core: 2. Of those that a mesh axis runs over, the one named last changes fastest.
Arguments:
- psi: bfloat16 [32, 256, 256], P(('grp', 'sec'), 'rep'), parts along dimension 0, may hold values from -6 to 6
- left_env: bfloat16 [32, 16, 256, 256], P(('grp', 'op'), 'sec', 'rep'), parts along dimension 0, may hold values from -0.09375 to 0.09375
- right_env: bfloat16 [32, 256, 256], P(('grp', 'op')), parts along dimension 0, may hold values from -0.375 to 0.375
- pairing: int32 [32, 16], P(('grp', 'op'), 'sec'), parts along dimension 0, may hold values from 0 to 15, as said below
- block_rows: int32 [32], P(('grp', 'sec')), parts along dimension 0, may hold values from 64 to 256, as said below
- block_cols: int32 [32], P(('grp', 'sec')), parts along dimension 0, may hold values from 64 to 256, as said below
- energy: float32 [32, 256], P(('grp', 'sec'), 'rep'), parts along dimension 0, may hold values from 1 to 4
Outputs:
- sigma_first: bfloat16 [32, 256, 256], P(('grp', 'sec'), 'rep'), parts along dimension 0
- sigma_second: bfloat16 [32, 256, 256], P(('grp', 'sec'), 'rep'), parts along dimension 0
There are 2 independent parts, one for each index of `grp`. A program takes and returns all parts, laid end to end along the dimension named above; each array names one. Nothing has to cross between parts.
Inputs may be any that keep to these rules, and one draw needn't show every extreme that they name: `pairing`: the 8 x 4 entries of one op index and one sec index name sectors of any one sec index at most 9 times, and all of them that name sectors of one sec index name the same sector; in every op index some sec index is named exactly 9 times from every sec index. `block_rows`: some sector has exactly 256 live rows. `block_cols`: some sector has exactly 256 live columns.
All inputs are finite; a program needn't handle non-finite values.
Results may differ from a plain program's by a relative error of at most 0.0085.
Values may be sent and summed in bfloat16 or wider, within the bound.
No kernel may reach another device: no remote copies, remote signals or barrier semaphores. Data moves between devices by JAX's collectives and lax.ppermute only.
A program may use at most 64 MiB of HBM per device.

v0:
```python
import functools

import jax
import jax.numpy as jnp
from jax import lax
from jax.experimental import pallas as pl
from jax.experimental.pallas import tpu as pltpu
from jax.sharding import PartitionSpec as P

EPSILON = 1e-06
HEAD = 8
PARTS = 3
EARLY_FLOPS = 10**9
MORE_ROWS = 16
LANES = 128
VMEM_BYTES = 24 * 1024 * 1024
F32 = jnp.float32
BF16 = jnp.bfloat16


def whole(space):
    return pl.BlockSpec(memory_space=space)


def live(limit_ref, s, first_row, shape):
    sec_dev = limit_ref.shape[0] // 2
    repeat = shape[1] // LANES
    rows = jnp.concatenate([limit_ref[s:s + 1, :]] * repeat, axis=1)
    cols = jnp.concatenate([limit_ref[sec_dev + s:sec_dev + s + 1, :]] * repeat, axis=1)
    row_ids = first_row + lax.broadcasted_iota(jnp.int32, shape, 0)
    col_ids = lax.broadcasted_iota(jnp.int32, shape, 1)
    return (row_ids < rows) & (col_ids < cols)


def energy_columns(level):
    missing = -level.shape[0] % 8
    if missing:
        level = jnp.concatenate([level, jnp.zeros((missing, level.shape[1]), F32)], axis=0)
    return level.T


def spread(array, width):
    return jnp.concatenate([array] * (width // LANES), axis=1)


def quotient(value, count):
    return value >> (count.bit_length() - 1) if count & (count - 1) == 0 else lax.div(value, count)


def remainder(value, count):
    return value & (count - 1) if count & (count - 1) == 0 else lax.rem(value, count)


def fold(array):
    rows, width = array.shape
    return jnp.sum(array.reshape(rows // 8, 8, width), axis=0)


def total(array):
    return jnp.sum(jnp.sum(array, axis=0, keepdims=True), axis=1, keepdims=True)


def header(slot, scalars, shape=(HEAD, LANES)):
    row_ids = lax.broadcasted_iota(jnp.int32, shape, 0)
    head = jnp.where(row_ids == 0, slot.astype(F32), 0.0)
    row = 1
    for scalar in scalars:
        rest = jnp.broadcast_to(scalar, shape)
        for _ in range(PARTS):
            piece = rest.astype(BF16).astype(F32)
            head = jnp.where(row_ids == row, piece, head)
            rest = rest - piece
            row += 1
    return head.astype(BF16)


def head_scalar(head_sum, index):
    first = 1 + PARTS * index
    return jnp.sum(head_sum[first:first + PARTS], axis=0, keepdims=True)


def most_pairs(pairs, sec_count):
    return pairs // sec_count + 1


def load_kernel(
    psi_hbm, left_hbm, pairing_hbm, rows_hbm, cols_hbm, energy_hbm,
    start_ref, left_ref, list_ref, limit_ref, energy_ref, scalar_ref,
    psi_ref, level_ref, rows_ref, cols_ref, pairing_ref, entry_ref, count_ref, sems,
):
    sec_dev, half, width = psi_ref.shape
    terms = left_ref.shape[0]
    sec_count = list_ref.shape[0]
    cap = most_pairs(terms * sec_dev, sec_count)
    pairs = [
        (rows_hbm, rows_ref), (cols_hbm, cols_ref), (energy_hbm, level_ref),
        (pairing_hbm, pairing_ref), (psi_hbm, psi_ref),
    ]
    for t in range(left_ref.shape[0]):
        pairs.append((left_hbm.at[t], left_ref.at[t]))
    copies = [
        pltpu.make_async_copy(source, target, sems.at[i])
        for i, (source, target) in enumerate(pairs)
    ]
    for copy in copies:
        copy.start()
    for owner in range(sec_count):
        count_ref[owner] = 0
        entry_ref[owner, cap] = 0
        for i in range(cap):
            entry_ref[owner, i] = terms * sec_dev
    for copy in copies[:3]:
        copy.wait()
    for s in range(sec_dev):
        limit_ref[s:s + 1, :] = jnp.full((1, LANES), rows_ref[s], jnp.int32)
        limit_ref[sec_dev + s:sec_dev + s + 1, :] = jnp.full((1, LANES), cols_ref[s], jnp.int32)
    columns = energy_columns(level_ref[...])
    for s in range(sec_dev):
        energy_ref[s] = jnp.broadcast_to(columns[:, s:s + 1], (half, LANES))
    copies[3].wait()
    for t in range(terms):
        for s in range(sec_dev):
            target = pairing_ref[s, t]
            owner = quotient(target, sec_dev)
            count = count_ref[owner]
            entry_ref[owner, count] = t * sec_dev + s
            entry_ref[owner, cap] = remainder(target, sec_dev)
            count_ref[owner] = count + 1
    entries = pltpu.make_async_copy(entry_ref, list_ref, sems.at[len(copies)])
    entries.start()
    copies[4].wait()
    first_row = lax.axis_index("rep") * half
    norm = jnp.zeros((8, width), F32)
    level = jnp.zeros((8, width), F32)
    for s in range(sec_dev):
        vector = jnp.where(
            live(limit_ref, s, first_row, (half, width)), psi_ref[s].astype(F32), 0.0
        )
        start_ref[s] = vector.astype(BF16)
        square = vector * vector
        norm += fold(square)
        level += fold(square * spread(energy_ref[s], width))
    scalar_ref[0:8, :] = norm
    scalar_ref[8:16, :] = level
    for copy in copies[5:]:
        copy.wait()
    entries.wait()


def product_kernel(is_first, split, paired, rep_count, sec_count, *refs):
    refs = list(refs)
    take = lambda count: [refs.pop(0) for _ in range(count)]
    list_ref, left_ref, right_ref = take(3)
    if is_first:
        start_ref, limit_ref, scalar_ref = take(3)
        psi_refs = take(rep_count - 1)
        level_refs = take(rep_count - 1)
    else:
        vector_refs = take(rep_count)
    out_refs = take(sec_count if split else 1)
    inner_ref, entry_ref, sem = refs
    terms, sec_dev, half, width = left_ref.shape
    pairs = terms * sec_dev
    cap = most_pairs(pairs, sec_count)
    rep = lax.axis_index("rep")
    sec = lax.axis_index("sec")
    fetch = pltpu.make_async_copy(list_ref, entry_ref, sem)
    fetch.start()
    inner_ref[pairs] = jnp.zeros((half, width), BF16)

    def first_row(step):
        return remainder(rep + step, rep_count) * half

    if is_first:
        folded = [scalar_ref[0:8, :], scalar_ref[8:16, :]]
        columns = [energy_columns(ref[...]) for ref in level_refs]
    for s in range(sec_dev):
        if is_first:
            blocks = [start_ref[s]]
            for step in range(1, rep_count):
                psi = psi_refs[step - 1][s]
                mask = live(limit_ref, s, first_row(step), (half, width))
                blocks.append(jnp.where(mask, psi.astype(F32), 0.0).astype(BF16))
        else:
            blocks = [ref[s * half:(s + 1) * half] for ref in vector_refs]
        vector = jnp.concatenate(blocks, axis=0)
        for turn in range(1, rep_count):
            turned = blocks[rep_count - turn:] + blocks[:rep_count - turn]
            vector = jnp.where(rep == turn, jnp.concatenate(turned, axis=0), vector)
        inner = jnp.dot(
            left_ref[:, s].reshape(terms * half, width), vector, preferred_element_type=F32
        ).astype(BF16)
        for t in range(terms):
            inner_ref[t * sec_dev + s] = inner[t * half:(t + 1) * half]
        if is_first:
            for step in range(1, rep_count):
                block = blocks[step].astype(F32)
                square = block * block
                energy = jnp.broadcast_to(columns[step - 1][:, s:s + 1], (half, width))
                folded = [folded[0] + fold(square), folded[1] + fold(square * energy)]
    if is_first:
        scalars = [total(array) for array in folded]
    else:
        head = sum(ref[sec_dev * half:].astype(F32) for ref in vector_refs)
        scalars = [head_scalar(head, i)[:, :LANES] for i in range(2)]
    fetch.wait()
    for d in range(sec_count):
        if not split:
            owner = d
        elif paired:
            owner = sec ^ d
        else:
            owner = remainder(sec + d, sec_count)
        packet = jnp.zeros((half, width), F32)
        for i in range(cap):
            pair = entry_ref[owner, i]
            term = jnp.minimum(quotient(pair, sec_dev), terms - 1)
            packet += jnp.dot(inner_ref[pair], right_ref[term], preferred_element_type=F32)
        out = out_refs[d] if split else out_refs[0].at[d]
        for column in range(width // LANES):
            out[column * half:(column + 1) * half, :] = packet[
                :, column * LANES:(column + 1) * LANES
            ].astype(BF16)
        out[width // LANES * half:, :] = header(entry_ref[owner, cap], scalars)


def sigma_packets(is_first, split, paired, rep_count, lists, left_env, right_env, more):
    terms, sec_dev, half, width = left_env.shape
    sec_count = lax.axis_size("sec")
    packet = (width // LANES * half + HEAD, LANES)
    if split:
        outs = [jax.ShapeDtypeStruct(packet, BF16)] * sec_count
    else:
        outs = [jax.ShapeDtypeStruct((sec_count,) + packet, BF16)]
    pair_flops = 2 * half * width * width * 2
    operands = [lists, left_env, right_env, *more]
    return pl.pallas_call(
        functools.partial(product_kernel, is_first, split, paired, rep_count, sec_count),
        out_shape=outs,
        in_specs=[whole(pltpu.VMEM)] * len(operands),
        out_specs=[whole(pltpu.VMEM)] * len(outs),
        scratch_shapes=[
            pltpu.VMEM((terms * sec_dev + 1, half, width), BF16),
            pltpu.SMEM(lists.shape, jnp.int32),
            pltpu.SemaphoreType.DMA,
        ],
        compiler_params=pltpu.CompilerParams(vmem_limit_bytes=VMEM_BYTES),
        cost_estimate=pl.CostEstimate(
            flops=terms * sec_dev * pair_flops,
            bytes_accessed=2 * (left_env.size + right_env.size),
            transcendentals=0,
        ),
        name="products_first" if is_first else "products_second",
    )(*operands)


def exchange(packets, split, paired, order, together):
    sec_count = lax.axis_size("sec")
    op_count = lax.axis_size("op")
    op_turns = [
        [(i, (i + step) % op_count) for i in range(op_count)] for step in range(1, op_count)
    ]
    over_op = lambda packet: [lax.ppermute(packet, "op", turn) for turn in op_turns]
    if not split:
        arrived = lax.all_to_all(packets[0], "sec", split_axis=0, concat_axis=0, tiled=True)
        return [arrived] + over_op(arrived), []
    arrived = {0: packets[0]}
    for step in order:
        reach = (lambda i: i ^ step) if paired else (lambda i: (i + step) % sec_count)
        turn = [(i, reach(i)) for i in range(sec_count)]
        arrived[step] = lax.ppermute(packets[step], "sec", turn)
    steps = [0, *order]
    alone = steps[:len(steps) - together]
    crossed = sum([over_op(arrived[step]) for step in alone], [])
    waiting = [arrived[step] for step in steps[len(alone):]]
    last = jnp.stack(waiting)
    return [arrived[step] for step in steps] + crossed, over_op(last)


def add_packets(packet_refs, split, half, base_ref):
    sec_dev, _, width = base_ref.shape
    own = lax.axis_size("sec") if split else 1
    body_rows = width // LANES * half
    if split:
        heads = [ref[body_rows:].astype(F32) for ref in packet_refs]
        for column in range(width // LANES):
            lanes = slice(column * LANES, (column + 1) * LANES)
            for s in range(sec_dev):
                part = base_ref[s, :, lanes]
                for ref, head in zip(packet_refs, heads):
                    body = ref[column * half:(column + 1) * half].astype(F32)
                    part += jnp.where(head[0:1] == s, body, 0.0)
                base_ref[s, :, lanes] = part
        return sum(heads[1:own], heads[0])

    head_sum = jnp.zeros((HEAD, LANES), F32)
    for index, ref in enumerate(packet_refs):
        def add_one(p, carry):
            head = ref[p, body_rows:, :].astype(F32)
            for column in range(width // LANES):
                body = ref[p, column * half:(column + 1) * half, :].astype(F32)
                lanes = slice(column * LANES, (column + 1) * LANES)
                for s in range(sec_dev):
                    base_ref[s, :, lanes] += jnp.where(head[0:1] == s, body, 0.0)
            return carry + head
        result = lax.fori_loop(0, ref.shape[0], add_one, jnp.zeros((HEAD, LANES), F32))
        if index < own:
            head_sum = head_sum + result
    return head_sum


def late_sum(packet_refs, s, half, width):
    body_rows = width // LANES * half
    value = jnp.zeros((half, width), F32)
    for ref in packet_refs:
        for i in range(ref.shape[0]):
            body = jnp.concatenate(
                [ref[i, c * half:(c + 1) * half].astype(F32) for c in range(width // LANES)],
                axis=1,
            )
            slot = spread(ref[i, body_rows:].astype(F32)[0:1], width)
            value += jnp.where(slot == s, body, 0.0)
    return value


def first_early_kernel(split, count, *refs):
    packet_refs = refs[:count]
    start_ref, energy_ref, base_ref, scalar_ref = refs[count:]
    sec_dev, half, width = start_ref.shape
    for s in range(sec_dev):
        base_ref[s] = spread(energy_ref[s], width) * start_ref[s].astype(F32)
    head_sum = add_packets(packet_refs, split, half, base_ref)
    norm = head_scalar(head_sum, 0)
    scalar_ref[0:1] = norm
    scalar_ref[1:2] = head_scalar(head_sum, 1) / norm


def first_kernel(count, *refs):
    packet_refs = refs[:count]
    limit_ref, start_ref, base_ref, scalar_ref, first_ref, one_ref, vec_ref = refs[count:]
    sec_dev, half, width = start_ref.shape
    shift = spread(scalar_ref[1:2], width)
    first_row = lax.axis_index("rep") * half
    cross = jnp.zeros((8, width), F32)
    square = jnp.zeros((8, width), F32)
    for s in range(sec_dev):
        mask = live(limit_ref, s, first_row, (half, width))
        start = start_ref[s].astype(F32)
        one = jnp.where(mask, base_ref[s] + late_sum(packet_refs, s, half, width), 0.0)
        one_ref[s] = one
        first_ref[s] = one.astype(BF16)
        vector = one - shift * start
        vec_ref[s * half:(s + 1) * half] = vector.astype(BF16)
        cross += fold(start * vector)
        square += fold(vector * vector)
    scalars = (total(cross), total(square))
    vec_ref[sec_dev * half:] = header(jnp.int32(0), scalars, (MORE_ROWS, width))


def second_early_kernel(split, count, entries, *refs):
    packet_refs = refs[:count]
    vec_ref, energy_ref, one_ref, scalar_ref, base_ref, scale_ref = refs[count:]
    sec_dev, half, width = one_ref.shape
    for s in range(sec_dev):
        vector = vec_ref[s * half:(s + 1) * half].astype(F32)
        base_ref[s] = spread(energy_ref[s], width) * vector
    head_sum = add_packets(packet_refs, split, half, base_ref)
    cross = head_scalar(head_sum, 0)
    square = head_scalar(head_sum, 1)
    excess = cross / scalar_ref[0:1]
    resid_sq = jnp.maximum(square - excess * cross, 0.0)
    scale = lax.rsqrt(resid_sq / entries + EPSILON)
    scale_ref[...] = jnp.broadcast_to(scale, scale_ref.shape)
    for s in range(sec_dev):
        base_ref[s] = base_ref[s] - spread(excess, width) * one_ref[s]


def second_kernel(count, *refs):
    packet_refs = refs[:count]
    limit_ref, base_ref, scale_ref, second_ref = refs[count:]
    sec_dev, half, width = base_ref.shape
    scale = spread(scale_ref[0:1], width)
    first_row = lax.axis_index("rep") * half
    for s in range(sec_dev):
        mask = live(limit_ref, s, first_row, (half, width))
        value = scale * (base_ref[s] + late_sum(packet_refs, s, half, width))
        second_ref[s] = jnp.where(mask, value, 0.0).astype(BF16)


def call(kernel, name, outs, *operands, flops=0):
    return pl.pallas_call(
        kernel,
        out_shape=outs,
        in_specs=[whole(pltpu.VMEM)] * len(operands),
        out_specs=[whole(pltpu.VMEM)] * len(outs),
        compiler_params=pltpu.CompilerParams(vmem_limit_bytes=VMEM_BYTES),
        cost_estimate=pl.CostEstimate(flops=flops, bytes_accessed=0, transcendentals=0),
        name=name,
    )(*operands)


def body(psi, left_env, right_env, pairing, block_rows, block_cols, energy):
    sec_count = lax.axis_size("sec")
    op_count = lax.axis_size("op")
    rep_count = lax.axis_size("rep")
    terms, sec_dev, half, width = left_env.shape
    entries = sec_count * sec_dev * rep_count * half * width
    split = sec_count * op_count <= 8
    can_pair = sec_count & (sec_count - 1) == 0
    steps = list(range(1, sec_count))
    first_plan = (False, steps, 2)
    second_plan = (can_pair, steps[1:2] + steps[:1] + steps[2:], 1)
    params = pltpu.CompilerParams(vmem_limit_bytes=VMEM_BYTES)
    vec_shape = (sec_dev, half, width)
    vec_bf16 = jax.ShapeDtypeStruct(vec_shape, BF16)

    def from_others(array):
        arrays = []
        for step in range(1, rep_count):
            turn = [((i + step) % rep_count, i) for i in range(rep_count)]
            arrays.append(lax.ppermute(array, "rep", turn))
        return arrays

    psi_others = from_others(psi)
    level_others = from_others(energy)
    start, left_env, lists, limits, levels, scalars = pl.pallas_call(
        load_kernel,
        out_shape=[
            vec_bf16,
            jax.ShapeDtypeStruct(left_env.shape, BF16),
            jax.ShapeDtypeStruct((sec_count, LANES), jnp.int32),
            jax.ShapeDtypeStruct((2 * sec_dev, LANES), jnp.int32),
            jax.ShapeDtypeStruct((sec_dev, half, LANES), F32),
            jax.ShapeDtypeStruct((16, width), F32),
        ],
        in_specs=[whole(pltpu.HBM)] * 6,
        out_specs=[whole(pltpu.VMEM)] * 6,
        scratch_shapes=[
            pltpu.VMEM(vec_shape, BF16),
            pltpu.VMEM((sec_dev, half), F32),
            pltpu.SMEM((sec_dev,), jnp.int32),
            pltpu.SMEM((sec_dev,), jnp.int32),
            pltpu.SMEM((sec_dev, terms), jnp.int32),
            pltpu.SMEM((sec_count, LANES), jnp.int32),
            pltpu.SMEM((sec_count,), jnp.int32),
            pltpu.SemaphoreType.DMA((6 + terms,)),
        ],
        compiler_params=params,
        name="load",
    )(*(
        pltpu.with_memory_space_constraint(array, pltpu.HBM)
        for array in (psi, left_env, pairing.T, block_rows, block_cols, energy)
    ))

    block_f32 = jax.ShapeDtypeStruct(vec_shape, F32)
    row_f32 = jax.ShapeDtypeStruct((8, LANES), F32)

    packets = sigma_packets(
        True, split, first_plan[0], rep_count, lists, left_env, right_env,
        [start, limits, scalars, *psi_others, *level_others],
    )
    early, late = exchange(packets, split, *first_plan)
    base, scalars = call(
        functools.partial(first_early_kernel, split, len(early)), "combine_first_early",
        [block_f32, row_f32], *early, start, levels, flops=EARLY_FLOPS,
    )
    first_out, sigma_one, vector = call(
        functools.partial(first_kernel, len(late)), "combine_first",
        [
            pltpu.VMEM(vec_shape, BF16),
            block_f32,
            jax.ShapeDtypeStruct((sec_dev * half + MORE_ROWS, width), BF16),
        ],
        *late, limits, start, base, scalars,
    )

    packets = sigma_packets(
        False, split, second_plan[0], rep_count, lists, left_env, right_env,
        [vector, *from_others(vector)],
    )
    early, late = exchange(packets, split, *second_plan)
    base, scale = call(
        functools.partial(second_early_kernel, split, len(early), entries),
        "combine_second_early", [block_f32, row_f32], *early, vector, levels, sigma_one, scalars,
    )
    (second_out,) = call(
        functools.partial(second_kernel, len(late)), "combine_second", [vec_bf16],
        *late, limits, base, scale,
    )
    return (first_out, second_out)


def solution(mesh):
    return jax.shard_map(
        body,
        mesh=mesh,
        in_specs=(
            P(("grp", "sec"), "rep", None),
            P(("grp", "op"), "sec", "rep", None),
            P(("grp", "op"), None, None),
            P(("grp", "op"), "sec"),
            P(("grp", "sec")),
            P(("grp", "sec")),
            P(("grp", "sec"), "rep"),
        ),
        out_specs=(P(("grp", "sec"), "rep", None), P(("grp", "sec"), "rep", None)),
        check_vma=False,
    )
```

profile of v0, /device:TPU:0, one launch (start us, length us, event | category | flops | bytes accessed | tf_op | source)
XLA Modules:
  0.0 38.9 jit_solution(3115307027677351195)
XLA Ops:
  0.6 0.0 copy-start
  0.6 0.5 %collective-permute-start = (bf16[4,128,256]{2,1,0:T(8,128)(2,1)}, bf16[4,128,256]{2,1,0:T(8,128)(2,1)S(1)}, u32[]{:S(2)}, u32[]{:S(2)}) collective-permute-start(bf16[4,128,256]{2,1,0:T(8,128)(2,1)} %psi_hbm.1), channel_id=1, source_target_pairs={{1,0},{0,1},{3,2},{2,3},{5,4},{4,5},{7,6},{6,7},{9,8},{8,9},{11,10... | collective-permute-start | bytes 786440 | tf_op jit(solution)/shard_map/ppermute | solution.py:421
  1.2 0.1 collective-permute-start.1
  1.2 1.8 %load.1 = (bf16[4,128,256]{2,1,0:T(8,128)(2,1)S(1)}, bf16[8,4,128,256]{3,2,1,0:T(8,128)(2,1)S(1)}, s32[4,128]{1,0:T(4,128)S(1)}, s32[8,128]{1,0:T(8,128)S(1)}, f...) custom-call(bf16[4,128,256]{2,1,0:T(8,128)(2,1)} %psi_hbm.1, bf16[8,4,128,256]{3,2,1,0:T(8,128)(2,1)} %left_hbm.1, ...), custom_call_target="tpu_custom_call" | custom-call | tf_op jit(solution)/shard_map/load/pallas_call | solution.py:426
  3.1 0.0 collective-permute-done.1.refs_7_
  3.1 0.0 collective-permute-done.refs_6_
  3.1 0.0 copy-done
  3.1 1.6 %products_first.1 = (bf16[264,128]{1,0:T(8,128)(2,1)S(1)}, bf16[264,128]{1,0:T(8,128)(2,1)S(1)}, bf16[264,128]{1,0:T(8,128)(2,1)S(1)}, bf16[264,128]{1,0:T(8,128)(2,1)S(1)}) custom-call(s32[4,128]{1,0:T(4,128)S(1)} %get-tuple-element.23.refs_0_, bf16[8,4,128,256]{3,2,1,0:T(8,128)(2,1)S(1)} %get-tuple-element.24.refs_1_, bf16[8,256,256]{2,1,0:T(8,128)(2,1)S(1)} %copy-done, ...), custom_call_target="tpu_custom_call" | custom-call | flops 1073741824 | bytes 3145728 | tf_op jit(solution)/shard_map/products_first/pallas_call | solution.py:237
  4.7 3.1 %collective-permute-start.5 = (bf16[264,128]{1,0:T(8,128)(2,1)S(1)}, bf16[264,128]{1,0:T(8,128)(2,1)S(1)}, u32[]{:S(2)}, u32[]{:S(2)}) collective-permute-start(bf16[264,128]{1,0:T(8,128)(2,1)S(1)} %get-tuple-element.31), channel_id=1, source_target_pairs={{0,4},{4,8},{8,12},{12,0},{1,5},{5,9},{9,13},{13,1},{2,6},{6,10},{... | collective-permute-start | bytes 202760 | tf_op jit(solution)/shard_map/ppermute | solution.py:271
  7.8 2.6 %collective-permute-start.2 = (bf16[264,128]{1,0:T(8,128)(2,1)S(1)}, bf16[264,128]{1,0:T(8,128)(2,1)S(1)}, u32[]{:S(2)}, u32[]{:S(2)}) collective-permute-start(bf16[264,128]{1,0:T(8,128)(2,1)S(1)} %get-tuple-element.28), channel_id=1, source_target_pairs={{0,8},{4,12},{8,0},{12,4},{1,9},{5,13},{9,1},{13,5},{2,10},{6,14},... | collective-permute-start | bytes 202760 | tf_op jit(solution)/shard_map/ppermute | solution.py:271
  10.3 1.3 %collective-permute-start.3 = (bf16[264,128]{1,0:T(8,128)(2,1)S(1)}, bf16[264,128]{1,0:T(8,128)(2,1)S(1)}, u32[]{:S(2)}, u32[]{:S(2)}) collective-permute-start(bf16[264,128]{1,0:T(8,128)(2,1)S(1)} %get-tuple-element.29), channel_id=1, source_target_pairs={{0,12},{4,0},{8,4},{12,8},{1,13},{5,1},{9,5},{13,9},{2,14},{6,2},{... | collective-permute-start | bytes 202760 | tf_op jit(solution)/shard_map/ppermute | solution.py:271
  11.7 1.5 %collective-permute-start.6 = (bf16[264,128]{1,0:T(8,128)(2,1)S(1)}, bf16[264,128]{1,0:T(8,128)(2,1)S(1)}, u32[]{:S(2)}, u32[]{:S(2)}) collective-permute-start(bf16[264,128]{1,0:T(8,128)(2,1)S(1)} %get-tuple-element.30.refs_0_), channel_id=1, source_target_pairs={{0,2},{2,0},{1,3},{3,1},{4,6},{6,4},{5,7},{7,5},{8,10},{10,8},{9,1... | collective-permute-start | bytes 202760 | tf_op jit(solution)/shard_map/ppermute | solution.py:263
  13.2 0.0 collective-permute-done.5.refs_1_
  13.2 0.8 %collective-permute-start.7 = (bf16[264,128]{1,0:T(8,128)(2,1)S(1)}, bf16[264,128]{1,0:T(8,128)(2,1)S(1)}, u32[]{:S(2)}, u32[]{:S(2)}) collective-permute-start(bf16[264,128]{1,0:T(8,128)(2,1)S(1)} %collective-permute-done.5.refs_1_), channel_id=1, source_target_pairs={{0,2},{2,0},{1,3},{3,1},{4,6},{6,4},{5,7},{7,5},{8,10},{10,8},{9,1... | collective-permute-start | bytes 202760 | tf_op jit(solution)/shard_map/ppermute | solution.py:263
  14.0 1.1 %collective-permute-done.2.refs_2_ = bf16[264,128]{1,0:T(8,128)(2,1)S(1)} collective-permute-done((bf16[264,128]{1,0:T(8,128)(2,1)S(1)}, bf16[264,128]{1,0:T(8,128)(2,1)S(1)}, u32[]{:S(2)}, u32[]{:S(2)}) %collective-permute-start.2) | collective-permute-done | bytes 67616 | tf_op jit(solution)/shard_map/ppermute | solution.py:271
  15.2 0.2 collective-permute-done.3.refs_3_
  15.4 1.6 %collective-permute-start.4 = (bf16[2,264,128]{2,1,0:T(8,128)(2,1)S(1)}, bf16[2,264,128]{2,1,0:T(8,128)(2,1)S(1)}, u32[]{:S(2)}, u32[]{:S(2)}) collective-permute-start(bf16[2,264,128]{2,1,0:T(8,128)(2,1)S(1)} %pad_maximum_fusion), channel_id=1, source_target_pairs={{0,2},{2,0},{1,3},{3,1},{4,6},{6,4},{5,7},{7,5},{8,10},{10,8},{9,1... | collective-permute-start | bytes 405512 | tf_op jit(solution)/shard_map/ppermute | solution.py:263
  17.0 0.0 collective-permute-done.6.refs_4_
  17.0 0.5 %collective-permute-done.7.refs_5_ = bf16[264,128]{1,0:T(8,128)(2,1)S(1)} collective-permute-done((bf16[264,128]{1,0:T(8,128)(2,1)S(1)}, bf16[264,128]{1,0:T(8,128)(2,1)S(1)}, u32[]{:S(2)}, u32[]{:S(2)}) %collective-permute-start.7) | collective-permute-done | bytes 67616 | tf_op jit(solution)/shard_map/ppermute | solution.py:263
  17.5 0.4 combine_first_early.1
  17.9 2.8 %collective-permute-done.4.refs_0_ = bf16[2,264,128]{2,1,0:T(8,128)(2,1)S(1)} collective-permute-done((bf16[2,264,128]{2,1,0:T(8,128)(2,1)S(1)}, bf16[2,264,128]{2,1,0:T(8,128)(2,1)S(1)}, u32[]{:S(2)}, u32[]{:S(2)}) %collective-permute-start.4) | collective-permute-done | bytes 135200 | tf_op jit(solution)/shard_map/ppermute | solution.py:263
  20.6 0.4 %combine_first.1 = (bf16[4,128,256]{2,1,0:T(8,128)(2,1)S(1)}, f32[4,128,256]{2,1,0:T(8,128)S(1)}, bf16[528,256]{1,0:T(8,128)(2,1)S(1)}) custom-call(bf16[2,264,128]{2,1,0:T(8,128)(2,1)S(1)} %collective-permute-done.4.refs_0_, s32[8,128]{1,0:T(8,128)S(1)} %get-tuple-element.26.refs_4_.refs_1_, ...), custom_call_target="tpu_custom_call" | custom-call | tf_op jit(solution)/shard_map/combine_first/pallas_call | solution.py:391
  21.1 0.1 collective-permute-start.8
  21.1 1.5 %collective-permute-done.8.refs_4_ = bf16[528,256]{1,0:T(8,128)(2,1)S(1)} collective-permute-done((bf16[528,256]{1,0:T(8,128)(2,1)S(1)}, bf16[528,256]{1,0:T(8,128)(2,1)S(1)}, u32[]{:S(2)}, u32[]{:S(2)}) %collective-permute-start.8) | collective-permute-done | bytes 270368 | tf_op jit(solution)/shard_map/ppermute | solution.py:421
  22.7 1.5 %products_second.1 = (bf16[264,128]{1,0:T(8,128)(2,1)S(1)}, bf16[264,128]{1,0:T(8,128)(2,1)S(1)}, bf16[264,128]{1,0:T(8,128)(2,1)S(1)}, bf16[264,128]{1,0:T(8,128)(2,1)S(1)}) custom-call(s32[4,128]{1,0:T(4,128)S(1)} %get-tuple-element.23.refs_0_, bf16[8,4,128,256]{3,2,1,0:T(8,128)(2,1)S(1)} %get-tuple-element.24.refs_1_, bf16[8,256,256]{2,1,0:T(8,128)(2,1)S(1)} %copy-done, ...), custom_call_target="tpu_custom_call" | custom-call | flops 1073741824 | bytes 3145728 | tf_op jit(solution)/shard_map/products_second/pallas_call | solution.py:237
  24.2 1.1 %collective-permute-start.11 = (bf16[264,128]{1,0:T(8,128)(2,1)S(1)}, bf16[264,128]{1,0:T(8,128)(2,1)S(1)}, u32[]{:S(2)}, u32[]{:S(2)}) collective-permute-start(bf16[264,128]{1,0:T(8,128)(2,1)S(1)} %get-tuple-element.39), channel_id=1, source_target_pairs={{0,8},{4,12},{8,0},{12,4},{1,9},{5,13},{9,1},{13,5},{2,10},{6,14},... | collective-permute-start | bytes 202760 | tf_op jit(solution)/shard_map/ppermute | solution.py:271
  25.3 2.3 %collective-permute-start.12 = (bf16[264,128]{1,0:T(8,128)(2,1)S(1)}, bf16[264,128]{1,0:T(8,128)(2,1)S(1)}, u32[]{:S(2)}, u32[]{:S(2)}) collective-permute-start(bf16[264,128]{1,0:T(8,128)(2,1)S(1)} %get-tuple-element.40), channel_id=1, source_target_pairs={{0,4},{4,0},{8,12},{12,8},{1,5},{5,1},{9,13},{13,9},{2,6},{6,2},{1... | collective-permute-start | bytes 202760 | tf_op jit(solution)/shard_map/ppermute | solution.py:271
  27.6 1.1 %collective-permute-start.9 = (bf16[264,128]{1,0:T(8,128)(2,1)S(1)}, bf16[264,128]{1,0:T(8,128)(2,1)S(1)}, u32[]{:S(2)}, u32[]{:S(2)}) collective-permute-start(bf16[264,128]{1,0:T(8,128)(2,1)S(1)} %get-tuple-element.37), channel_id=1, source_target_pairs={{0,12},{4,8},{8,4},{12,0},{1,13},{5,9},{9,5},{13,1},{2,14},{6,10},... | collective-permute-start | bytes 202760 | tf_op jit(solution)/shard_map/ppermute | solution.py:271
  28.7 1.5 %collective-permute-start.13 = (bf16[264,128]{1,0:T(8,128)(2,1)S(1)}, bf16[264,128]{1,0:T(8,128)(2,1)S(1)}, u32[]{:S(2)}, u32[]{:S(2)}) collective-permute-start(bf16[264,128]{1,0:T(8,128)(2,1)S(1)} %get-tuple-element.38.refs_0_), channel_id=1, source_target_pairs={{0,2},{2,0},{1,3},{3,1},{4,6},{6,4},{5,7},{7,5},{8,10},{10,8},{9,1... | collective-permute-start | bytes 202760 | tf_op jit(solution)/shard_map/ppermute | solution.py:263
  30.2 0.1 collective-permute-done.11.refs_1_
  30.3 1.5 %collective-permute-start.14 = (bf16[264,128]{1,0:T(8,128)(2,1)S(1)}, bf16[264,128]{1,0:T(8,128)(2,1)S(1)}, u32[]{:S(2)}, u32[]{:S(2)}) collective-permute-start(bf16[264,128]{1,0:T(8,128)(2,1)S(1)} %collective-permute-done.11.refs_1_), channel_id=1, source_target_pairs={{0,2},{2,0},{1,3},{3,1},{4,6},{6,4},{5,7},{7,5},{8,10},{10,8},{9,1... | collective-permute-start | bytes 202760 | tf_op jit(solution)/shard_map/ppermute | solution.py:263
  31.8 0.0 collective-permute-done.12.refs_2_
  31.8 0.5 %collective-permute-start.15 = (bf16[264,128]{1,0:T(8,128)(2,1)S(1)}, bf16[264,128]{1,0:T(8,128)(2,1)S(1)}, u32[]{:S(2)}, u32[]{:S(2)}) collective-permute-start(bf16[264,128]{1,0:T(8,128)(2,1)S(1)} %collective-permute-done.12.refs_2_), channel_id=1, source_target_pairs={{0,2},{2,0},{1,3},{3,1},{4,6},{6,4},{5,7},{7,5},{8,10},{10,8},{9,1... | collective-permute-start | bytes 202760 | tf_op jit(solution)/shard_map/ppermute | solution.py:263
  32.3 1.4 %collective-permute-done.9.refs_3_ = bf16[264,128]{1,0:T(8,128)(2,1)S(1)} collective-permute-done((bf16[264,128]{1,0:T(8,128)(2,1)S(1)}, bf16[264,128]{1,0:T(8,128)(2,1)S(1)}, u32[]{:S(2)}, u32[]{:S(2)}) %collective-permute-start.9) | collective-permute-done | bytes 67616 | tf_op jit(solution)/shard_map/ppermute | solution.py:271
  33.7 1.5 %collective-permute-start.10 = (bf16[1,264,128]{2,1,0:T(8,128)(2,1)S(1)}, bf16[1,264,128]{2,1,0:T(8,128)(2,1)S(1)}, u32[]{:S(2)}, u32[]{:S(2)}) collective-permute-start(bf16[1,264,128]{2,1,0:T(8,128)(2,1)S(1)} %bitcast.4), channel_id=1, source_target_pairs={{0,2},{2,0},{1,3},{3,1},{4,6},{6,4},{5,7},{7,5},{8,10},{10,8},{9,1... | collective-permute-start | bytes 202760 | tf_op jit(solution)/shard_map/ppermute | solution.py:263
  35.2 0.7 %copy.9 = bf16[4,128,256]{2,1,0:T(8,128)(2,1)} copy(bf16[4,128,256]{2,1,0:T(8,128)(2,1)S(1)} %get-tuple-element.44) | data formatting | bytes 524288
  35.9 0.0 collective-permute-done.13.refs_4_
  35.9 0.0 collective-permute-done.14.refs_5_
  35.9 0.8 %collective-permute-done.15.refs_6_ = bf16[264,128]{1,0:T(8,128)(2,1)S(1)} collective-permute-done((bf16[264,128]{1,0:T(8,128)(2,1)S(1)}, bf16[264,128]{1,0:T(8,128)(2,1)S(1)}, u32[]{:S(2)}, u32[]{:S(2)}) %collective-permute-start.15) | collective-permute-done | bytes 67616 | tf_op jit(solution)/shard_map/ppermute | solution.py:263
  36.8 0.5 %combine_second_early.1 = (f32[4,128,256]{2,1,0:T(8,128)S(1)}, f32[8,128]{1,0:T(8,128)S(1)}) custom-call(bf16[264,128]{1,0:T(8,128)(2,1)S(1)} %get-tuple-element.38.refs_0_, bf16[264,128]{1,0:T(8,128)(2,1)S(1)} %collective-permute-done.11.refs_1_, bf16[264,128]{1,0:T(8,128)(2,1)S(1)} %collective-permute-done.12.refs_2_, ...), custom_call_target="tpu_custom_call" | custom-call | tf_op jit(solution)/shard_map/combine_second_early/pallas_call | solution.py:391
  37.3 0.7 %collective-permute-done.10.refs_0_ = bf16[1,264,128]{2,1,0:T(8,128)(2,1)S(1)} collective-permute-done((bf16[1,264,128]{2,1,0:T(8,128)(2,1)S(1)}, bf16[1,264,128]{2,1,0:T(8,128)(2,1)S(1)}, u32[]{:S(2)}, u32[]{:S(2)}) %collective-permute-start.10) | collective-permute-done | bytes 67616 | tf_op jit(solution)/shard_map/ppermute | solution.py:263
  38.0 0.8 %combine_second.1 = bf16[4,128,256]{2,1,0:T(8,128)(2,1)} custom-call(bf16[1,264,128]{2,1,0:T(8,128)(2,1)S(1)} %collective-permute-done.10.refs_0_, s32[8,128]{1,0:T(8,128)S(1)} %get-tuple-element.26.refs_4_.refs_1_, f32[4,128,256]{2,1,0:T(8,128)S(1)} %get-tuple-element.42.refs_2_, f32[8,128]{1,0:T(8,128)S(1)} %get-tuple-element.43.refs_3_), custom_call_target="tpu_custom_call" | custom-call | tf_op jit(solution)/shard_map/combine_second/pallas_call | solution.py:391
  (1 shorter events, 0.0 us)
Async XLA Ops:
  0.6 2.5 %copy-start = (bf16[8,256,256]{2,1,0:T(8,128)(2,1)S(1)}, bf16[8,256,256]{2,1,0:T(8,128)(2,1)}, u32[]{:S(2)}) copy-start(bf16[8,256,256]{2,1,0:T(8,128)(2,1)} %refs_2_.3) | copy-start | bytes 3145732
  0.6 2.5 %collective-permute-start = (bf16[4,128,256]{2,1,0:T(8,128)(2,1)}, bf16[4,128,256]{2,1,0:T(8,128)(2,1)S(1)}, u32[]{:S(2)}, u32[]{:S(2)}) collective-permute-start(bf16[4,128,256]{2,1,0:T(8,128)(2,1)} %psi_hbm.1), channel_id=1, source_target_pairs={{1,0},{0,1},{3,2},{2,3},{5,4},{4,5},{7,6},{6,7},{9,8},{8,9},{11,10... | collective-permute-start | bytes 786440 | tf_op jit(solution)/shard_map/ppermute | solution.py:421
  1.2 1.9 %collective-permute-start.1 = (f32[4,128]{1,0:T(4,128)}, f32[4,128]{1,0:T(4,128)S(1)}, u32[]{:S(2)}, u32[]{:S(2)}) collective-permute-start(f32[4,128]{1,0:T(4,128)} %energy_hbm.1), channel_id=1, source_target_pairs={{1,0},{0,1},{3,2},{2,3},{5,4},{4,5},{7,6},{6,7},{9,8},{8,9},{11,10... | collective-permute-start | bytes 6152 | tf_op jit(solution)/shard_map/ppermute | solution.py:421
  4.7 8.5 %collective-permute-start.5 = (bf16[264,128]{1,0:T(8,128)(2,1)S(1)}, bf16[264,128]{1,0:T(8,128)(2,1)S(1)}, u32[]{:S(2)}, u32[]{:S(2)}) collective-permute-start(bf16[264,128]{1,0:T(8,128)(2,1)S(1)} %get-tuple-element.31), channel_id=1, source_target_pairs={{0,4},{4,8},{8,12},{12,0},{1,5},{5,9},{9,13},{13,1},{2,6},{6,10},{... | collective-permute-start | bytes 202760 | tf_op jit(solution)/shard_map/ppermute | solution.py:271
  7.8 7.4 %collective-permute-start.2 = (bf16[264,128]{1,0:T(8,128)(2,1)S(1)}, bf16[264,128]{1,0:T(8,128)(2,1)S(1)}, u32[]{:S(2)}, u32[]{:S(2)}) collective-permute-start(bf16[264,128]{1,0:T(8,128)(2,1)S(1)} %get-tuple-element.28), channel_id=1, source_target_pairs={{0,8},{4,12},{8,0},{12,4},{1,9},{5,13},{9,1},{13,5},{2,10},{6,14},... | collective-permute-start | bytes 202760 | tf_op jit(solution)/shard_map/ppermute | solution.py:271
  10.3 5.0 %collective-permute-start.3 = (bf16[264,128]{1,0:T(8,128)(2,1)S(1)}, bf16[264,128]{1,0:T(8,128)(2,1)S(1)}, u32[]{:S(2)}, u32[]{:S(2)}) collective-permute-start(bf16[264,128]{1,0:T(8,128)(2,1)S(1)} %get-tuple-element.29), channel_id=1, source_target_pairs={{0,12},{4,0},{8,4},{12,8},{1,13},{5,1},{9,5},{13,9},{2,14},{6,2},{... | collective-permute-start | bytes 202760 | tf_op jit(solution)/shard_map/ppermute | solution.py:271
  11.7 5.3 %collective-permute-start.6 = (bf16[264,128]{1,0:T(8,128)(2,1)S(1)}, bf16[264,128]{1,0:T(8,128)(2,1)S(1)}, u32[]{:S(2)}, u32[]{:S(2)}) collective-permute-start(bf16[264,128]{1,0:T(8,128)(2,1)S(1)} %get-tuple-element.30.refs_0_), channel_id=1, source_target_pairs={{0,2},{2,0},{1,3},{3,1},{4,6},{6,4},{5,7},{7,5},{8,10},{10,8},{9,1... | collective-permute-start | bytes 202760 | tf_op jit(solution)/shard_map/ppermute | solution.py:263
  13.2 4.3 %collective-permute-start.7 = (bf16[264,128]{1,0:T(8,128)(2,1)S(1)}, bf16[264,128]{1,0:T(8,128)(2,1)S(1)}, u32[]{:S(2)}, u32[]{:S(2)}) collective-permute-start(bf16[264,128]{1,0:T(8,128)(2,1)S(1)} %collective-permute-done.5.refs_1_), channel_id=1, source_target_pairs={{0,2},{2,0},{1,3},{3,1},{4,6},{6,4},{5,7},{7,5},{8,10},{10,8},{9,1... | collective-permute-start | bytes 202760 | tf_op jit(solution)/shard_map/ppermute | solution.py:263
  15.4 5.2 %collective-permute-start.4 = (bf16[2,264,128]{2,1,0:T(8,128)(2,1)S(1)}, bf16[2,264,128]{2,1,0:T(8,128)(2,1)S(1)}, u32[]{:S(2)}, u32[]{:S(2)}) collective-permute-start(bf16[2,264,128]{2,1,0:T(8,128)(2,1)S(1)} %pad_maximum_fusion), channel_id=1, source_target_pairs={{0,2},{2,0},{1,3},{3,1},{4,6},{6,4},{5,7},{7,5},{8,10},{10,8},{9,1... | collective-permute-start | bytes 405512 | tf_op jit(solution)/shard_map/ppermute | solution.py:263
  21.1 1.6 %collective-permute-start.8 = (bf16[528,256]{1,0:T(8,128)(2,1)S(1)}, bf16[528,256]{1,0:T(8,128)(2,1)S(1)}, u32[]{:S(2)}, u32[]{:S(2)}) collective-permute-start(bf16[528,256]{1,0:T(8,128)(2,1)S(1)} %get-tuple-element.36.refs_3_.refs_7_), channel_id=1, source_target_pairs={{1,0},{0,1},{3,2},{2,3},{5,4},{4,5},{7,6},{6,7},{9,8},{8,9},{11,10... | collective-permute-start | bytes 811016 | tf_op jit(solution)/shard_map/ppermute | solution.py:421
  24.2 6.1 %collective-permute-start.11 = (bf16[264,128]{1,0:T(8,128)(2,1)S(1)}, bf16[264,128]{1,0:T(8,128)(2,1)S(1)}, u32[]{:S(2)}, u32[]{:S(2)}) collective-permute-start(bf16[264,128]{1,0:T(8,128)(2,1)S(1)} %get-tuple-element.39), channel_id=1, source_target_pairs={{0,8},{4,12},{8,0},{12,4},{1,9},{5,13},{9,1},{13,5},{2,10},{6,14},... | collective-permute-start | bytes 202760 | tf_op jit(solution)/shard_map/ppermute | solution.py:271
  25.3 6.5 %collective-permute-start.12 = (bf16[264,128]{1,0:T(8,128)(2,1)S(1)}, bf16[264,128]{1,0:T(8,128)(2,1)S(1)}, u32[]{:S(2)}, u32[]{:S(2)}) collective-permute-start(bf16[264,128]{1,0:T(8,128)(2,1)S(1)} %get-tuple-element.40), channel_id=1, source_target_pairs={{0,4},{4,0},{8,12},{12,8},{1,5},{5,1},{9,13},{13,9},{2,6},{6,2},{1... | collective-permute-start | bytes 202760 | tf_op jit(solution)/shard_map/ppermute | solution.py:271
  27.6 6.2 %collective-permute-start.9 = (bf16[264,128]{1,0:T(8,128)(2,1)S(1)}, bf16[264,128]{1,0:T(8,128)(2,1)S(1)}, u32[]{:S(2)}, u32[]{:S(2)}) collective-permute-start(bf16[264,128]{1,0:T(8,128)(2,1)S(1)} %get-tuple-element.37), channel_id=1, source_target_pairs={{0,12},{4,8},{8,4},{12,0},{1,13},{5,9},{9,5},{13,1},{2,14},{6,10},... | collective-permute-start | bytes 202760 | tf_op jit(solution)/shard_map/ppermute | solution.py:271
  28.7 7.3 %collective-permute-start.13 = (bf16[264,128]{1,0:T(8,128)(2,1)S(1)}, bf16[264,128]{1,0:T(8,128)(2,1)S(1)}, u32[]{:S(2)}, u32[]{:S(2)}) collective-permute-start(bf16[264,128]{1,0:T(8,128)(2,1)S(1)} %get-tuple-element.38.refs_0_), channel_id=1, source_target_pairs={{0,2},{2,0},{1,3},{3,1},{4,6},{6,4},{5,7},{7,5},{8,10},{10,8},{9,1... | collective-permute-start | bytes 202760 | tf_op jit(solution)/shard_map/ppermute | solution.py:263
  30.3 5.7 %collective-permute-start.14 = (bf16[264,128]{1,0:T(8,128)(2,1)S(1)}, bf16[264,128]{1,0:T(8,128)(2,1)S(1)}, u32[]{:S(2)}, u32[]{:S(2)}) collective-permute-start(bf16[264,128]{1,0:T(8,128)(2,1)S(1)} %collective-permute-done.11.refs_1_), channel_id=1, source_target_pairs={{0,2},{2,0},{1,3},{3,1},{4,6},{6,4},{5,7},{7,5},{8,10},{10,8},{9,1... | collective-permute-start | bytes 202760 | tf_op jit(solution)/shard_map/ppermute | solution.py:263
  31.8 5.0 %collective-permute-start.15 = (bf16[264,128]{1,0:T(8,128)(2,1)S(1)}, bf16[264,128]{1,0:T(8,128)(2,1)S(1)}, u32[]{:S(2)}, u32[]{:S(2)}) collective-permute-start(bf16[264,128]{1,0:T(8,128)(2,1)S(1)} %collective-permute-done.12.refs_2_), channel_id=1, source_target_pairs={{0,2},{2,0},{1,3},{3,1},{4,6},{6,4},{5,7},{7,5},{8,10},{10,8},{9,1... | collective-permute-start | bytes 202760 | tf_op jit(solution)/shard_map/ppermute | solution.py:263
  33.7 4.3 %collective-permute-start.10 = (bf16[1,264,128]{2,1,0:T(8,128)(2,1)S(1)}, bf16[1,264,128]{2,1,0:T(8,128)(2,1)S(1)}, u32[]{:S(2)}, u32[]{:S(2)}) collective-permute-start(bf16[1,264,128]{2,1,0:T(8,128)(2,1)S(1)} %bitcast.4), channel_id=1, source_target_pairs={{0,2},{2,0},{1,3},{3,1},{4,6},{6,4},{5,7},{7,5},{8,10},{10,8},{9,1... | collective-permute-start | bytes 202760 | tf_op jit(solution)/shard_map/ppermute | solution.py:263
where the time goes:
time: 39 us; the launch traced here: 38.9 us
  starting transfers between devices  21 us (54%)
  waiting for transfers between devices  9.34 us (24%)
  Pallas kernels  7.07 us (18%)
  between operations  0.72 us (2%)
  local copies, waits for them, and re-layouts  0.71 us (2%)
    ppermute x6, starting transfers between devices, exchange(): arrived[step] = lax.ppermute(packets[step], 'sec', turn)  11.4 us
    ppermute x7, starting transfers between devices, exchange(): lax.ppermute(packet, 'op', turn)  8.92 us
    ppermute x7, waiting for transfers between devices, exchange(): lax.ppermute(packet, 'op', turn)  4.89 us
    pallas_call x2, Pallas kernels, sigma_packets(): pl.pallas_call(functools.partial(product_kernel, is_first, split, paired,...  3.11 us
    ppermute x6, waiting for transfers between devices, exchange(): arrived[step] = lax.ppermute(packets[step], 'sec', turn)  2.91 us
    pallas_call x4, Pallas kernels, call(): pl.pallas_call(kernel, out_shape=outs, in_specs=[whole(pltpu.VMEM)] * len...  2.12 us
    pallas_call x1, Pallas kernels, body(): pl.pallas_call(load_kernel, out_shape=[vec_bf16, jax.ShapeDtypeStruct(lef...  1.84 us
    ppermute x3, waiting for transfers between devices, from_others(): arrays.append(lax.ppermute(array, 'rep', turn))  1.54 us
  transfers between devices with their start and end apart: 16, of which 9 were waited for; matrix products, arithmetic and copies ran while one was open for 2% of the time, Pallas kernels for 7%

commit v1 on v0

--- a/solution.py
+++ b/solution.py
@@ -156,16 +156,22 @@
         psi_refs = take(rep_count - 1)
         level_refs = take(rep_count - 1)
     else:
+        (first_ref,) = take(1)
         vector_refs = take(rep_count)
     out_refs = take(sec_count if split else 1)
-    inner_ref, entry_ref, sem = refs
+    if not is_first:
+        (first_hbm,) = take(1)
+    inner_ref, entry_ref, sems = refs
     terms, sec_dev, half, width = left_ref.shape
     pairs = terms * sec_dev
     cap = most_pairs(pairs, sec_count)
     rep = lax.axis_index("rep")
     sec = lax.axis_index("sec")
-    fetch = pltpu.make_async_copy(list_ref, entry_ref, sem)
+    fetch = pltpu.make_async_copy(list_ref, entry_ref, sems.at[0])
     fetch.start()
+    if not is_first:
+        put = pltpu.make_async_copy(first_ref, first_hbm, sems.at[1])
+        put.start()
     inner_ref[pairs] = jnp.zeros((half, width), BF16)
 
     def first_row(step):
@@ -222,6 +228,8 @@
                 :, column * LANES:(column + 1) * LANES
             ].astype(BF16)
         out[width // LANES * half:, :] = header(entry_ref[owner, cap], scalars)
+    if not is_first:
+        put.wait()
 
 
 def sigma_packets(is_first, split, paired, rep_count, lists, left_env, right_env, more):
@@ -232,17 +240,21 @@
         outs = [jax.ShapeDtypeStruct(packet, BF16)] * sec_count
     else:
         outs = [jax.ShapeDtypeStruct((sec_count,) + packet, BF16)]
+    out_specs = [whole(pltpu.VMEM)] * len(outs)
+    if not is_first:
+        outs.append(jax.ShapeDtypeStruct((sec_dev, half, width), BF16))
+        out_specs.append(whole(pltpu.HBM))
     pair_flops = 2 * half * width * width * 2
     operands = [lists, left_env, right_env, *more]
     return pl.pallas_call(
         functools.partial(product_kernel, is_first, split, paired, rep_count, sec_count),
         out_shape=outs,
         in_specs=[whole(pltpu.VMEM)] * len(operands),
-        out_specs=[whole(pltpu.VMEM)] * len(outs),
+        out_specs=out_specs,
         scratch_shapes=[
             pltpu.VMEM((terms * sec_dev + 1, half, width), BF16),
             pltpu.SMEM(lists.shape, jnp.int32),
-            pltpu.SemaphoreType.DMA,
+            pltpu.SemaphoreType.DMA((2,)),
         ],
         compiler_params=pltpu.CompilerParams(vmem_limit_bytes=VMEM_BYTES),
         cost_estimate=pl.CostEstimate(
@@ -254,7 +266,7 @@
     )(*operands)
 
 
-def exchange(packets, split, paired, order, together):
+def exchange(packets, split, paired, order, groups):
     sec_count = lax.axis_size("sec")
     op_count = lax.axis_size("op")
     op_turns = [
@@ -269,12 +281,16 @@
         reach = (lambda i: i ^ step) if paired else (lambda i: (i + step) % sec_count)
         turn = [(i, reach(i)) for i in range(sec_count)]
         arrived[step] = lax.ppermute(packets[step], "sec", turn)
-    steps = [0, *order]
-    alone = steps[:len(steps) - together]
-    crossed = sum([over_op(arrived[step]) for step in alone], [])
-    waiting = [arrived[step] for step in steps[len(alone):]]
-    last = jnp.stack(waiting)
-    return [arrived[step] for step in steps] + crossed, over_op(last)
+    crossed = [over_op(jnp.stack([arrived[step] for step in group])) for group in groups]
+    return [arrived[step] for step in [0, *order]] + sum(crossed[:-1], []), crossed[-1]
+
+
+def views(refs):
+    return [
+        view
+        for ref in refs
+        for view in ([ref] if len(ref.shape) == 2 else [ref.at[i] for i in range(ref.shape[0])])
+    ]
 
 
 def add_packets(packet_refs, split, half, base_ref):
@@ -282,6 +298,7 @@
     own = lax.axis_size("sec") if split else 1
     body_rows = width // LANES * half
     if split:
+        packet_refs = views(packet_refs)
         heads = [ref[body_rows:].astype(F32) for ref in packet_refs]
         for column in range(width // LANES):
             lanes = slice(column * LANES, (column + 1) * LANES)
@@ -312,14 +329,12 @@
 def late_sum(packet_refs, s, half, width):
     body_rows = width // LANES * half
     value = jnp.zeros((half, width), F32)
-    for ref in packet_refs:
-        for i in range(ref.shape[0]):
-            body = jnp.concatenate(
-                [ref[i, c * half:(c + 1) * half].astype(F32) for c in range(width // LANES)],
-                axis=1,
-            )
-            slot = spread(ref[i, body_rows:].astype(F32)[0:1], width)
-            value += jnp.where(slot == s, body, 0.0)
+    for ref in views(packet_refs):
+        body = jnp.concatenate(
+            [ref[c * half:(c + 1) * half].astype(F32) for c in range(width // LANES)], axis=1
+        )
+        slot = spread(ref[body_rows:].astype(F32)[0:1], width)
+        value += jnp.where(slot == s, body, 0.0)
     return value
 
 
@@ -408,8 +423,8 @@
     split = sec_count * op_count <= 8
     can_pair = sec_count & (sec_count - 1) == 0
     steps = list(range(1, sec_count))
-    first_plan = (False, steps, 2)
-    second_plan = (can_pair, steps[1:2] + steps[:1] + steps[2:], 1)
+    first_plan = (False, steps, [[0]] + [[k] for k in steps[:-2]] + [steps[-2:]])
+    second_plan = (can_pair, steps[::-1], [[0]] + [[k] for k in steps[::-1]])
     params = pltpu.CompilerParams(vmem_limit_bytes=VMEM_BYTES)
     vec_shape = (sec_dev, half, width)
     vec_bf16 = jax.ShapeDtypeStruct(vec_shape, BF16)
@@ -464,7 +479,7 @@
         functools.partial(first_early_kernel, split, len(early)), "combine_first_early",
         [block_f32, row_f32], *early, start, levels, flops=EARLY_FLOPS,
     )
-    first_out, sigma_one, vector = call(
+    first, sigma_one, vector = call(
         functools.partial(first_kernel, len(late)), "combine_first",
         [
             pltpu.VMEM(vec_shape, BF16),
@@ -474,14 +489,15 @@
         *late, limits, start, base, scalars,
     )
 
-    packets = sigma_packets(
+    *packets, first_out = sigma_packets(
         False, split, second_plan[0], rep_count, lists, left_env, right_env,
-        [vector, *from_others(vector)],
+        [first, vector, *from_others(vector)],
     )
     early, late = exchange(packets, split, *second_plan)
     base, scale = call(
         functools.partial(second_early_kernel, split, len(early), entries),
         "combine_second_early", [block_f32, row_f32], *early, vector, levels, sigma_one, scalars,
+        flops=EARLY_FLOPS,
     )
     (second_out,) = call(
         functools.partial(second_kernel, len(late)), "combine_second", [vec_bf16],

time: 39 us -> 41 us (1.051)
  waiting for transfers between devices: 9.34 us -> 12 us
  local copies, waits for them, and re-layouts: 0.71 us -> 0.01 us
    ppermute x7, waiting for transfers between devices: 4.89 us -> 6.55 us  [exchange(): lax.ppermute(packet, 'op', turn)]
    ppermute x6, waiting for transfers between devices: 2.91 us -> 3.95 us  [exchange(): arrived[step] = lax.ppermute(packets[step], 'sec', turn)]
    unnamed x3 -> x2, local copies, waits for them, and re-layouts: 0.71 us -> 0.01 us
  transfers between devices with their start and end apart: 16 -> 16, of which waited for: 9 -> 9; matrix products, arithmetic and copies ran while one was open for 2% -> 0% of each run, Pallas kernels for 7% -> 7%
where the time goes in v1:
time: 41 us; the launch traced here: 40.9 us
  starting transfers between devices  21 us (51%)
  waiting for transfers between devices  12 us (29%)
  Pallas kernels  7.12 us (17%)
  between operations  0.72 us (2%)
    ppermute x6, starting transfers between devices, exchange(): arrived[step] = lax.ppermute(packets[step], 'sec', turn)  11.4 us
    ppermute x7, starting transfers between devices, exchange(): lax.ppermute(packet, 'op', turn)  8.89 us
    ppermute x7, waiting for transfers between devices, exchange(): lax.ppermute(packet, 'op', turn)  6.55 us
    ppermute x6, waiting for transfers between devices, exchange(): arrived[step] = lax.ppermute(packets[step], 'sec', turn)  3.95 us
    pallas_call x2, Pallas kernels, sigma_packets(): pl.pallas_call(functools.partial(product_kernel, is_first, split, paired,...  3.16 us
    pallas_call x4, Pallas kernels, call(): pl.pallas_call(kernel, out_shape=outs, in_specs=[whole(pltpu.VMEM)] * len...  2.12 us
    pallas_call x1, Pallas kernels, body(): pl.pallas_call(load_kernel, out_shape=[vec_bf16, jax.ShapeDtypeStruct(lef...  1.84 us
    ppermute x3, waiting for transfers between devices, from_others(): arrays.append(lax.ppermute(array, 'rep', turn))  1.54 us
  transfers between devices with their start and end apart: 16, of which 9 were waited for; matrix products, arithmetic and copies ran while one was open for 0% of the time, Pallas kernels for 7%

profile of v1, /device:TPU:0, one launch (start us, length us, event | category | flops | bytes accessed | tf_op | source)
XLA Modules:
  0.0 40.9 jit_solution(12404892293701605921)
XLA Ops:
  0.6 0.0 copy-start
  0.6 0.5 %collective-permute-start = (bf16[4,128,256]{2,1,0:T(8,128)(2,1)}, bf16[4,128,256]{2,1,0:T(8,128)(2,1)S(1)}, u32[]{:S(2)}, u32[]{:S(2)}) collective-permute-start(bf16[4,128,256]{2,1,0:T(8,128)(2,1)} %psi_hbm.1), channel_id=1, source_target_pairs={{1,0},{0,1},{3,2},{2,3},{5,4},{4,5},{7,6},{6,7},{9,8},{8,9},{11,10... | collective-permute-start | bytes 786440 | tf_op jit(solution)/shard_map/ppermute | solution.py:436
  1.2 0.1 collective-permute-start.1
  1.2 1.8 %load.1 = (bf16[4,128,256]{2,1,0:T(8,128)(2,1)S(1)}, bf16[8,4,128,256]{3,2,1,0:T(8,128)(2,1)S(1)}, s32[4,128]{1,0:T(4,128)S(1)}, s32[8,128]{1,0:T(8,128)S(1)}, f...) custom-call(bf16[4,128,256]{2,1,0:T(8,128)(2,1)} %psi_hbm.1, bf16[8,4,128,256]{3,2,1,0:T(8,128)(2,1)} %left_hbm.1, ...), custom_call_target="tpu_custom_call" | custom-call | tf_op jit(solution)/shard_map/load/pallas_call | solution.py:441
  3.1 0.0 collective-permute-done.1.refs_7_
  3.1 0.0 collective-permute-done.refs_6_
  3.1 0.0 copy-done
  3.1 1.6 %products_first.1 = (bf16[264,128]{1,0:T(8,128)(2,1)S(1)}, bf16[264,128]{1,0:T(8,128)(2,1)S(1)}, bf16[264,128]{1,0:T(8,128)(2,1)S(1)}, bf16[264,128]{1,0:T(8,128)(2,1)S(1)}) custom-call(s32[4,128]{1,0:T(4,128)S(1)} %get-tuple-element.24.refs_0_, bf16[8,4,128,256]{3,2,1,0:T(8,128)(2,1)S(1)} %get-tuple-element.25.refs_1_, bf16[8,256,256]{2,1,0:T(8,128)(2,1)S(1)} %copy-done, ...), custom_call_target="tpu_custom_call" | custom-call | flops 1073741824 | bytes 3145728 | tf_op jit(solution)/shard_map/products_first/pallas_call | solution.py:249
  4.7 3.1 %collective-permute-start.5 = (bf16[264,128]{1,0:T(8,128)(2,1)S(1)}, bf16[264,128]{1,0:T(8,128)(2,1)S(1)}, u32[]{:S(2)}, u32[]{:S(2)}) collective-permute-start(bf16[264,128]{1,0:T(8,128)(2,1)S(1)} %get-tuple-element.32), channel_id=1, source_target_pairs={{0,4},{4,8},{8,12},{12,0},{1,5},{5,9},{9,13},{13,1},{2,6},{6,10},{... | collective-permute-start | bytes 202760 | tf_op jit(solution)/shard_map/ppermute | solution.py:283
  7.8 2.6 %collective-permute-start.2 = (bf16[264,128]{1,0:T(8,128)(2,1)S(1)}, bf16[264,128]{1,0:T(8,128)(2,1)S(1)}, u32[]{:S(2)}, u32[]{:S(2)}) collective-permute-start(bf16[264,128]{1,0:T(8,128)(2,1)S(1)} %get-tuple-element.29), channel_id=1, source_target_pairs={{0,8},{4,12},{8,0},{12,4},{1,9},{5,13},{9,1},{13,5},{2,10},{6,14},... | collective-permute-start | bytes 202760 | tf_op jit(solution)/shard_map/ppermute | solution.py:283
  10.4 1.4 %collective-permute-start.3 = (bf16[264,128]{1,0:T(8,128)(2,1)S(1)}, bf16[264,128]{1,0:T(8,128)(2,1)S(1)}, u32[]{:S(2)}, u32[]{:S(2)}) collective-permute-start(bf16[264,128]{1,0:T(8,128)(2,1)S(1)} %get-tuple-element.30), channel_id=1, source_target_pairs={{0,12},{4,0},{8,4},{12,8},{1,13},{5,1},{9,5},{13,9},{2,14},{6,2},{... | collective-permute-start | bytes 202760 | tf_op jit(solution)/shard_map/ppermute | solution.py:283
  11.7 1.5 %collective-permute-start.6 = (bf16[1,264,128]{2,1,0:T(8,128)(2,1)S(1)}, bf16[1,264,128]{2,1,0:T(8,128)(2,1)S(1)}, u32[]{:S(2)}, u32[]{:S(2)}) collective-permute-start(bf16[1,264,128]{2,1,0:T(8,128)(2,1)S(1)} %bitcast.13), channel_id=1, source_target_pairs={{0,2},{2,0},{1,3},{3,1},{4,6},{6,4},{5,7},{7,5},{8,10},{10,8},{9,1... | collective-permute-start | bytes 202760 | tf_op jit(solution)/shard_map/ppermute | solution.py:275
  13.2 0.0 collective-permute-done.5.refs_1_
  13.2 0.8 %collective-permute-start.7 = (bf16[1,264,128]{2,1,0:T(8,128)(2,1)S(1)}, bf16[1,264,128]{2,1,0:T(8,128)(2,1)S(1)}, u32[]{:S(2)}, u32[]{:S(2)}) collective-permute-start(bf16[1,264,128]{2,1,0:T(8,128)(2,1)S(1)} %bitcast.16), channel_id=1, source_target_pairs={{0,2},{2,0},{1,3},{3,1},{4,6},{6,4},{5,7},{7,5},{8,10},{10,8},{9,1... | collective-permute-start | bytes 202760 | tf_op jit(solution)/shard_map/ppermute | solution.py:275
  14.1 1.1 %collective-permute-done.2.refs_2_ = bf16[264,128]{1,0:T(8,128)(2,1)S(1)} collective-permute-done((bf16[264,128]{1,0:T(8,128)(2,1)S(1)}, bf16[264,128]{1,0:T(8,128)(2,1)S(1)}, u32[]{:S(2)}, u32[]{:S(2)}) %collective-permute-start.2) | collective-permute-done | bytes 67616 | tf_op jit(solution)/shard_map/ppermute | solution.py:283
  15.2 0.2 collective-permute-done.3.refs_3_
  15.4 1.6 %collective-permute-start.4 = (bf16[2,264,128]{2,1,0:T(8,128)(2,1)S(1)}, bf16[2,264,128]{2,1,0:T(8,128)(2,1)S(1)}, u32[]{:S(2)}, u32[]{:S(2)}) collective-permute-start(bf16[2,264,128]{2,1,0:T(8,128)(2,1)S(1)} %pad_maximum_fusion), channel_id=1, source_target_pairs={{0,2},{2,0},{1,3},{3,1},{4,6},{6,4},{5,7},{7,5},{8,10},{10,8},{9,1... | collective-permute-start | bytes 405512 | tf_op jit(solution)/shard_map/ppermute | solution.py:275
  17.0 0.0 collective-permute-done.6.refs_4_
  17.0 0.5 %collective-permute-done.7.refs_5_ = bf16[1,264,128]{2,1,0:T(8,128)(2,1)S(1)} collective-permute-done((bf16[1,264,128]{2,1,0:T(8,128)(2,1)S(1)}, bf16[1,264,128]{2,1,0:T(8,128)(2,1)S(1)}, u32[]{:S(2)}, u32[]{:S(2)}) %collective-permute-start.7) | collective-permute-done | bytes 67616 | tf_op jit(solution)/shard_map/ppermute | solution.py:275
  17.5 0.4 combine_first_early.1
  17.9 2.8 %collective-permute-done.4.refs_0_ = bf16[2,264,128]{2,1,0:T(8,128)(2,1)S(1)} collective-permute-done((bf16[2,264,128]{2,1,0:T(8,128)(2,1)S(1)}, bf16[2,264,128]{2,1,0:T(8,128)(2,1)S(1)}, u32[]{:S(2)}, u32[]{:S(2)}) %collective-permute-start.4) | collective-permute-done | bytes 135200 | tf_op jit(solution)/shard_map/ppermute | solution.py:275
  20.7 0.4 %combine_first.1 = (bf16[4,128,256]{2,1,0:T(8,128)(2,1)S(1)}, f32[4,128,256]{2,1,0:T(8,128)S(1)}, bf16[528,256]{1,0:T(8,128)(2,1)S(1)}) custom-call(bf16[2,264,128]{2,1,0:T(8,128)(2,1)S(1)} %collective-permute-done.4.refs_0_, s32[8,128]{1,0:T(8,128)S(1)} %get-tuple-element.27.refs_4_.refs_1_, ...), custom_call_target="tpu_custom_call" | custom-call | tf_op jit(solution)/shard_map/combine_first/pallas_call | solution.py:406
  21.1 0.1 collective-permute-start.8
  21.2 1.5 %collective-permute-done.8.refs_5_ = bf16[528,256]{1,0:T(8,128)(2,1)S(1)} collective-permute-done((bf16[528,256]{1,0:T(8,128)(2,1)S(1)}, bf16[528,256]{1,0:T(8,128)(2,1)S(1)}, u32[]{:S(2)}, u32[]{:S(2)}) %collective-permute-start.8) | collective-permute-done | bytes 270368 | tf_op jit(solution)/shard_map/ppermute | solution.py:436
  22.7 1.6 %products_second.1 = (bf16[264,128]{1,0:T(8,128)(2,1)S(1)}, bf16[264,128]{1,0:T(8,128)(2,1)S(1)}, bf16[264,128]{1,0:T(8,128)(2,1)S(1)}, bf16[264,128]{1,0:T(8,128)(2,1)S(1)}, bf16[4,128,256]{2,1,0:T(8,128)(2,1)}) custom-call(s32[4,128]{1,0:T(4,128)S(1)} %get-tuple-element.24.refs_0_, bf16[8,4,128,256]{3,2,1,0:T(8,128)(2,1)S(1)} %get-tuple-element.25.refs_1_, ...), custom_call_target="tpu_custom_call" | custom-call | flops 1073741824 | bytes 3145728 | tf_op jit(solution)/shard_map/products_second/pallas_call | solution.py:249
  24.3 2.8 %collective-permute-start.11 = (bf16[264,128]{1,0:T(8,128)(2,1)S(1)}, bf16[264,128]{1,0:T(8,128)(2,1)S(1)}, u32[]{:S(2)}, u32[]{:S(2)}) collective-permute-start(bf16[264,128]{1,0:T(8,128)(2,1)S(1)} %get-tuple-element.41), channel_id=1, source_target_pairs={{0,12},{4,8},{8,4},{12,0},{1,13},{5,9},{9,5},{13,1},{2,14},{6,10},... | collective-permute-start | bytes 202760 | tf_op jit(solution)/shard_map/ppermute | solution.py:283
  27.1 0.7 %collective-permute-start.12 = (bf16[264,128]{1,0:T(8,128)(2,1)S(1)}, bf16[264,128]{1,0:T(8,128)(2,1)S(1)}, u32[]{:S(2)}, u32[]{:S(2)}) collective-permute-start(bf16[264,128]{1,0:T(8,128)(2,1)S(1)} %get-tuple-element.42), channel_id=1, source_target_pairs={{0,8},{4,12},{8,0},{12,4},{1,9},{5,13},{9,1},{13,5},{2,10},{6,14},... | collective-permute-start | bytes 202760 | tf_op jit(solution)/shard_map/ppermute | solution.py:283
  27.8 0.9 %collective-permute-start.9 = (bf16[264,128]{1,0:T(8,128)(2,1)S(1)}, bf16[264,128]{1,0:T(8,128)(2,1)S(1)}, u32[]{:S(2)}, u32[]{:S(2)}) collective-permute-start(bf16[264,128]{1,0:T(8,128)(2,1)S(1)} %get-tuple-element.39), channel_id=1, source_target_pairs={{0,4},{4,0},{8,12},{12,8},{1,5},{5,1},{9,13},{13,9},{2,6},{6,2},{1... | collective-permute-start | bytes 202760 | tf_op jit(solution)/shard_map/ppermute | solution.py:283
  28.7 1.5 %collective-permute-start.13 = (bf16[1,264,128]{2,1,0:T(8,128)(2,1)S(1)}, bf16[1,264,128]{2,1,0:T(8,128)(2,1)S(1)}, u32[]{:S(2)}, u32[]{:S(2)}) collective-permute-start(bf16[1,264,128]{2,1,0:T(8,128)(2,1)S(1)} %bitcast.11), channel_id=1, source_target_pairs={{0,2},{2,0},{1,3},{3,1},{4,6},{6,4},{5,7},{7,5},{8,10},{10,8},{9,1... | collective-permute-start | bytes 202760 | tf_op jit(solution)/shard_map/ppermute | solution.py:275
  30.2 1.0 %collective-permute-done.11.refs_1_ = bf16[264,128]{1,0:T(8,128)(2,1)S(1)} collective-permute-done((bf16[264,128]{1,0:T(8,128)(2,1)S(1)}, bf16[264,128]{1,0:T(8,128)(2,1)S(1)}, u32[]{:S(2)}, u32[]{:S(2)}) %collective-permute-start.11) | collective-permute-done | bytes 67616 | tf_op jit(solution)/shard_map/ppermute | solution.py:283
  31.2 1.5 %collective-permute-start.14 = (bf16[1,264,128]{2,1,0:T(8,128)(2,1)S(1)}, bf16[1,264,128]{2,1,0:T(8,128)(2,1)S(1)}, u32[]{:S(2)}, u32[]{:S(2)}) collective-permute-start(bf16[1,264,128]{2,1,0:T(8,128)(2,1)S(1)} %bitcast.12), channel_id=1, source_target_pairs={{0,2},{2,0},{1,3},{3,1},{4,6},{6,4},{5,7},{7,5},{8,10},{10,8},{9,1... | collective-permute-start | bytes 202760 | tf_op jit(solution)/shard_map/ppermute | solution.py:275
  32.7 1.6 %collective-permute-done.12.refs_2_ = bf16[264,128]{1,0:T(8,128)(2,1)S(1)} collective-permute-done((bf16[264,128]{1,0:T(8,128)(2,1)S(1)}, bf16[264,128]{1,0:T(8,128)(2,1)S(1)}, u32[]{:S(2)}, u32[]{:S(2)}) %collective-permute-start.12) | collective-permute-done | bytes 67616 | tf_op jit(solution)/shard_map/ppermute | solution.py:283
  34.3 1.5 %collective-permute-start.15 = (bf16[1,264,128]{2,1,0:T(8,128)(2,1)S(1)}, bf16[1,264,128]{2,1,0:T(8,128)(2,1)S(1)}, u32[]{:S(2)}, u32[]{:S(2)}) collective-permute-start(bf16[1,264,128]{2,1,0:T(8,128)(2,1)S(1)} %bitcast.14), channel_id=1, source_target_pairs={{0,2},{2,0},{1,3},{3,1},{4,6},{6,4},{5,7},{7,5},{8,10},{10,8},{9,1... | collective-permute-start | bytes 202760 | tf_op jit(solution)/shard_map/ppermute | solution.py:275
  35.8 0.0 collective-permute-done.9.refs_3_
  35.8 0.5 %collective-permute-start.10 = (bf16[1,264,128]{2,1,0:T(8,128)(2,1)S(1)}, bf16[1,264,128]{2,1,0:T(8,128)(2,1)S(1)}, u32[]{:S(2)}, u32[]{:S(2)}) collective-permute-start(bf16[1,264,128]{2,1,0:T(8,128)(2,1)S(1)} %bitcast.15), channel_id=1, source_target_pairs={{0,2},{2,0},{1,3},{3,1},{4,6},{6,4},{5,7},{7,5},{8,10},{10,8},{9,1... | collective-permute-start | bytes 202760 | tf_op jit(solution)/shard_map/ppermute | solution.py:275
  36.3 0.0 collective-permute-done.13.refs_4_
  36.3 0.0 collective-permute-done.14.refs_5_
  36.3 2.9 %collective-permute-done.15.refs_6_ = bf16[1,264,128]{2,1,0:T(8,128)(2,1)S(1)} collective-permute-done((bf16[1,264,128]{2,1,0:T(8,128)(2,1)S(1)}, bf16[1,264,128]{2,1,0:T(8,128)(2,1)S(1)}, u32[]{:S(2)}, u32[]{:S(2)}) %collective-permute-start.15) | collective-permute-done | bytes 67616 | tf_op jit(solution)/shard_map/ppermute | solution.py:275
  39.2 0.5 %combine_second_early.1 = (f32[4,128,256]{2,1,0:T(8,128)S(1)}, f32[8,128]{1,0:T(8,128)S(1)}) custom-call(bf16[264,128]{1,0:T(8,128)(2,1)S(1)} %get-tuple-element.40.refs_0_, bf16[264,128]{1,0:T(8,128)(2,1)S(1)} %collective-permute-done.11.refs_1_, bf16[264,128]{1,0:T(8,128)(2,1)S(1)} %collective-permute-done.12.refs_2_, ...), custom_call_target="tpu_custom_call" | custom-call | flops 1000000000 | tf_op jit(solution)/shard_map/combine_second_early/pallas_call | solution.py:406
  39.7 0.4 collective-permute-done.10.refs_0_
  40.1 0.8 %combine_second.1 = bf16[4,128,256]{2,1,0:T(8,128)(2,1)} custom-call(bf16[1,264,128]{2,1,0:T(8,128)(2,1)S(1)} %collective-permute-done.10.refs_0_, s32[8,128]{1,0:T(8,128)S(1)} %get-tuple-element.27.refs_4_.refs_1_, f32[4,128,256]{2,1,0:T(8,128)S(1)} %get-tuple-element.44.refs_2_, f32[8,128]{1,0:T(8,128)S(1)} %get-tuple-element.45.refs_3_), custom_call_target="tpu_custom_call" | custom-call | tf_op jit(solution)/shard_map/combine_second/pallas_call | solution.py:406
  (1 shorter events, 0.0 us)
Async XLA Ops:
  0.6 2.5 %copy-start = (bf16[8,256,256]{2,1,0:T(8,128)(2,1)S(1)}, bf16[8,256,256]{2,1,0:T(8,128)(2,1)}, u32[]{:S(2)}) copy-start(bf16[8,256,256]{2,1,0:T(8,128)(2,1)} %refs_2_.3) | copy-start | bytes 3145732
  0.6 2.5 %collective-permute-start = (bf16[4,128,256]{2,1,0:T(8,128)(2,1)}, bf16[4,128,256]{2,1,0:T(8,128)(2,1)S(1)}, u32[]{:S(2)}, u32[]{:S(2)}) collective-permute-start(bf16[4,128,256]{2,1,0:T(8,128)(2,1)} %psi_hbm.1), channel_id=1, source_target_pairs={{1,0},{0,1},{3,2},{2,3},{5,4},{4,5},{7,6},{6,7},{9,8},{8,9},{11,10... | collective-permute-start | bytes 786440 | tf_op jit(solution)/shard_map/ppermute | solution.py:436
  1.2 1.9 %collective-permute-start.1 = (f32[4,128]{1,0:T(4,128)}, f32[4,128]{1,0:T(4,128)S(1)}, u32[]{:S(2)}, u32[]{:S(2)}) collective-permute-start(f32[4,128]{1,0:T(4,128)} %energy_hbm.1), channel_id=1, source_target_pairs={{1,0},{0,1},{3,2},{2,3},{5,4},{4,5},{7,6},{6,7},{9,8},{8,9},{11,10... | collective-permute-start | bytes 6152 | tf_op jit(solution)/shard_map/ppermute | solution.py:436
  4.7 8.5 %collective-permute-start.5 = (bf16[264,128]{1,0:T(8,128)(2,1)S(1)}, bf16[264,128]{1,0:T(8,128)(2,1)S(1)}, u32[]{:S(2)}, u32[]{:S(2)}) collective-permute-start(bf16[264,128]{1,0:T(8,128)(2,1)S(1)} %get-tuple-element.32), channel_id=1, source_target_pairs={{0,4},{4,8},{8,12},{12,0},{1,5},{5,9},{9,13},{13,1},{2,6},{6,10},{... | collective-permute-start | bytes 202760 | tf_op jit(solution)/shard_map/ppermute | solution.py:283
  7.8 7.4 %collective-permute-start.2 = (bf16[264,128]{1,0:T(8,128)(2,1)S(1)}, bf16[264,128]{1,0:T(8,128)(2,1)S(1)}, u32[]{:S(2)}, u32[]{:S(2)}) collective-permute-start(bf16[264,128]{1,0:T(8,128)(2,1)S(1)} %get-tuple-element.29), channel_id=1, source_target_pairs={{0,8},{4,12},{8,0},{12,4},{1,9},{5,13},{9,1},{13,5},{2,10},{6,14},... | collective-permute-start | bytes 202760 | tf_op jit(solution)/shard_map/ppermute | solution.py:283
  10.4 5.0 %collective-permute-start.3 = (bf16[264,128]{1,0:T(8,128)(2,1)S(1)}, bf16[264,128]{1,0:T(8,128)(2,1)S(1)}, u32[]{:S(2)}, u32[]{:S(2)}) collective-permute-start(bf16[264,128]{1,0:T(8,128)(2,1)S(1)} %get-tuple-element.30), channel_id=1, source_target_pairs={{0,12},{4,0},{8,4},{12,8},{1,13},{5,1},{9,5},{13,9},{2,14},{6,2},{... | collective-permute-start | bytes 202760 | tf_op jit(solution)/shard_map/ppermute | solution.py:283
  11.7 5.3 %collective-permute-start.6 = (bf16[1,264,128]{2,1,0:T(8,128)(2,1)S(1)}, bf16[1,264,128]{2,1,0:T(8,128)(2,1)S(1)}, u32[]{:S(2)}, u32[]{:S(2)}) collective-permute-start(bf16[1,264,128]{2,1,0:T(8,128)(2,1)S(1)} %bitcast.13), channel_id=1, source_target_pairs={{0,2},{2,0},{1,3},{3,1},{4,6},{6,4},{5,7},{7,5},{8,10},{10,8},{9,1... | collective-permute-start | bytes 202760 | tf_op jit(solution)/shard_map/ppermute | solution.py:275
  13.2 4.3 %collective-permute-start.7 = (bf16[1,264,128]{2,1,0:T(8,128)(2,1)S(1)}, bf16[1,264,128]{2,1,0:T(8,128)(2,1)S(1)}, u32[]{:S(2)}, u32[]{:S(2)}) collective-permute-start(bf16[1,264,128]{2,1,0:T(8,128)(2,1)S(1)} %bitcast.16), channel_id=1, source_target_pairs={{0,2},{2,0},{1,3},{3,1},{4,6},{6,4},{5,7},{7,5},{8,10},{10,8},{9,1... | collective-permute-start | bytes 202760 | tf_op jit(solution)/shard_map/ppermute | solution.py:275
  15.4 5.3 %collective-permute-start.4 = (bf16[2,264,128]{2,1,0:T(8,128)(2,1)S(1)}, bf16[2,264,128]{2,1,0:T(8,128)(2,1)S(1)}, u32[]{:S(2)}, u32[]{:S(2)}) collective-permute-start(bf16[2,264,128]{2,1,0:T(8,128)(2,1)S(1)} %pad_maximum_fusion), channel_id=1, source_target_pairs={{0,2},{2,0},{1,3},{3,1},{4,6},{6,4},{5,7},{7,5},{8,10},{10,8},{9,1... | collective-permute-start | bytes 405512 | tf_op jit(solution)/shard_map/ppermute | solution.py:275
  21.1 1.6 %collective-permute-start.8 = (bf16[528,256]{1,0:T(8,128)(2,1)S(1)}, bf16[528,256]{1,0:T(8,128)(2,1)S(1)}, u32[]{:S(2)}, u32[]{:S(2)}) collective-permute-start(bf16[528,256]{1,0:T(8,128)(2,1)S(1)} %get-tuple-element.37.refs_4_.refs_7_), channel_id=1, source_target_pairs={{1,0},{0,1},{3,2},{2,3},{5,4},{4,5},{7,6},{6,7},{9,8},{8,9},{11,10... | collective-permute-start | bytes 811016 | tf_op jit(solution)/shard_map/ppermute | solution.py:436
  24.3 7.0 %collective-permute-start.11 = (bf16[264,128]{1,0:T(8,128)(2,1)S(1)}, bf16[264,128]{1,0:T(8,128)(2,1)S(1)}, u32[]{:S(2)}, u32[]{:S(2)}) collective-permute-start(bf16[264,128]{1,0:T(8,128)(2,1)S(1)} %get-tuple-element.41), channel_id=1, source_target_pairs={{0,12},{4,8},{8,4},{12,0},{1,13},{5,9},{9,5},{13,1},{2,14},{6,10},... | collective-permute-start | bytes 202760 | tf_op jit(solution)/shard_map/ppermute | solution.py:283
  27.1 7.2 %collective-permute-start.12 = (bf16[264,128]{1,0:T(8,128)(2,1)S(1)}, bf16[264,128]{1,0:T(8,128)(2,1)S(1)}, u32[]{:S(2)}, u32[]{:S(2)}) collective-permute-start(bf16[264,128]{1,0:T(8,128)(2,1)S(1)} %get-tuple-element.42), channel_id=1, source_target_pairs={{0,8},{4,12},{8,0},{12,4},{1,9},{5,13},{9,1},{13,5},{2,10},{6,14},... | collective-permute-start | bytes 202760 | tf_op jit(solution)/shard_map/ppermute | solution.py:283
  27.8 8.0 %collective-permute-start.9 = (bf16[264,128]{1,0:T(8,128)(2,1)S(1)}, bf16[264,128]{1,0:T(8,128)(2,1)S(1)}, u32[]{:S(2)}, u32[]{:S(2)}) collective-permute-start(bf16[264,128]{1,0:T(8,128)(2,1)S(1)} %get-tuple-element.39), channel_id=1, source_target_pairs={{0,4},{4,0},{8,12},{12,8},{1,5},{5,1},{9,13},{13,9},{2,6},{6,2},{1... | collective-permute-start | bytes 202760 | tf_op jit(solution)/shard_map/ppermute | solution.py:283
  28.7 7.6 %collective-permute-start.13 = (bf16[1,264,128]{2,1,0:T(8,128)(2,1)S(1)}, bf16[1,264,128]{2,1,0:T(8,128)(2,1)S(1)}, u32[]{:S(2)}, u32[]{:S(2)}) collective-permute-start(bf16[1,264,128]{2,1,0:T(8,128)(2,1)S(1)} %bitcast.11), channel_id=1, source_target_pairs={{0,2},{2,0},{1,3},{3,1},{4,6},{6,4},{5,7},{7,5},{8,10},{10,8},{9,1... | collective-permute-start | bytes 202760 | tf_op jit(solution)/shard_map/ppermute | solution.py:275
  31.2 5.1 %collective-permute-start.14 = (bf16[1,264,128]{2,1,0:T(8,128)(2,1)S(1)}, bf16[1,264,128]{2,1,0:T(8,128)(2,1)S(1)}, u32[]{:S(2)}, u32[]{:S(2)}) collective-permute-start(bf16[1,264,128]{2,1,0:T(8,128)(2,1)S(1)} %bitcast.12), channel_id=1, source_target_pairs={{0,2},{2,0},{1,3},{3,1},{4,6},{6,4},{5,7},{7,5},{8,10},{10,8},{9,1... | collective-permute-start | bytes 202760 | tf_op jit(solution)/shard_map/ppermute | solution.py:275
  34.3 4.9 %collective-permute-start.15 = (bf16[1,264,128]{2,1,0:T(8,128)(2,1)S(1)}, bf16[1,264,128]{2,1,0:T(8,128)(2,1)S(1)}, u32[]{:S(2)}, u32[]{:S(2)}) collective-permute-start(bf16[1,264,128]{2,1,0:T(8,128)(2,1)S(1)} %bitcast.14), channel_id=1, source_target_pairs={{0,2},{2,0},{1,3},{3,1},{4,6},{6,4},{5,7},{7,5},{8,10},{10,8},{9,1... | collective-permute-start | bytes 202760 | tf_op jit(solution)/shard_map/ppermute | solution.py:275
  35.8 4.3 %collective-permute-start.10 = (bf16[1,264,128]{2,1,0:T(8,128)(2,1)S(1)}, bf16[1,264,128]{2,1,0:T(8,128)(2,1)S(1)}, u32[]{:S(2)}, u32[]{:S(2)}) collective-permute-start(bf16[1,264,128]{2,1,0:T(8,128)(2,1)S(1)} %bitcast.15), channel_id=1, source_target_pairs={{0,2},{2,0},{1,3},{3,1},{4,6},{6,4},{5,7},{7,5},{8,10},{10,8},{9,1... | collective-permute-start | bytes 202760 | tf_op jit(solution)/shard_map/ppermute | solution.py:275

commit v2 on v1

--- a/solution.py
+++ b/solution.py
@@ -424,7 +424,8 @@
     can_pair = sec_count & (sec_count - 1) == 0
     steps = list(range(1, sec_count))
     first_plan = (False, steps, [[0]] + [[k] for k in steps[:-2]] + [steps[-2:]])
-    second_plan = (can_pair, steps[::-1], [[0]] + [[k] for k in steps[::-1]])
+    second_groups = [[0]] + [[k] for k in steps[1:2] + steps[:1] + steps[2:]]
+    second_plan = (can_pair, steps[1:2] + steps[:1] + steps[2:], second_groups)
     params = pltpu.CompilerParams(vmem_limit_bytes=VMEM_BYTES)
     vec_shape = (sec_dev, half, width)
     vec_bf16 = jax.ShapeDtypeStruct(vec_shape, BF16)
@@ -497,7 +498,7 @@
     base, scale = call(
         functools.partial(second_early_kernel, split, len(early), entries),
         "combine_second_early", [block_f32, row_f32], *early, vector, levels, sigma_one, scalars,
-        flops=EARLY_FLOPS,
+        flops=10**8,
     )
     (second_out,) = call(
         functools.partial(second_kernel, len(late)), "combine_second", [vec_bf16],

time: 41 us -> 39 us (0.951)
  waiting for transfers between devices: 12 us -> 10 us
    ppermute x6, waiting for transfers between devices: 3.95 us -> 2.92 us  [exchange(): arrived[step] = lax.ppermute(packets[step], 'sec', turn)]
    ppermute x7, waiting for transfers between devices: 6.55 us -> 5.58 us  [exchange(): lax.ppermute(packet, 'op', turn)]
where the time goes in v2:
time: 39 us; the launch traced here: 38.9 us
  starting transfers between devices  21 us (54%)
  waiting for transfers between devices  10 us (26%)
  Pallas kernels  7.1 us (18%)
  between operations  0.72 us (2%)
    ppermute x6, starting transfers between devices, exchange(): arrived[step] = lax.ppermute(packets[step], 'sec', turn)  11.4 us
    ppermute x7, starting transfers between devices, exchange(): lax.ppermute(packet, 'op', turn)  8.91 us
    ppermute x7, waiting for transfers between devices, exchange(): lax.ppermute(packet, 'op', turn)  5.58 us
    pallas_call x2, Pallas kernels, sigma_packets(): pl.pallas_call(functools.partial(product_kernel, is_first, split, paired,...  3.14 us
    ppermute x6, waiting for transfers between devices, exchange(): arrived[step] = lax.ppermute(packets[step], 'sec', turn)  2.92 us
    pallas_call x4, Pallas kernels, call(): pl.pallas_call(kernel, out_shape=outs, in_specs=[whole(pltpu.VMEM)] * len...  2.12 us
    pallas_call x1, Pallas kernels, body(): pl.pallas_call(load_kernel, out_shape=[vec_bf16, jax.ShapeDtypeStruct(lef...  1.84 us
    ppermute x3, waiting for transfers between devices, from_others(): arrays.append(lax.ppermute(array, 'rep', turn))  1.54 us
  transfers between devices with their start and end apart: 16, of which 9 were waited for; matrix products, arithmetic and copies ran while one was open for 0% of the time, Pallas kernels for 7%

profile of v2, /device:TPU:0, one launch (start us, length us, event | category | flops | bytes accessed | tf_op | source)
XLA Modules:
  0.0 38.9 jit_solution(5859099258594505617)
XLA Ops:
  0.6 0.0 copy-start
  0.6 0.5 %collective-permute-start = (bf16[4,128,256]{2,1,0:T(8,128)(2,1)}, bf16[4,128,256]{2,1,0:T(8,128)(2,1)S(1)}, u32[]{:S(2)}, u32[]{:S(2)}) collective-permute-start(bf16[4,128,256]{2,1,0:T(8,128)(2,1)} %psi_hbm.1), channel_id=1, source_target_pairs={{1,0},{0,1},{3,2},{2,3},{5,4},{4,5},{7,6},{6,7},{9,8},{8,9},{11,10... | collective-permute-start | bytes 786440 | tf_op jit(solution)/shard_map/ppermute | solution.py:437
  1.2 0.1 collective-permute-start.1
  1.2 1.8 %load.1 = (bf16[4,128,256]{2,1,0:T(8,128)(2,1)S(1)}, bf16[8,4,128,256]{3,2,1,0:T(8,128)(2,1)S(1)}, s32[4,128]{1,0:T(4,128)S(1)}, s32[8,128]{1,0:T(8,128)S(1)}, f...) custom-call(bf16[4,128,256]{2,1,0:T(8,128)(2,1)} %psi_hbm.1, bf16[8,4,128,256]{3,2,1,0:T(8,128)(2,1)} %left_hbm.1, ...), custom_call_target="tpu_custom_call" | custom-call | tf_op jit(solution)/shard_map/load/pallas_call | solution.py:442
  3.1 0.0 collective-permute-done.1.refs_7_
  3.1 0.0 collective-permute-done.refs_6_
  3.1 0.0 copy-done
  3.1 1.6 %products_first.1 = (bf16[264,128]{1,0:T(8,128)(2,1)S(1)}, bf16[264,128]{1,0:T(8,128)(2,1)S(1)}, bf16[264,128]{1,0:T(8,128)(2,1)S(1)}, bf16[264,128]{1,0:T(8,128)(2,1)S(1)}) custom-call(s32[4,128]{1,0:T(4,128)S(1)} %get-tuple-element.24.refs_0_, bf16[8,4,128,256]{3,2,1,0:T(8,128)(2,1)S(1)} %get-tuple-element.25.refs_1_, bf16[8,256,256]{2,1,0:T(8,128)(2,1)S(1)} %copy-done, ...), custom_call_target="tpu_custom_call" | custom-call | flops 1073741824 | bytes 3145728 | tf_op jit(solution)/shard_map/products_first/pallas_call | solution.py:249
  4.7 3.1 %collective-permute-start.5 = (bf16[264,128]{1,0:T(8,128)(2,1)S(1)}, bf16[264,128]{1,0:T(8,128)(2,1)S(1)}, u32[]{:S(2)}, u32[]{:S(2)}) collective-permute-start(bf16[264,128]{1,0:T(8,128)(2,1)S(1)} %get-tuple-element.32), channel_id=1, source_target_pairs={{0,4},{4,8},{8,12},{12,0},{1,5},{5,9},{9,13},{13,1},{2,6},{6,10},{... | collective-permute-start | bytes 202760 | tf_op jit(solution)/shard_map/ppermute | solution.py:283
  7.8 2.6 %collective-permute-start.2 = (bf16[264,128]{1,0:T(8,128)(2,1)S(1)}, bf16[264,128]{1,0:T(8,128)(2,1)S(1)}, u32[]{:S(2)}, u32[]{:S(2)}) collective-permute-start(bf16[264,128]{1,0:T(8,128)(2,1)S(1)} %get-tuple-element.29), channel_id=1, source_target_pairs={{0,8},{4,12},{8,0},{12,4},{1,9},{5,13},{9,1},{13,5},{2,10},{6,14},... | collective-permute-start | bytes 202760 | tf_op jit(solution)/shard_map/ppermute | solution.py:283
  10.4 1.3 %collective-permute-start.3 = (bf16[264,128]{1,0:T(8,128)(2,1)S(1)}, bf16[264,128]{1,0:T(8,128)(2,1)S(1)}, u32[]{:S(2)}, u32[]{:S(2)}) collective-permute-start(bf16[264,128]{1,0:T(8,128)(2,1)S(1)} %get-tuple-element.30), channel_id=1, source_target_pairs={{0,12},{4,0},{8,4},{12,8},{1,13},{5,1},{9,5},{13,9},{2,14},{6,2},{... | collective-permute-start | bytes 202760 | tf_op jit(solution)/shard_map/ppermute | solution.py:283
  11.7 1.5 %collective-permute-start.6 = (bf16[1,264,128]{2,1,0:T(8,128)(2,1)S(1)}, bf16[1,264,128]{2,1,0:T(8,128)(2,1)S(1)}, u32[]{:S(2)}, u32[]{:S(2)}) collective-permute-start(bf16[1,264,128]{2,1,0:T(8,128)(2,1)S(1)} %bitcast.15), channel_id=1, source_target_pairs={{0,2},{2,0},{1,3},{3,1},{4,6},{6,4},{5,7},{7,5},{8,10},{10,8},{9,1... | collective-permute-start | bytes 202760 | tf_op jit(solution)/shard_map/ppermute | solution.py:275
  13.2 0.0 collective-permute-done.5.refs_1_
  13.2 0.8 %collective-permute-start.7 = (bf16[1,264,128]{2,1,0:T(8,128)(2,1)S(1)}, bf16[1,264,128]{2,1,0:T(8,128)(2,1)S(1)}, u32[]{:S(2)}, u32[]{:S(2)}) collective-permute-start(bf16[1,264,128]{2,1,0:T(8,128)(2,1)S(1)} %bitcast.16), channel_id=1, source_target_pairs={{0,2},{2,0},{1,3},{3,1},{4,6},{6,4},{5,7},{7,5},{8,10},{10,8},{9,1... | collective-permute-start | bytes 202760 | tf_op jit(solution)/shard_map/ppermute | solution.py:275
  14.0 1.1 %collective-permute-done.2.refs_2_ = bf16[264,128]{1,0:T(8,128)(2,1)S(1)} collective-permute-done((bf16[264,128]{1,0:T(8,128)(2,1)S(1)}, bf16[264,128]{1,0:T(8,128)(2,1)S(1)}, u32[]{:S(2)}, u32[]{:S(2)}) %collective-permute-start.2) | collective-permute-done | bytes 67616 | tf_op jit(solution)/shard_map/ppermute | solution.py:283
  15.2 0.2 collective-permute-done.3.refs_3_
  15.4 1.6 %collective-permute-start.4 = (bf16[2,264,128]{2,1,0:T(8,128)(2,1)S(1)}, bf16[2,264,128]{2,1,0:T(8,128)(2,1)S(1)}, u32[]{:S(2)}, u32[]{:S(2)}) collective-permute-start(bf16[2,264,128]{2,1,0:T(8,128)(2,1)S(1)} %pad_maximum_fusion), channel_id=1, source_target_pairs={{0,2},{2,0},{1,3},{3,1},{4,6},{6,4},{5,7},{7,5},{8,10},{10,8},{9,1... | collective-permute-start | bytes 405512 | tf_op jit(solution)/shard_map/ppermute | solution.py:275
  17.0 0.0 collective-permute-done.6.refs_4_
  17.0 0.5 %collective-permute-done.7.refs_5_ = bf16[1,264,128]{2,1,0:T(8,128)(2,1)S(1)} collective-permute-done((bf16[1,264,128]{2,1,0:T(8,128)(2,1)S(1)}, bf16[1,264,128]{2,1,0:T(8,128)(2,1)S(1)}, u32[]{:S(2)}, u32[]{:S(2)}) %collective-permute-start.7) | collective-permute-done | bytes 67616 | tf_op jit(solution)/shard_map/ppermute | solution.py:275
  17.5 0.4 combine_first_early.1
  17.9 2.8 %collective-permute-done.4.refs_0_ = bf16[2,264,128]{2,1,0:T(8,128)(2,1)S(1)} collective-permute-done((bf16[2,264,128]{2,1,0:T(8,128)(2,1)S(1)}, bf16[2,264,128]{2,1,0:T(8,128)(2,1)S(1)}, u32[]{:S(2)}, u32[]{:S(2)}) %collective-permute-start.4) | collective-permute-done | bytes 135200 | tf_op jit(solution)/shard_map/ppermute | solution.py:275
  20.7 0.4 %combine_first.1 = (bf16[4,128,256]{2,1,0:T(8,128)(2,1)S(1)}, f32[4,128,256]{2,1,0:T(8,128)S(1)}, bf16[528,256]{1,0:T(8,128)(2,1)S(1)}) custom-call(bf16[2,264,128]{2,1,0:T(8,128)(2,1)S(1)} %collective-permute-done.4.refs_0_, s32[8,128]{1,0:T(8,128)S(1)} %get-tuple-element.27.refs_4_.refs_1_, ...), custom_call_target="tpu_custom_call" | custom-call | tf_op jit(solution)/shard_map/combine_first/pallas_call | solution.py:406
  21.1 0.1 collective-permute-start.8
  21.1 1.5 %collective-permute-done.8.refs_5_ = bf16[528,256]{1,0:T(8,128)(2,1)S(1)} collective-permute-done((bf16[528,256]{1,0:T(8,128)(2,1)S(1)}, bf16[528,256]{1,0:T(8,128)(2,1)S(1)}, u32[]{:S(2)}, u32[]{:S(2)}) %collective-permute-start.8) | collective-permute-done | bytes 270368 | tf_op jit(solution)/shard_map/ppermute | solution.py:437
  22.7 1.6 %products_second.1 = (bf16[264,128]{1,0:T(8,128)(2,1)S(1)}, bf16[264,128]{1,0:T(8,128)(2,1)S(1)}, bf16[264,128]{1,0:T(8,128)(2,1)S(1)}, bf16[264,128]{1,0:T(8,128)(2,1)S(1)}, bf16[4,128,256]{2,1,0:T(8,128)(2,1)}) custom-call(s32[4,128]{1,0:T(4,128)S(1)} %get-tuple-element.24.refs_0_, bf16[8,4,128,256]{3,2,1,0:T(8,128)(2,1)S(1)} %get-tuple-element.25.refs_1_, ...), custom_call_target="tpu_custom_call" | custom-call | flops 1073741824 | bytes 3145728 | tf_op jit(solution)/shard_map/products_second/pallas_call | solution.py:249
  24.2 1.1 %collective-permute-start.11 = (bf16[264,128]{1,0:T(8,128)(2,1)S(1)}, bf16[264,128]{1,0:T(8,128)(2,1)S(1)}, u32[]{:S(2)}, u32[]{:S(2)}) collective-permute-start(bf16[264,128]{1,0:T(8,128)(2,1)S(1)} %get-tuple-element.41), channel_id=1, source_target_pairs={{0,8},{4,12},{8,0},{12,4},{1,9},{5,13},{9,1},{13,5},{2,10},{6,14},... | collective-permute-start | bytes 202760 | tf_op jit(solution)/shard_map/ppermute | solution.py:283
  25.3 2.3 %collective-permute-start.12 = (bf16[264,128]{1,0:T(8,128)(2,1)S(1)}, bf16[264,128]{1,0:T(8,128)(2,1)S(1)}, u32[]{:S(2)}, u32[]{:S(2)}) collective-permute-start(bf16[264,128]{1,0:T(8,128)(2,1)S(1)} %get-tuple-element.42), channel_id=1, source_target_pairs={{0,4},{4,0},{8,12},{12,8},{1,5},{5,1},{9,13},{13,9},{2,6},{6,2},{1... | collective-permute-start | bytes 202760 | tf_op jit(solution)/shard_map/ppermute | solution.py:283
  27.6 1.1 %collective-permute-start.9 = (bf16[264,128]{1,0:T(8,128)(2,1)S(1)}, bf16[264,128]{1,0:T(8,128)(2,1)S(1)}, u32[]{:S(2)}, u32[]{:S(2)}) collective-permute-start(bf16[264,128]{1,0:T(8,128)(2,1)S(1)} %get-tuple-element.39), channel_id=1, source_target_pairs={{0,12},{4,8},{8,4},{12,0},{1,13},{5,9},{9,5},{13,1},{2,14},{6,10},... | collective-permute-start | bytes 202760 | tf_op jit(solution)/shard_map/ppermute | solution.py:283
  28.7 1.5 %collective-permute-start.13 = (bf16[1,264,128]{2,1,0:T(8,128)(2,1)S(1)}, bf16[1,264,128]{2,1,0:T(8,128)(2,1)S(1)}, u32[]{:S(2)}, u32[]{:S(2)}) collective-permute-start(bf16[1,264,128]{2,1,0:T(8,128)(2,1)S(1)} %bitcast.9), channel_id=1, source_target_pairs={{0,2},{2,0},{1,3},{3,1},{4,6},{6,4},{5,7},{7,5},{8,10},{10,8},{9,1... | collective-permute-start | bytes 202760 | tf_op jit(solution)/shard_map/ppermute | solution.py:275
  30.2 0.1 collective-permute-done.11.refs_1_
  30.3 0.7 %collective-permute-start.14 = (bf16[1,264,128]{2,1,0:T(8,128)(2,1)S(1)}, bf16[1,264,128]{2,1,0:T(8,128)(2,1)S(1)}, u32[]{:S(2)}, u32[]{:S(2)}) collective-permute-start(bf16[1,264,128]{2,1,0:T(8,128)(2,1)S(1)} %bitcast.10), channel_id=1, source_target_pairs={{0,2},{2,0},{1,3},{3,1},{4,6},{6,4},{5,7},{7,5},{8,10},{10,8},{9,1... | collective-permute-start | bytes 202760 | tf_op jit(solution)/shard_map/ppermute | solution.py:275
  31.0 0.0 collective-permute-done.12.refs_2_
  31.0 1.3 %collective-permute-start.15 = (bf16[1,264,128]{2,1,0:T(8,128)(2,1)S(1)}, bf16[1,264,128]{2,1,0:T(8,128)(2,1)S(1)}, u32[]{:S(2)}, u32[]{:S(2)}) collective-permute-start(bf16[1,264,128]{2,1,0:T(8,128)(2,1)S(1)} %bitcast.11), channel_id=1, source_target_pairs={{0,2},{2,0},{1,3},{3,1},{4,6},{6,4},{5,7},{7,5},{8,10},{10,8},{9,1... | collective-permute-start | bytes 202760 | tf_op jit(solution)/shard_map/ppermute | solution.py:275
  32.3 1.4 %collective-permute-done.9.refs_3_ = bf16[264,128]{1,0:T(8,128)(2,1)S(1)} collective-permute-done((bf16[264,128]{1,0:T(8,128)(2,1)S(1)}, bf16[264,128]{1,0:T(8,128)(2,1)S(1)}, u32[]{:S(2)}, u32[]{:S(2)}) %collective-permute-start.9) | collective-permute-done | bytes 67616 | tf_op jit(solution)/shard_map/ppermute | solution.py:283
  33.8 1.5 %collective-permute-start.10 = (bf16[1,264,128]{2,1,0:T(8,128)(2,1)S(1)}, bf16[1,264,128]{2,1,0:T(8,128)(2,1)S(1)}, u32[]{:S(2)}, u32[]{:S(2)}) collective-permute-start(bf16[1,264,128]{2,1,0:T(8,128)(2,1)S(1)} %bitcast.12), channel_id=1, source_target_pairs={{0,2},{2,0},{1,3},{3,1},{4,6},{6,4},{5,7},{7,5},{8,10},{10,8},{9,1... | collective-permute-start | bytes 202760 | tf_op jit(solution)/shard_map/ppermute | solution.py:275
  35.3 0.0 collective-permute-done.13.refs_4_
  35.3 0.0 collective-permute-done.14.refs_5_
  35.3 0.6 %collective-permute-done.15.refs_6_ = bf16[1,264,128]{2,1,0:T(8,128)(2,1)S(1)} collective-permute-done((bf16[1,264,128]{2,1,0:T(8,128)(2,1)S(1)}, bf16[1,264,128]{2,1,0:T(8,128)(2,1)S(1)}, u32[]{:S(2)}, u32[]{:S(2)}) %collective-permute-start.15) | collective-permute-done | bytes 67616 | tf_op jit(solution)/shard_map/ppermute | solution.py:275
  35.9 0.5 %combine_second_early.1 = (f32[4,128,256]{2,1,0:T(8,128)S(1)}, f32[8,128]{1,0:T(8,128)S(1)}) custom-call(bf16[264,128]{1,0:T(8,128)(2,1)S(1)} %get-tuple-element.40.refs_0_, bf16[264,128]{1,0:T(8,128)(2,1)S(1)} %collective-permute-done.11.refs_1_, bf16[264,128]{1,0:T(8,128)(2,1)S(1)} %collective-permute-done.12.refs_2_, ...), custom_call_target="tpu_custom_call" | custom-call | flops 100000000 | tf_op jit(solution)/shard_map/combine_second_early/pallas_call | solution.py:406
  36.4 1.7 %collective-permute-done.10.refs_0_ = bf16[1,264,128]{2,1,0:T(8,128)(2,1)S(1)} collective-permute-done((bf16[1,264,128]{2,1,0:T(8,128)(2,1)S(1)}, bf16[1,264,128]{2,1,0:T(8,128)(2,1)S(1)}, u32[]{:S(2)}, u32[]{:S(2)}) %collective-permute-start.10) | collective-permute-done | bytes 67616 | tf_op jit(solution)/shard_map/ppermute | solution.py:275
  38.1 0.8 %combine_second.1 = bf16[4,128,256]{2,1,0:T(8,128)(2,1)} custom-call(bf16[1,264,128]{2,1,0:T(8,128)(2,1)S(1)} %collective-permute-done.10.refs_0_, s32[8,128]{1,0:T(8,128)S(1)} %get-tuple-element.27.refs_4_.refs_1_, f32[4,128,256]{2,1,0:T(8,128)S(1)} %get-tuple-element.44.refs_2_, f32[8,128]{1,0:T(8,128)S(1)} %get-tuple-element.45.refs_3_), custom_call_target="tpu_custom_call" | custom-call | tf_op jit(solution)/shard_map/combine_second/pallas_call | solution.py:406
  (1 shorter events, 0.0 us)
Async XLA Ops:
  0.6 2.5 %copy-start = (bf16[8,256,256]{2,1,0:T(8,128)(2,1)S(1)}, bf16[8,256,256]{2,1,0:T(8,128)(2,1)}, u32[]{:S(2)}) copy-start(bf16[8,256,256]{2,1,0:T(8,128)(2,1)} %refs_2_.3) | copy-start | bytes 3145732
  0.6 2.5 %collective-permute-start = (bf16[4,128,256]{2,1,0:T(8,128)(2,1)}, bf16[4,128,256]{2,1,0:T(8,128)(2,1)S(1)}, u32[]{:S(2)}, u32[]{:S(2)}) collective-permute-start(bf16[4,128,256]{2,1,0:T(8,128)(2,1)} %psi_hbm.1), channel_id=1, source_target_pairs={{1,0},{0,1},{3,2},{2,3},{5,4},{4,5},{7,6},{6,7},{9,8},{8,9},{11,10... | collective-permute-start | bytes 786440 | tf_op jit(solution)/shard_map/ppermute | solution.py:437
  1.2 1.9 %collective-permute-start.1 = (f32[4,128]{1,0:T(4,128)}, f32[4,128]{1,0:T(4,128)S(1)}, u32[]{:S(2)}, u32[]{:S(2)}) collective-permute-start(f32[4,128]{1,0:T(4,128)} %energy_hbm.1), channel_id=1, source_target_pairs={{1,0},{0,1},{3,2},{2,3},{5,4},{4,5},{7,6},{6,7},{9,8},{8,9},{11,10... | collective-permute-start | bytes 6152 | tf_op jit(solution)/shard_map/ppermute | solution.py:437
  4.7 8.5 %collective-permute-start.5 = (bf16[264,128]{1,0:T(8,128)(2,1)S(1)}, bf16[264,128]{1,0:T(8,128)(2,1)S(1)}, u32[]{:S(2)}, u32[]{:S(2)}) collective-permute-start(bf16[264,128]{1,0:T(8,128)(2,1)S(1)} %get-tuple-element.32), channel_id=1, source_target_pairs={{0,4},{4,8},{8,12},{12,0},{1,5},{5,9},{9,13},{13,1},{2,6},{6,10},{... | collective-permute-start | bytes 202760 | tf_op jit(solution)/shard_map/ppermute | solution.py:283
  7.8 7.4 %collective-permute-start.2 = (bf16[264,128]{1,0:T(8,128)(2,1)S(1)}, bf16[264,128]{1,0:T(8,128)(2,1)S(1)}, u32[]{:S(2)}, u32[]{:S(2)}) collective-permute-start(bf16[264,128]{1,0:T(8,128)(2,1)S(1)} %get-tuple-element.29), channel_id=1, source_target_pairs={{0,8},{4,12},{8,0},{12,4},{1,9},{5,13},{9,1},{13,5},{2,10},{6,14},... | collective-permute-start | bytes 202760 | tf_op jit(solution)/shard_map/ppermute | solution.py:283
  10.4 5.0 %collective-permute-start.3 = (bf16[264,128]{1,0:T(8,128)(2,1)S(1)}, bf16[264,128]{1,0:T(8,128)(2,1)S(1)}, u32[]{:S(2)}, u32[]{:S(2)}) collective-permute-start(bf16[264,128]{1,0:T(8,128)(2,1)S(1)} %get-tuple-element.30), channel_id=1, source_target_pairs={{0,12},{4,0},{8,4},{12,8},{1,13},{5,1},{9,5},{13,9},{2,14},{6,2},{... | collective-permute-start | bytes 202760 | tf_op jit(solution)/shard_map/ppermute | solution.py:283
  11.7 5.3 %collective-permute-start.6 = (bf16[1,264,128]{2,1,0:T(8,128)(2,1)S(1)}, bf16[1,264,128]{2,1,0:T(8,128)(2,1)S(1)}, u32[]{:S(2)}, u32[]{:S(2)}) collective-permute-start(bf16[1,264,128]{2,1,0:T(8,128)(2,1)S(1)} %bitcast.15), channel_id=1, source_target_pairs={{0,2},{2,0},{1,3},{3,1},{4,6},{6,4},{5,7},{7,5},{8,10},{10,8},{9,1... | collective-permute-start | bytes 202760 | tf_op jit(solution)/shard_map/ppermute | solution.py:275
  13.2 4.3 %collective-permute-start.7 = (bf16[1,264,128]{2,1,0:T(8,128)(2,1)S(1)}, bf16[1,264,128]{2,1,0:T(8,128)(2,1)S(1)}, u32[]{:S(2)}, u32[]{:S(2)}) collective-permute-start(bf16[1,264,128]{2,1,0:T(8,128)(2,1)S(1)} %bitcast.16), channel_id=1, source_target_pairs={{0,2},{2,0},{1,3},{3,1},{4,6},{6,4},{5,7},{7,5},{8,10},{10,8},{9,1... | collective-permute-start | bytes 202760 | tf_op jit(solution)/shard_map/ppermute | solution.py:275
  15.4 5.2 %collective-permute-start.4 = (bf16[2,264,128]{2,1,0:T(8,128)(2,1)S(1)}, bf16[2,264,128]{2,1,0:T(8,128)(2,1)S(1)}, u32[]{:S(2)}, u32[]{:S(2)}) collective-permute-start(bf16[2,264,128]{2,1,0:T(8,128)(2,1)S(1)} %pad_maximum_fusion), channel_id=1, source_target_pairs={{0,2},{2,0},{1,3},{3,1},{4,6},{6,4},{5,7},{7,5},{8,10},{10,8},{9,1... | collective-permute-start | bytes 405512 | tf_op jit(solution)/shard_map/ppermute | solution.py:275
  21.1 1.6 %collective-permute-start.8 = (bf16[528,256]{1,0:T(8,128)(2,1)S(1)}, bf16[528,256]{1,0:T(8,128)(2,1)S(1)}, u32[]{:S(2)}, u32[]{:S(2)}) collective-permute-start(bf16[528,256]{1,0:T(8,128)(2,1)S(1)} %get-tuple-element.37.refs_4_.refs_7_), channel_id=1, source_target_pairs={{1,0},{0,1},{3,2},{2,3},{5,4},{4,5},{7,6},{6,7},{9,8},{8,9},{11,10... | collective-permute-start | bytes 811016 | tf_op jit(solution)/shard_map/ppermute | solution.py:437
  24.2 6.1 %collective-permute-start.11 = (bf16[264,128]{1,0:T(8,128)(2,1)S(1)}, bf16[264,128]{1,0:T(8,128)(2,1)S(1)}, u32[]{:S(2)}, u32[]{:S(2)}) collective-permute-start(bf16[264,128]{1,0:T(8,128)(2,1)S(1)} %get-tuple-element.41), channel_id=1, source_target_pairs={{0,8},{4,12},{8,0},{12,4},{1,9},{5,13},{9,1},{13,5},{2,10},{6,14},... | collective-permute-start | bytes 202760 | tf_op jit(solution)/shard_map/ppermute | solution.py:283
  25.3 5.8 %collective-permute-start.12 = (bf16[264,128]{1,0:T(8,128)(2,1)S(1)}, bf16[264,128]{1,0:T(8,128)(2,1)S(1)}, u32[]{:S(2)}, u32[]{:S(2)}) collective-permute-start(bf16[264,128]{1,0:T(8,128)(2,1)S(1)} %get-tuple-element.42), channel_id=1, source_target_pairs={{0,4},{4,0},{8,12},{12,8},{1,5},{5,1},{9,13},{13,9},{2,6},{6,2},{1... | collective-permute-start | bytes 202760 | tf_op jit(solution)/shard_map/ppermute | solution.py:283
  27.6 6.2 %collective-permute-start.9 = (bf16[264,128]{1,0:T(8,128)(2,1)S(1)}, bf16[264,128]{1,0:T(8,128)(2,1)S(1)}, u32[]{:S(2)}, u32[]{:S(2)}) collective-permute-start(bf16[264,128]{1,0:T(8,128)(2,1)S(1)} %get-tuple-element.39), channel_id=1, source_target_pairs={{0,12},{4,8},{8,4},{12,0},{1,13},{5,9},{9,5},{13,1},{2,14},{6,10},... | collective-permute-start | bytes 202760 | tf_op jit(solution)/shard_map/ppermute | solution.py:283
  28.7 6.6 %collective-permute-start.13 = (bf16[1,264,128]{2,1,0:T(8,128)(2,1)S(1)}, bf16[1,264,128]{2,1,0:T(8,128)(2,1)S(1)}, u32[]{:S(2)}, u32[]{:S(2)}) collective-permute-start(bf16[1,264,128]{2,1,0:T(8,128)(2,1)S(1)} %bitcast.9), channel_id=1, source_target_pairs={{0,2},{2,0},{1,3},{3,1},{4,6},{6,4},{5,7},{7,5},{8,10},{10,8},{9,1... | collective-permute-start | bytes 202760 | tf_op jit(solution)/shard_map/ppermute | solution.py:275
  30.3 5.0 %collective-permute-start.14 = (bf16[1,264,128]{2,1,0:T(8,128)(2,1)S(1)}, bf16[1,264,128]{2,1,0:T(8,128)(2,1)S(1)}, u32[]{:S(2)}, u32[]{:S(2)}) collective-permute-start(bf16[1,264,128]{2,1,0:T(8,128)(2,1)S(1)} %bitcast.10), channel_id=1, source_target_pairs={{0,2},{2,0},{1,3},{3,1},{4,6},{6,4},{5,7},{7,5},{8,10},{10,8},{9,1... | collective-permute-start | bytes 202760 | tf_op jit(solution)/shard_map/ppermute | solution.py:275
  31.0 4.8 %collective-permute-start.15 = (bf16[1,264,128]{2,1,0:T(8,128)(2,1)S(1)}, bf16[1,264,128]{2,1,0:T(8,128)(2,1)S(1)}, u32[]{:S(2)}, u32[]{:S(2)}) collective-permute-start(bf16[1,264,128]{2,1,0:T(8,128)(2,1)S(1)} %bitcast.11), channel_id=1, source_target_pairs={{0,2},{2,0},{1,3},{3,1},{4,6},{6,4},{5,7},{7,5},{8,10},{10,8},{9,1... | collective-permute-start | bytes 202760 | tf_op jit(solution)/shard_map/ppermute | solution.py:275
  33.8 4.3 %collective-permute-start.10 = (bf16[1,264,128]{2,1,0:T(8,128)(2,1)S(1)}, bf16[1,264,128]{2,1,0:T(8,128)(2,1)S(1)}, u32[]{:S(2)}, u32[]{:S(2)}) collective-permute-start(bf16[1,264,128]{2,1,0:T(8,128)(2,1)S(1)} %bitcast.12), channel_id=1, source_target_pairs={{0,2},{2,0},{1,3},{3,1},{4,6},{6,4},{5,7},{7,5},{8,10},{10,8},{9,1... | collective-permute-start | bytes 202760 | tf_op jit(solution)/shard_map/ppermute | solution.py:275

commit v3 on v1

--- a/solution.py
+++ b/solution.py
@@ -424,7 +424,8 @@
     can_pair = sec_count & (sec_count - 1) == 0
     steps = list(range(1, sec_count))
     first_plan = (False, steps, [[0]] + [[k] for k in steps[:-2]] + [steps[-2:]])
-    second_plan = (can_pair, steps[::-1], [[0]] + [[k] for k in steps[::-1]])
+    second_groups = [[0]] + [[k] for k in steps[1:2] + steps[:1] + steps[2:]]
+    second_plan = (can_pair, steps[1:] + steps[:1], [[0], steps[1:2], steps[2:] + steps[:1]])
     params = pltpu.CompilerParams(vmem_limit_bytes=VMEM_BYTES)
     vec_shape = (sec_dev, half, width)
     vec_bf16 = jax.ShapeDtypeStruct(vec_shape, BF16)

time: 41 us -> 39.7 us (0.968)
  waiting for transfers between devices: 12 us -> 11.2 us
  starting transfers between devices: 21 us -> 20.5 us
    ppermute x6, waiting for transfers between devices: 3.95 us -> 3.12 us  [exchange(): arrived[step] = lax.ppermute(packets[step], 'sec', turn)]
    ppermute x7 -> x6, starting transfers between devices: 8.89 us -> 8.38 us  [exchange(): lax.ppermute(packet, 'op', turn)]
    ppermute x7 -> x6, waiting for transfers between devices: 6.55 us -> 6.52 us  [exchange(): lax.ppermute(packet, 'op', turn)]
  transfers between devices with their start and end apart: 16 -> 15, of which waited for: 9 -> 9; matrix products, arithmetic and copies ran while one was open for 0% -> 0% of each run, Pallas kernels for 7% -> 7%
where the time goes in v3:
time: 39.7 us; the launch traced here: 39.5 us
  starting transfers between devices  20.5 us (52%)
  waiting for transfers between devices  11.2 us (28%)
  Pallas kernels  7.13 us (18%)
  between operations  0.72 us (2%)
    ppermute x6, starting transfers between devices, exchange(): arrived[step] = lax.ppermute(packets[step], 'sec', turn)  11.4 us
    ppermute x6, starting transfers between devices, exchange(): lax.ppermute(packet, 'op', turn)  8.38 us
    ppermute x6, waiting for transfers between devices, exchange(): lax.ppermute(packet, 'op', turn)  6.52 us
    pallas_call x2, Pallas kernels, sigma_packets(): pl.pallas_call(functools.partial(product_kernel, is_first, split, paired,...  3.16 us
    ppermute x6, waiting for transfers between devices, exchange(): arrived[step] = lax.ppermute(packets[step], 'sec', turn)  3.12 us
    pallas_call x4, Pallas kernels, call(): pl.pallas_call(kernel, out_shape=outs, in_specs=[whole(pltpu.VMEM)] * len...  2.12 us
    pallas_call x1, Pallas kernels, body(): pl.pallas_call(load_kernel, out_shape=[vec_bf16, jax.ShapeDtypeStruct(lef...  1.84 us
    ppermute x3, waiting for transfers between devices, from_others(): arrays.append(lax.ppermute(array, 'rep', turn))  1.54 us
  transfers between devices with their start and end apart: 15, of which 9 were waited for; matrix products, arithmetic and copies ran while one was open for 0% of the time, Pallas kernels for 7%

profile of v3, /device:TPU:0, one launch (start us, length us, event | category | flops | bytes accessed | tf_op | source)
XLA Modules:
  0.0 39.5 jit_solution(7152704972268655142)
XLA Ops:
  0.6 0.0 copy-start
  0.6 0.5 %collective-permute-start = (bf16[4,128,256]{2,1,0:T(8,128)(2,1)}, bf16[4,128,256]{2,1,0:T(8,128)(2,1)S(1)}, u32[]{:S(2)}, u32[]{:S(2)}) collective-permute-start(bf16[4,128,256]{2,1,0:T(8,128)(2,1)} %psi_hbm.1), channel_id=1, source_target_pairs={{1,0},{0,1},{3,2},{2,3},{5,4},{4,5},{7,6},{6,7},{9,8},{8,9},{11,10... | collective-permute-start | bytes 786440 | tf_op jit(solution)/shard_map/ppermute | solution.py:437
  1.2 0.1 collective-permute-start.1
  1.2 1.8 %load.1 = (bf16[4,128,256]{2,1,0:T(8,128)(2,1)S(1)}, bf16[8,4,128,256]{3,2,1,0:T(8,128)(2,1)S(1)}, s32[4,128]{1,0:T(4,128)S(1)}, s32[8,128]{1,0:T(8,128)S(1)}, f...) custom-call(bf16[4,128,256]{2,1,0:T(8,128)(2,1)} %psi_hbm.1, bf16[8,4,128,256]{3,2,1,0:T(8,128)(2,1)} %left_hbm.1, ...), custom_call_target="tpu_custom_call" | custom-call | tf_op jit(solution)/shard_map/load/pallas_call | solution.py:442
  3.1 0.0 collective-permute-done.1.refs_7_
  3.1 0.0 collective-permute-done.refs_6_
  3.1 0.0 copy-done
  3.1 1.6 %products_first.1 = (bf16[264,128]{1,0:T(8,128)(2,1)S(1)}, bf16[264,128]{1,0:T(8,128)(2,1)S(1)}, bf16[264,128]{1,0:T(8,128)(2,1)S(1)}, bf16[264,128]{1,0:T(8,128)(2,1)S(1)}) custom-call(s32[4,128]{1,0:T(4,128)S(1)} %get-tuple-element.24.refs_0_, bf16[8,4,128,256]{3,2,1,0:T(8,128)(2,1)S(1)} %get-tuple-element.25.refs_1_, bf16[8,256,256]{2,1,0:T(8,128)(2,1)S(1)} %copy-done, ...), custom_call_target="tpu_custom_call" | custom-call | flops 1073741824 | bytes 3145728 | tf_op jit(solution)/shard_map/products_first/pallas_call | solution.py:249
  4.7 3.1 %collective-permute-start.5 = (bf16[264,128]{1,0:T(8,128)(2,1)S(1)}, bf16[264,128]{1,0:T(8,128)(2,1)S(1)}, u32[]{:S(2)}, u32[]{:S(2)}) collective-permute-start(bf16[264,128]{1,0:T(8,128)(2,1)S(1)} %get-tuple-element.32), channel_id=1, source_target_pairs={{0,4},{4,8},{8,12},{12,0},{1,5},{5,9},{9,13},{13,1},{2,6},{6,10},{... | collective-permute-start | bytes 202760 | tf_op jit(solution)/shard_map/ppermute | solution.py:283
  7.8 2.6 %collective-permute-start.2 = (bf16[264,128]{1,0:T(8,128)(2,1)S(1)}, bf16[264,128]{1,0:T(8,128)(2,1)S(1)}, u32[]{:S(2)}, u32[]{:S(2)}) collective-permute-start(bf16[264,128]{1,0:T(8,128)(2,1)S(1)} %get-tuple-element.29), channel_id=1, source_target_pairs={{0,8},{4,12},{8,0},{12,4},{1,9},{5,13},{9,1},{13,5},{2,10},{6,14},... | collective-permute-start | bytes 202760 | tf_op jit(solution)/shard_map/ppermute | solution.py:283
  10.4 1.4 %collective-permute-start.3 = (bf16[264,128]{1,0:T(8,128)(2,1)S(1)}, bf16[264,128]{1,0:T(8,128)(2,1)S(1)}, u32[]{:S(2)}, u32[]{:S(2)}) collective-permute-start(bf16[264,128]{1,0:T(8,128)(2,1)S(1)} %get-tuple-element.30), channel_id=1, source_target_pairs={{0,12},{4,0},{8,4},{12,8},{1,13},{5,1},{9,5},{13,9},{2,14},{6,2},{... | collective-permute-start | bytes 202760 | tf_op jit(solution)/shard_map/ppermute | solution.py:283
  11.7 1.5 %collective-permute-start.6 = (bf16[1,264,128]{2,1,0:T(8,128)(2,1)S(1)}, bf16[1,264,128]{2,1,0:T(8,128)(2,1)S(1)}, u32[]{:S(2)}, u32[]{:S(2)}) collective-permute-start(bf16[1,264,128]{2,1,0:T(8,128)(2,1)S(1)} %bitcast.14), channel_id=1, source_target_pairs={{0,2},{2,0},{1,3},{3,1},{4,6},{6,4},{5,7},{7,5},{8,10},{10,8},{9,1... | collective-permute-start | bytes 202760 | tf_op jit(solution)/shard_map/ppermute | solution.py:275
  13.2 0.0 collective-permute-done.5.refs_1_
  13.2 0.8 %collective-permute-start.7 = (bf16[1,264,128]{2,1,0:T(8,128)(2,1)S(1)}, bf16[1,264,128]{2,1,0:T(8,128)(2,1)S(1)}, u32[]{:S(2)}, u32[]{:S(2)}) collective-permute-start(bf16[1,264,128]{2,1,0:T(8,128)(2,1)S(1)} %bitcast.16), channel_id=1, source_target_pairs={{0,2},{2,0},{1,3},{3,1},{4,6},{6,4},{5,7},{7,5},{8,10},{10,8},{9,1... | collective-permute-start | bytes 202760 | tf_op jit(solution)/shard_map/ppermute | solution.py:275
  14.1 1.1 %collective-permute-done.2.refs_2_ = bf16[264,128]{1,0:T(8,128)(2,1)S(1)} collective-permute-done((bf16[264,128]{1,0:T(8,128)(2,1)S(1)}, bf16[264,128]{1,0:T(8,128)(2,1)S(1)}, u32[]{:S(2)}, u32[]{:S(2)}) %collective-permute-start.2) | collective-permute-done | bytes 67616 | tf_op jit(solution)/shard_map/ppermute | solution.py:283
  15.2 0.2 collective-permute-done.3.refs_3_
  15.4 1.6 %collective-permute-start.4 = (bf16[2,264,128]{2,1,0:T(8,128)(2,1)S(1)}, bf16[2,264,128]{2,1,0:T(8,128)(2,1)S(1)}, u32[]{:S(2)}, u32[]{:S(2)}) collective-permute-start(bf16[2,264,128]{2,1,0:T(8,128)(2,1)S(1)} %pad_maximum_fusion), channel_id=1, source_target_pairs={{0,2},{2,0},{1,3},{3,1},{4,6},{6,4},{5,7},{7,5},{8,10},{10,8},{9,1... | collective-permute-start | bytes 405512 | tf_op jit(solution)/shard_map/ppermute | solution.py:275
  17.0 0.0 collective-permute-done.6.refs_4_
  17.0 0.5 %collective-permute-done.7.refs_5_ = bf16[1,264,128]{2,1,0:T(8,128)(2,1)S(1)} collective-permute-done((bf16[1,264,128]{2,1,0:T(8,128)(2,1)S(1)}, bf16[1,264,128]{2,1,0:T(8,128)(2,1)S(1)}, u32[]{:S(2)}, u32[]{:S(2)}) %collective-permute-start.7) | collective-permute-done | bytes 67616 | tf_op jit(solution)/shard_map/ppermute | solution.py:275
  17.5 0.4 combine_first_early.1
  17.9 2.8 %collective-permute-done.4.refs_0_ = bf16[2,264,128]{2,1,0:T(8,128)(2,1)S(1)} collective-permute-done((bf16[2,264,128]{2,1,0:T(8,128)(2,1)S(1)}, bf16[2,264,128]{2,1,0:T(8,128)(2,1)S(1)}, u32[]{:S(2)}, u32[]{:S(2)}) %collective-permute-start.4) | collective-permute-done | bytes 135200 | tf_op jit(solution)/shard_map/ppermute | solution.py:275
  20.7 0.4 %combine_first.1 = (bf16[4,128,256]{2,1,0:T(8,128)(2,1)S(1)}, f32[4,128,256]{2,1,0:T(8,128)S(1)}, bf16[528,256]{1,0:T(8,128)(2,1)S(1)}) custom-call(bf16[2,264,128]{2,1,0:T(8,128)(2,1)S(1)} %collective-permute-done.4.refs_0_, s32[8,128]{1,0:T(8,128)S(1)} %get-tuple-element.27.refs_4_.refs_1_, ...), custom_call_target="tpu_custom_call" | custom-call | tf_op jit(solution)/shard_map/combine_first/pallas_call | solution.py:406
  21.1 0.1 collective-permute-start.8
  21.2 1.5 %collective-permute-done.8.refs_5_ = bf16[528,256]{1,0:T(8,128)(2,1)S(1)} collective-permute-done((bf16[528,256]{1,0:T(8,128)(2,1)S(1)}, bf16[528,256]{1,0:T(8,128)(2,1)S(1)}, u32[]{:S(2)}, u32[]{:S(2)}) %collective-permute-start.8) | collective-permute-done | bytes 270368 | tf_op jit(solution)/shard_map/ppermute | solution.py:437
  22.7 1.6 %products_second.1 = (bf16[264,128]{1,0:T(8,128)(2,1)S(1)}, bf16[264,128]{1,0:T(8,128)(2,1)S(1)}, bf16[264,128]{1,0:T(8,128)(2,1)S(1)}, bf16[264,128]{1,0:T(8,128)(2,1)S(1)}, bf16[4,128,256]{2,1,0:T(8,128)(2,1)}) custom-call(s32[4,128]{1,0:T(4,128)S(1)} %get-tuple-element.24.refs_0_, bf16[8,4,128,256]{3,2,1,0:T(8,128)(2,1)S(1)} %get-tuple-element.25.refs_1_, ...), custom_call_target="tpu_custom_call" | custom-call | flops 1073741824 | bytes 3145728 | tf_op jit(solution)/shard_map/products_second/pallas_call | solution.py:249
  24.3 1.1 %collective-permute-start.12 = (bf16[264,128]{1,0:T(8,128)(2,1)S(1)}, bf16[264,128]{1,0:T(8,128)(2,1)S(1)}, u32[]{:S(2)}, u32[]{:S(2)}) collective-permute-start(bf16[264,128]{1,0:T(8,128)(2,1)S(1)} %get-tuple-element.42), channel_id=1, source_target_pairs={{0,8},{4,12},{8,0},{12,4},{1,9},{5,13},{9,1},{13,5},{2,10},{6,14},... | collective-permute-start | bytes 202760 | tf_op jit(solution)/shard_map/ppermute | solution.py:283
  25.3 3.4 %collective-permute-start.9 = (bf16[264,128]{1,0:T(8,128)(2,1)S(1)}, bf16[264,128]{1,0:T(8,128)(2,1)S(1)}, u32[]{:S(2)}, u32[]{:S(2)}) collective-permute-start(bf16[264,128]{1,0:T(8,128)(2,1)S(1)} %get-tuple-element.39), channel_id=1, source_target_pairs={{0,12},{4,8},{8,4},{12,0},{1,13},{5,9},{9,5},{13,1},{2,14},{6,10},... | collective-permute-start | bytes 202760 | tf_op jit(solution)/shard_map/ppermute | solution.py:283
  28.7 0.0 collective-permute-start.10
  28.7 1.5 %collective-permute-start.13 = (bf16[1,264,128]{2,1,0:T(8,128)(2,1)S(1)}, bf16[1,264,128]{2,1,0:T(8,128)(2,1)S(1)}, u32[]{:S(2)}, u32[]{:S(2)}) collective-permute-start(bf16[1,264,128]{2,1,0:T(8,128)(2,1)S(1)} %bitcast.13), channel_id=1, source_target_pairs={{0,2},{2,0},{1,3},{3,1},{4,6},{6,4},{5,7},{7,5},{8,10},{10,8},{9,1... | collective-permute-start | bytes 202760 | tf_op jit(solution)/shard_map/ppermute | solution.py:275
  30.2 1.7 %collective-permute-done.12.refs_1_ = bf16[264,128]{1,0:T(8,128)(2,1)S(1)} collective-permute-done((bf16[264,128]{1,0:T(8,128)(2,1)S(1)}, bf16[264,128]{1,0:T(8,128)(2,1)S(1)}, u32[]{:S(2)}, u32[]{:S(2)}) %collective-permute-start.12) | collective-permute-done | bytes 67616 | tf_op jit(solution)/shard_map/ppermute | solution.py:283
  31.9 1.5 %collective-permute-start.14 = (bf16[1,264,128]{2,1,0:T(8,128)(2,1)S(1)}, bf16[1,264,128]{2,1,0:T(8,128)(2,1)S(1)}, u32[]{:S(2)}, u32[]{:S(2)}) collective-permute-start(bf16[1,264,128]{2,1,0:T(8,128)(2,1)S(1)} %bitcast.15), channel_id=1, source_target_pairs={{0,2},{2,0},{1,3},{3,1},{4,6},{6,4},{5,7},{7,5},{8,10},{10,8},{9,1... | collective-permute-start | bytes 202760 | tf_op jit(solution)/shard_map/ppermute | solution.py:275
  33.4 0.0 collective-permute-done.9.refs_2_
  33.4 0.1 collective-permute-done.10.refs_3_
  33.4 1.5 %collective-permute-start.11 = (bf16[2,264,128]{2,1,0:T(8,128)(2,1)S(1)}, bf16[2,264,128]{2,1,0:T(8,128)(2,1)S(1)}, u32[]{:S(2)}, u32[]{:S(2)}) collective-permute-start(bf16[2,264,128]{2,1,0:T(8,128)(2,1)S(1)} %pad_maximum_fusion.1), channel_id=1, source_target_pairs={{0,2},{2,0},{1,3},{3,1},{4,6},{6,4},{5,7},{7,5},{8,10},{10,8},{9,1... | collective-permute-start | bytes 405512 | tf_op jit(solution)/shard_map/ppermute | solution.py:275
  35.0 0.0 collective-permute-done.13.refs_4_
  35.0 1.8 %collective-permute-done.14.refs_5_ = bf16[1,264,128]{2,1,0:T(8,128)(2,1)S(1)} collective-permute-done((bf16[1,264,128]{2,1,0:T(8,128)(2,1)S(1)}, bf16[1,264,128]{2,1,0:T(8,128)(2,1)S(1)}, u32[]{:S(2)}, u32[]{:S(2)}) %collective-permute-start.14) | collective-permute-done | bytes 67616 | tf_op jit(solution)/shard_map/ppermute | solution.py:275
  36.8 0.4 %combine_second_early.1 = (f32[4,128,256]{2,1,0:T(8,128)S(1)}, f32[8,128]{1,0:T(8,128)S(1)}) custom-call(bf16[264,128]{1,0:T(8,128)(2,1)S(1)} %get-tuple-element.41.refs_0_, bf16[264,128]{1,0:T(8,128)(2,1)S(1)} %collective-permute-done.12.refs_1_, bf16[264,128]{1,0:T(8,128)(2,1)S(1)} %collective-permute-done.9.refs_2_, ...), custom_call_target="tpu_custom_call" | custom-call | flops 1000000000 | tf_op jit(solution)/shard_map/combine_second_early/pallas_call | solution.py:406
  37.2 1.4 %collective-permute-done.11.refs_0_ = bf16[2,264,128]{2,1,0:T(8,128)(2,1)S(1)} collective-permute-done((bf16[2,264,128]{2,1,0:T(8,128)(2,1)S(1)}, bf16[2,264,128]{2,1,0:T(8,128)(2,1)S(1)}, u32[]{:S(2)}, u32[]{:S(2)}) %collective-permute-start.11) | collective-permute-done | bytes 135200 | tf_op jit(solution)/shard_map/ppermute | solution.py:275
  38.6 0.9 %combine_second.1 = bf16[4,128,256]{2,1,0:T(8,128)(2,1)} custom-call(bf16[2,264,128]{2,1,0:T(8,128)(2,1)S(1)} %collective-permute-done.11.refs_0_, s32[8,128]{1,0:T(8,128)S(1)} %get-tuple-element.27.refs_4_.refs_1_, f32[4,128,256]{2,1,0:T(8,128)S(1)} %get-tuple-element.44.refs_2_, f32[8,128]{1,0:T(8,128)S(1)} %get-tuple-element.45.refs_3_), custom_call_target="tpu_custom_call" | custom-call | tf_op jit(solution)/shard_map/combine_second/pallas_call | solution.py:406
  (2 shorter events, 0.0 us)
Async XLA Ops:
  0.6 2.5 %copy-start = (bf16[8,256,256]{2,1,0:T(8,128)(2,1)S(1)}, bf16[8,256,256]{2,1,0:T(8,128)(2,1)}, u32[]{:S(2)}) copy-start(bf16[8,256,256]{2,1,0:T(8,128)(2,1)} %refs_2_.3) | copy-start | bytes 3145732
  0.6 2.5 %collective-permute-start = (bf16[4,128,256]{2,1,0:T(8,128)(2,1)}, bf16[4,128,256]{2,1,0:T(8,128)(2,1)S(1)}, u32[]{:S(2)}, u32[]{:S(2)}) collective-permute-start(bf16[4,128,256]{2,1,0:T(8,128)(2,1)} %psi_hbm.1), channel_id=1, source_target_pairs={{1,0},{0,1},{3,2},{2,3},{5,4},{4,5},{7,6},{6,7},{9,8},{8,9},{11,10... | collective-permute-start | bytes 786440 | tf_op jit(solution)/shard_map/ppermute | solution.py:437
  1.2 1.9 %collective-permute-start.1 = (f32[4,128]{1,0:T(4,128)}, f32[4,128]{1,0:T(4,128)S(1)}, u32[]{:S(2)}, u32[]{:S(2)}) collective-permute-start(f32[4,128]{1,0:T(4,128)} %energy_hbm.1), channel_id=1, source_target_pairs={{1,0},{0,1},{3,2},{2,3},{5,4},{4,5},{7,6},{6,7},{9,8},{8,9},{11,10... | collective-permute-start | bytes 6152 | tf_op jit(solution)/shard_map/ppermute | solution.py:437
  4.7 8.5 %collective-permute-start.5 = (bf16[264,128]{1,0:T(8,128)(2,1)S(1)}, bf16[264,128]{1,0:T(8,128)(2,1)S(1)}, u32[]{:S(2)}, u32[]{:S(2)}) collective-permute-start(bf16[264,128]{1,0:T(8,128)(2,1)S(1)} %get-tuple-element.32), channel_id=1, source_target_pairs={{0,4},{4,8},{8,12},{12,0},{1,5},{5,9},{9,13},{13,1},{2,6},{6,10},{... | collective-permute-start | bytes 202760 | tf_op jit(solution)/shard_map/ppermute | solution.py:283
  7.8 7.4 %collective-permute-start.2 = (bf16[264,128]{1,0:T(8,128)(2,1)S(1)}, bf16[264,128]{1,0:T(8,128)(2,1)S(1)}, u32[]{:S(2)}, u32[]{:S(2)}) collective-permute-start(bf16[264,128]{1,0:T(8,128)(2,1)S(1)} %get-tuple-element.29), channel_id=1, source_target_pairs={{0,8},{4,12},{8,0},{12,4},{1,9},{5,13},{9,1},{13,5},{2,10},{6,14},... | collective-permute-start | bytes 202760 | tf_op jit(solution)/shard_map/ppermute | solution.py:283
  10.4 5.0 %collective-permute-start.3 = (bf16[264,128]{1,0:T(8,128)(2,1)S(1)}, bf16[264,128]{1,0:T(8,128)(2,1)S(1)}, u32[]{:S(2)}, u32[]{:S(2)}) collective-permute-start(bf16[264,128]{1,0:T(8,128)(2,1)S(1)} %get-tuple-element.30), channel_id=1, source_target_pairs={{0,12},{4,0},{8,4},{12,8},{1,13},{5,1},{9,5},{13,9},{2,14},{6,2},{... | collective-permute-start | bytes 202760 | tf_op jit(solution)/shard_map/ppermute | solution.py:283
  11.7 5.3 %collective-permute-start.6 = (bf16[1,264,128]{2,1,0:T(8,128)(2,1)S(1)}, bf16[1,264,128]{2,1,0:T(8,128)(2,1)S(1)}, u32[]{:S(2)}, u32[]{:S(2)}) collective-permute-start(bf16[1,264,128]{2,1,0:T(8,128)(2,1)S(1)} %bitcast.14), channel_id=1, source_target_pairs={{0,2},{2,0},{1,3},{3,1},{4,6},{6,4},{5,7},{7,5},{8,10},{10,8},{9,1... | collective-permute-start | bytes 202760 | tf_op jit(solution)/shard_map/ppermute | solution.py:275
  13.2 4.3 %collective-permute-start.7 = (bf16[1,264,128]{2,1,0:T(8,128)(2,1)S(1)}, bf16[1,264,128]{2,1,0:T(8,128)(2,1)S(1)}, u32[]{:S(2)}, u32[]{:S(2)}) collective-permute-start(bf16[1,264,128]{2,1,0:T(8,128)(2,1)S(1)} %bitcast.16), channel_id=1, source_target_pairs={{0,2},{2,0},{1,3},{3,1},{4,6},{6,4},{5,7},{7,5},{8,10},{10,8},{9,1... | collective-permute-start | bytes 202760 | tf_op jit(solution)/shard_map/ppermute | solution.py:275
  15.4 5.3 %collective-permute-start.4 = (bf16[2,264,128]{2,1,0:T(8,128)(2,1)S(1)}, bf16[2,264,128]{2,1,0:T(8,128)(2,1)S(1)}, u32[]{:S(2)}, u32[]{:S(2)}) collective-permute-start(bf16[2,264,128]{2,1,0:T(8,128)(2,1)S(1)} %pad_maximum_fusion), channel_id=1, source_target_pairs={{0,2},{2,0},{1,3},{3,1},{4,6},{6,4},{5,7},{7,5},{8,10},{10,8},{9,1... | collective-permute-start | bytes 405512 | tf_op jit(solution)/shard_map/ppermute | solution.py:275
  21.1 1.6 %collective-permute-start.8 = (bf16[528,256]{1,0:T(8,128)(2,1)S(1)}, bf16[528,256]{1,0:T(8,128)(2,1)S(1)}, u32[]{:S(2)}, u32[]{:S(2)}) collective-permute-start(bf16[528,256]{1,0:T(8,128)(2,1)S(1)} %get-tuple-element.37.refs_4_.refs_6_), channel_id=1, source_target_pairs={{1,0},{0,1},{3,2},{2,3},{5,4},{4,5},{7,6},{6,7},{9,8},{8,9},{11,10... | collective-permute-start | bytes 811016 | tf_op jit(solution)/shard_map/ppermute | solution.py:437
  24.3 7.6 %collective-permute-start.12 = (bf16[264,128]{1,0:T(8,128)(2,1)S(1)}, bf16[264,128]{1,0:T(8,128)(2,1)S(1)}, u32[]{:S(2)}, u32[]{:S(2)}) collective-permute-start(bf16[264,128]{1,0:T(8,128)(2,1)S(1)} %get-tuple-element.42), channel_id=1, source_target_pairs={{0,8},{4,12},{8,0},{12,4},{1,9},{5,13},{9,1},{13,5},{2,10},{6,14},... | collective-permute-start | bytes 202760 | tf_op jit(solution)/shard_map/ppermute | solution.py:283
  25.3 8.0 %collective-permute-start.9 = (bf16[264,128]{1,0:T(8,128)(2,1)S(1)}, bf16[264,128]{1,0:T(8,128)(2,1)S(1)}, u32[]{:S(2)}, u32[]{:S(2)}) collective-permute-start(bf16[264,128]{1,0:T(8,128)(2,1)S(1)} %get-tuple-element.39), channel_id=1, source_target_pairs={{0,12},{4,8},{8,4},{12,0},{1,13},{5,9},{9,5},{13,1},{2,14},{6,10},... | collective-permute-start | bytes 202760 | tf_op jit(solution)/shard_map/ppermute | solution.py:283
  28.7 4.7 %collective-permute-start.10 = (bf16[264,128]{1,0:T(8,128)(2,1)S(1)}, bf16[264,128]{1,0:T(8,128)(2,1)S(1)}, u32[]{:S(2)}, u32[]{:S(2)}) collective-permute-start(bf16[264,128]{1,0:T(8,128)(2,1)S(1)} %get-tuple-element.40), channel_id=1, source_target_pairs={{0,4},{4,0},{8,12},{12,8},{1,5},{5,1},{9,13},{13,9},{2,6},{6,2},{1... | collective-permute-start | bytes 202760 | tf_op jit(solution)/shard_map/ppermute | solution.py:283
  28.7 6.3 %collective-permute-start.13 = (bf16[1,264,128]{2,1,0:T(8,128)(2,1)S(1)}, bf16[1,264,128]{2,1,0:T(8,128)(2,1)S(1)}, u32[]{:S(2)}, u32[]{:S(2)}) collective-permute-start(bf16[1,264,128]{2,1,0:T(8,128)(2,1)S(1)} %bitcast.13), channel_id=1, source_target_pairs={{0,2},{2,0},{1,3},{3,1},{4,6},{6,4},{5,7},{7,5},{8,10},{10,8},{9,1... | collective-permute-start | bytes 202760 | tf_op jit(solution)/shard_map/ppermute | solution.py:275
  31.9 4.9 %collective-permute-start.14 = (bf16[1,264,128]{2,1,0:T(8,128)(2,1)S(1)}, bf16[1,264,128]{2,1,0:T(8,128)(2,1)S(1)}, u32[]{:S(2)}, u32[]{:S(2)}) collective-permute-start(bf16[1,264,128]{2,1,0:T(8,128)(2,1)S(1)} %bitcast.15), channel_id=1, source_target_pairs={{0,2},{2,0},{1,3},{3,1},{4,6},{6,4},{5,7},{7,5},{8,10},{10,8},{9,1... | collective-permute-start | bytes 202760 | tf_op jit(solution)/shard_map/ppermute | solution.py:275
  33.4 5.2 %collective-permute-start.11 = (bf16[2,264,128]{2,1,0:T(8,128)(2,1)S(1)}, bf16[2,264,128]{2,1,0:T(8,128)(2,1)S(1)}, u32[]{:S(2)}, u32[]{:S(2)}) collective-permute-start(bf16[2,264,128]{2,1,0:T(8,128)(2,1)S(1)} %pad_maximum_fusion.1), channel_id=1, source_target_pairs={{0,2},{2,0},{1,3},{3,1},{4,6},{6,4},{5,7},{7,5},{8,10},{10,8},{9,1... | collective-permute-start | bytes 405512 | tf_op jit(solution)/shard_map/ppermute | solution.py:275

commit v4 on v3

--- a/solution.py
+++ b/solution.py
@@ -11,6 +11,7 @@
 HEAD = 8
 PARTS = 3
 EARLY_FLOPS = 10**9
+VEC_PARTS = 2
 MORE_ROWS = 16
 LANES = 128
 VMEM_BYTES = 24 * 1024 * 1024
@@ -77,6 +78,11 @@
 def head_scalar(head_sum, index):
     first = 1 + PARTS * index
     return jnp.sum(head_sum[first:first + PARTS], axis=0, keepdims=True)
+
+
+def vec_place(s, sec_dev, half):
+    in_part = sec_dev // VEC_PARTS
+    return s // in_part, s % in_part * half
 
 
 def most_pairs(pairs, sec_count):
@@ -157,7 +163,7 @@
         level_refs = take(rep_count - 1)
     else:
         (first_ref,) = take(1)
-        vector_refs = take(rep_count)
+        vector_refs = [take(VEC_PARTS) for _ in range(rep_count)]
     out_refs = take(sec_count if split else 1)
     if not is_first:
         (first_hbm,) = take(1)
@@ -188,7 +194,8 @@
                 mask = live(limit_ref, s, first_row(step), (half, width))
                 blocks.append(jnp.where(mask, psi.astype(F32), 0.0).astype(BF16))
         else:
-            blocks = [ref[s * half:(s + 1) * half] for ref in vector_refs]
+            part, row = vec_place(s, sec_dev, half)
+            blocks = [parts[part][row:row + half] for parts in vector_refs]
         vector = jnp.concatenate(blocks, axis=0)
         for turn in range(1, rep_count):
             turned = blocks[rep_count - turn:] + blocks[:rep_count - turn]
@@ -207,7 +214,7 @@
     if is_first:
         scalars = [total(array) for array in folded]
     else:
-        head = sum(ref[sec_dev * half:].astype(F32) for ref in vector_refs)
+        head = sum(parts[-1][sec_dev // VEC_PARTS * half:].astype(F32) for parts in vector_refs)
         scalars = [head_scalar(head, i)[:, :LANES] for i in range(2)]
     fetch.wait()
     for d in range(sec_count):
@@ -352,7 +359,8 @@
 
 def first_kernel(count, *refs):
     packet_refs = refs[:count]
-    limit_ref, start_ref, base_ref, scalar_ref, first_ref, one_ref, vec_ref = refs[count:]
+    limit_ref, start_ref, base_ref, scalar_ref, first_ref, one_ref = refs[count:-VEC_PARTS]
+    vec_refs = refs[-VEC_PARTS:]
     sec_dev, half, width = start_ref.shape
     shift = spread(scalar_ref[1:2], width)
     first_row = lax.axis_index("rep") * half
@@ -365,19 +373,23 @@
         one_ref[s] = one
         first_ref[s] = one.astype(BF16)
         vector = one - shift * start
-        vec_ref[s * half:(s + 1) * half] = vector.astype(BF16)
+        part, row = vec_place(s, sec_dev, half)
+        vec_refs[part][row:row + half] = vector.astype(BF16)
         cross += fold(start * vector)
         square += fold(vector * vector)
     scalars = (total(cross), total(square))
-    vec_ref[sec_dev * half:] = header(jnp.int32(0), scalars, (MORE_ROWS, width))
+    more = header(jnp.int32(0), scalars, (MORE_ROWS, width))
+    vec_refs[-1][sec_dev // VEC_PARTS * half:] = more
 
 
 def second_early_kernel(split, count, entries, *refs):
     packet_refs = refs[:count]
-    vec_ref, energy_ref, one_ref, scalar_ref, base_ref, scale_ref = refs[count:]
+    vec_refs = refs[count:count + VEC_PARTS]
+    energy_ref, one_ref, scalar_ref, base_ref, scale_ref = refs[count + VEC_PARTS:]
     sec_dev, half, width = one_ref.shape
     for s in range(sec_dev):
-        vector = vec_ref[s * half:(s + 1) * half].astype(F32)
+        part, row = vec_place(s, sec_dev, half)
+        vector = vec_refs[part][row:row + half].astype(F32)
         base_ref[s] = spread(energy_ref[s], width) * vector
     head_sum = add_packets(packet_refs, split, half, base_ref)
     cross = head_scalar(head_sum, 0)
@@ -425,7 +437,7 @@
     steps = list(range(1, sec_count))
     first_plan = (False, steps, [[0]] + [[k] for k in steps[:-2]] + [steps[-2:]])
     second_groups = [[0]] + [[k] for k in steps[1:2] + steps[:1] + steps[2:]]
-    second_plan = (can_pair, steps[1:] + steps[:1], [[0], steps[1:2], steps[2:] + steps[:1]])
+    second_plan = (can_pair, steps[1:2] + steps[:1] + steps[2:], second_groups)
     params = pltpu.CompilerParams(vmem_limit_bytes=VMEM_BYTES)
     vec_shape = (sec_dev, half, width)
     vec_bf16 = jax.ShapeDtypeStruct(vec_shape, BF16)
@@ -480,24 +492,29 @@
         functools.partial(first_early_kernel, split, len(early)), "combine_first_early",
         [block_f32, row_f32], *early, start, levels, flops=EARLY_FLOPS,
     )
-    first, sigma_one, vector = call(
+    first, sigma_one, *vector = call(
         functools.partial(first_kernel, len(late)), "combine_first",
         [
             pltpu.VMEM(vec_shape, BF16),
             block_f32,
-            jax.ShapeDtypeStruct((sec_dev * half + MORE_ROWS, width), BF16),
+        ]
+        + [
+            jax.ShapeDtypeStruct(
+                (sec_dev // VEC_PARTS * half + (part + 1) // VEC_PARTS * MORE_ROWS, width), BF16
+            )
+            for part in range(VEC_PARTS)
         ],
         *late, limits, start, base, scalars,
     )
 
     *packets, first_out = sigma_packets(
         False, split, second_plan[0], rep_count, lists, left_env, right_env,
-        [first, vector, *from_others(vector)],
+        [first, *vector, *sum((list(other) for other in zip(*map(from_others, vector))), [])],
     )
     early, late = exchange(packets, split, *second_plan)
     base, scale = call(
         functools.partial(second_early_kernel, split, len(early), entries),
-        "combine_second_early", [block_f32, row_f32], *early, vector, levels, sigma_one, scalars,
+        "combine_second_early", [block_f32, row_f32], *early, *vector, levels, sigma_one, scalars,
         flops=EARLY_FLOPS,
     )
     (second_out,) = call(

time: 39.7 us -> 39.2 us (0.987)
  waiting for transfers between devices: 11.2 us -> 9.43 us
  starting transfers between devices: 20.5 us -> 21.8 us
    ppermute x6 -> x7, waiting for transfers between devices: 6.52 us -> 5.61 us  [exchange(): lax.ppermute(packet, 'op', turn)]
    ppermute x6 -> x7, starting transfers between devices: 8.38 us -> 9.17 us  [exchange(): lax.ppermute(packet, 'op', turn)]
    ppermute x3 -> x4, starting transfers between devices: 0.65 us -> 1.15 us  [from_others(): arrays.append(lax.ppermute(array, 'rep', turn))]
    ppermute x3 -> x4, waiting for transfers between devices: 1.54 us -> 1.04 us  [from_others(): arrays.append(lax.ppermute(array, 'rep', turn))]
  transfers between devices with their start and end apart: 15 -> 17, of which waited for: 9 -> 8; matrix products, arithmetic and copies ran while one was open for 0% -> 0% of each run, Pallas kernels for 7% -> 7%
where the time goes in v4:
time: 39.2 us; the launch traced here: 39.1 us
  starting transfers between devices  21.8 us (56%)
  waiting for transfers between devices  9.43 us (24%)
  Pallas kernels  7.14 us (18%)
  between operations  0.72 us (2%)
    ppermute x6, starting transfers between devices, exchange(): arrived[step] = lax.ppermute(packets[step], 'sec', turn)  11.4 us
    ppermute x7, starting transfers between devices, exchange(): lax.ppermute(packet, 'op', turn)  9.17 us
    ppermute x7, waiting for transfers between devices, exchange(): lax.ppermute(packet, 'op', turn)  5.61 us
    pallas_call x2, Pallas kernels, sigma_packets(): pl.pallas_call(functools.partial(product_kernel, is_first, split, paired,...  3.17 us
    ppermute x6, waiting for transfers between devices, exchange(): arrived[step] = lax.ppermute(packets[step], 'sec', turn)  2.78 us
    pallas_call x4, Pallas kernels, call(): pl.pallas_call(kernel, out_shape=outs, in_specs=[whole(pltpu.VMEM)] * len...  2.12 us
    pallas_call x1, Pallas kernels, body(): pl.pallas_call(load_kernel, out_shape=[vec_bf16, jax.ShapeDtypeStruct(lef...  1.84 us
    ppermute x4, starting transfers between devices, from_others(): arrays.append(lax.ppermute(array, 'rep', turn))  1.15 us
  transfers between devices with their start and end apart: 17, of which 8 were waited for; matrix products, arithmetic and copies ran while one was open for 0% of the time, Pallas kernels for 7%

profile of v4, /device:TPU:0, one launch (start us, length us, event | category | flops | bytes accessed | tf_op | source)
XLA Modules:
  0.0 39.1 jit_solution(378292303206804861)
XLA Ops:
  0.6 0.0 copy-start
  0.6 0.5 %collective-permute-start = (bf16[4,128,256]{2,1,0:T(8,128)(2,1)}, bf16[4,128,256]{2,1,0:T(8,128)(2,1)S(1)}, u32[]{:S(2)}, u32[]{:S(2)}) collective-permute-start(bf16[4,128,256]{2,1,0:T(8,128)(2,1)} %psi_hbm.1), channel_id=1, source_target_pairs={{1,0},{0,1},{3,2},{2,3},{5,4},{4,5},{7,6},{6,7},{9,8},{8,9},{11,10... | collective-permute-start | bytes 786440 | tf_op jit(solution)/shard_map/ppermute | solution.py:449
  1.2 0.1 collective-permute-start.1
  1.2 1.8 %load.1 = (bf16[4,128,256]{2,1,0:T(8,128)(2,1)S(1)}, bf16[8,4,128,256]{3,2,1,0:T(8,128)(2,1)S(1)}, s32[4,128]{1,0:T(4,128)S(1)}, s32[8,128]{1,0:T(8,128)S(1)}, f...) custom-call(bf16[4,128,256]{2,1,0:T(8,128)(2,1)} %psi_hbm.1, bf16[8,4,128,256]{3,2,1,0:T(8,128)(2,1)} %left_hbm.1, ...), custom_call_target="tpu_custom_call" | custom-call | tf_op jit(solution)/shard_map/load/pallas_call | solution.py:454
  3.1 0.0 collective-permute-done.1.refs_7_
  3.1 0.0 collective-permute-done.refs_6_
  3.1 0.0 copy-done
  3.1 1.6 %products_first.1 = (bf16[264,128]{1,0:T(8,128)(2,1)S(1)}, bf16[264,128]{1,0:T(8,128)(2,1)S(1)}, bf16[264,128]{1,0:T(8,128)(2,1)S(1)}, bf16[264,128]{1,0:T(8,128)(2,1)S(1)}) custom-call(s32[4,128]{1,0:T(4,128)S(1)} %get-tuple-element.25.refs_0_, bf16[8,4,128,256]{3,2,1,0:T(8,128)(2,1)S(1)} %get-tuple-element.26.refs_1_, bf16[8,256,256]{2,1,0:T(8,128)(2,1)S(1)} %copy-done, ...), custom_call_target="tpu_custom_call" | custom-call | flops 1073741824 | bytes 3145728 | tf_op jit(solution)/shard_map/products_first/pallas_call | solution.py:256
  4.7 3.0 %collective-permute-start.5 = (bf16[264,128]{1,0:T(8,128)(2,1)S(1)}, bf16[264,128]{1,0:T(8,128)(2,1)S(1)}, u32[]{:S(2)}, u32[]{:S(2)}) collective-permute-start(bf16[264,128]{1,0:T(8,128)(2,1)S(1)} %get-tuple-element.33), channel_id=1, source_target_pairs={{0,4},{4,8},{8,12},{12,0},{1,5},{5,9},{9,13},{13,1},{2,6},{6,10},{... | collective-permute-start | bytes 202760 | tf_op jit(solution)/shard_map/ppermute | solution.py:290
  7.8 2.6 %collective-permute-start.2 = (bf16[264,128]{1,0:T(8,128)(2,1)S(1)}, bf16[264,128]{1,0:T(8,128)(2,1)S(1)}, u32[]{:S(2)}, u32[]{:S(2)}) collective-permute-start(bf16[264,128]{1,0:T(8,128)(2,1)S(1)} %get-tuple-element.30), channel_id=1, source_target_pairs={{0,8},{4,12},{8,0},{12,4},{1,9},{5,13},{9,1},{13,5},{2,10},{6,14},... | collective-permute-start | bytes 202760 | tf_op jit(solution)/shard_map/ppermute | solution.py:290
  10.4 1.3 %collective-permute-start.3 = (bf16[264,128]{1,0:T(8,128)(2,1)S(1)}, bf16[264,128]{1,0:T(8,128)(2,1)S(1)}, u32[]{:S(2)}, u32[]{:S(2)}) collective-permute-start(bf16[264,128]{1,0:T(8,128)(2,1)S(1)} %get-tuple-element.31), channel_id=1, source_target_pairs={{0,12},{4,0},{8,4},{12,8},{1,13},{5,1},{9,5},{13,9},{2,14},{6,2},{... | collective-permute-start | bytes 202760 | tf_op jit(solution)/shard_map/ppermute | solution.py:290
  11.7 1.5 %collective-permute-start.6 = (bf16[1,264,128]{2,1,0:T(8,128)(2,1)S(1)}, bf16[1,264,128]{2,1,0:T(8,128)(2,1)S(1)}, u32[]{:S(2)}, u32[]{:S(2)}) collective-permute-start(bf16[1,264,128]{2,1,0:T(8,128)(2,1)S(1)} %bitcast.15), channel_id=1, source_target_pairs={{0,2},{2,0},{1,3},{3,1},{4,6},{6,4},{5,7},{7,5},{8,10},{10,8},{9,1... | collective-permute-start | bytes 202760 | tf_op jit(solution)/shard_map/ppermute | solution.py:282
  13.2 0.0 collective-permute-done.5.refs_1_
  13.2 0.8 %collective-permute-start.7 = (bf16[1,264,128]{2,1,0:T(8,128)(2,1)S(1)}, bf16[1,264,128]{2,1,0:T(8,128)(2,1)S(1)}, u32[]{:S(2)}, u32[]{:S(2)}) collective-permute-start(bf16[1,264,128]{2,1,0:T(8,128)(2,1)S(1)} %bitcast.16), channel_id=1, source_target_pairs={{0,2},{2,0},{1,3},{3,1},{4,6},{6,4},{5,7},{7,5},{8,10},{10,8},{9,1... | collective-permute-start | bytes 202760 | tf_op jit(solution)/shard_map/ppermute | solution.py:282
  14.1 1.1 %collective-permute-done.2.refs_2_ = bf16[264,128]{1,0:T(8,128)(2,1)S(1)} collective-permute-done((bf16[264,128]{1,0:T(8,128)(2,1)S(1)}, bf16[264,128]{1,0:T(8,128)(2,1)S(1)}, u32[]{:S(2)}, u32[]{:S(2)}) %collective-permute-start.2) | collective-permute-done | bytes 67616 | tf_op jit(solution)/shard_map/ppermute | solution.py:290
  15.2 0.2 collective-permute-done.3.refs_3_
  15.4 1.6 %collective-permute-start.4 = (bf16[2,264,128]{2,1,0:T(8,128)(2,1)S(1)}, bf16[2,264,128]{2,1,0:T(8,128)(2,1)S(1)}, u32[]{:S(2)}, u32[]{:S(2)}) collective-permute-start(bf16[2,264,128]{2,1,0:T(8,128)(2,1)S(1)} %pad_maximum_fusion), channel_id=1, source_target_pairs={{0,2},{2,0},{1,3},{3,1},{4,6},{6,4},{5,7},{7,5},{8,10},{10,8},{9,1... | collective-permute-start | bytes 405512 | tf_op jit(solution)/shard_map/ppermute | solution.py:282
  17.0 0.0 collective-permute-done.6.refs_4_
  17.0 0.5 %collective-permute-done.7.refs_5_ = bf16[1,264,128]{2,1,0:T(8,128)(2,1)S(1)} collective-permute-done((bf16[1,264,128]{2,1,0:T(8,128)(2,1)S(1)}, bf16[1,264,128]{2,1,0:T(8,128)(2,1)S(1)}, u32[]{:S(2)}, u32[]{:S(2)}) %collective-permute-start.7) | collective-permute-done | bytes 67616 | tf_op jit(solution)/shard_map/ppermute | solution.py:282
  17.5 0.4 combine_first_early.1
  17.9 2.8 %collective-permute-done.4.refs_0_ = bf16[2,264,128]{2,1,0:T(8,128)(2,1)S(1)} collective-permute-done((bf16[2,264,128]{2,1,0:T(8,128)(2,1)S(1)}, bf16[2,264,128]{2,1,0:T(8,128)(2,1)S(1)}, u32[]{:S(2)}, u32[]{:S(2)}) %collective-permute-start.4) | collective-permute-done | bytes 135200 | tf_op jit(solution)/shard_map/ppermute | solution.py:282
  20.7 0.4 %combine_first.1 = (bf16[4,128,256]{2,1,0:T(8,128)(2,1)S(1)}, f32[4,128,256]{2,1,0:T(8,128)S(1)}, bf16[256,256]{1,0:T(8,128)(2,1)S(1)}, bf16[272,256]{1,0:T(8,128)(2,1)S(1)}) custom-call(bf16[2,264,128]{2,1,0:T(8,128)(2,1)S(1)} %collective-permute-done.4.refs_0_, s32[8,128]{1,0:T(8,128)S(1)} %get-tuple-element.28.refs_4_.refs_1_, ...), custom_call_target="tpu_custom_call" | custom-call | tf_op jit(solution)/shard_map/combine_first/pallas_call | solution.py:418
  21.1 0.1 collective-permute-start.9
  21.2 0.5 %collective-permute-start.8 = (bf16[256,256]{1,0:T(8,128)(2,1)S(1)}, bf16[256,256]{1,0:T(8,128)(2,1)S(1)}, u32[]{:S(2)}, u32[]{:S(2)}) collective-permute-start(bf16[256,256]{1,0:T(8,128)(2,1)S(1)} %get-tuple-element.38.refs_4_.refs_7_), channel_id=1, source_target_pairs={{1,0},{0,1},{3,2},{2,3},{5,4},{4,5},{7,6},{6,7},{9,8},{8,9},{11,10... | collective-permute-start | bytes 393224 | tf_op jit(solution)/shard_map/ppermute | solution.py:449
  21.7 1.0 %collective-permute-done.8.refs_6_ = bf16[256,256]{1,0:T(8,128)(2,1)S(1)} collective-permute-done((bf16[256,256]{1,0:T(8,128)(2,1)S(1)}, bf16[256,256]{1,0:T(8,128)(2,1)S(1)}, u32[]{:S(2)}, u32[]{:S(2)}) %collective-permute-start.8) | collective-permute-done | bytes 131104 | tf_op jit(solution)/shard_map/ppermute | solution.py:449
  22.7 0.0 collective-permute-done.9.refs_7_
  22.7 1.6 %products_second.1 = (bf16[264,128]{1,0:T(8,128)(2,1)S(1)}, bf16[264,128]{1,0:T(8,128)(2,1)S(1)}, bf16[264,128]{1,0:T(8,128)(2,1)S(1)}, bf16[264,128]{1,0:T(8,128)(2,1)S(1)}, bf16[4,128,256]{2,1,0:T(8,128)(2,1)}) custom-call(s32[4,128]{1,0:T(4,128)S(1)} %get-tuple-element.25.refs_0_, bf16[8,4,128,256]{3,2,1,0:T(8,128)(2,1)S(1)} %get-tuple-element.26.refs_1_, ...), custom_call_target="tpu_custom_call" | custom-call | flops 1073741824 | bytes 3145728 | tf_op jit(solution)/shard_map/products_second/pallas_call | solution.py:256
  24.3 1.1 %collective-permute-start.12 = (bf16[264,128]{1,0:T(8,128)(2,1)S(1)}, bf16[264,128]{1,0:T(8,128)(2,1)S(1)}, u32[]{:S(2)}, u32[]{:S(2)}) collective-permute-start(bf16[264,128]{1,0:T(8,128)(2,1)S(1)} %get-tuple-element.43), channel_id=1, source_target_pairs={{0,8},{4,12},{8,0},{12,4},{1,9},{5,13},{9,1},{13,5},{2,10},{6,14},... | collective-permute-start | bytes 202760 | tf_op jit(solution)/shard_map/ppermute | solution.py:290
  25.3 2.3 %collective-permute-start.13 = (bf16[264,128]{1,0:T(8,128)(2,1)S(1)}, bf16[264,128]{1,0:T(8,128)(2,1)S(1)}, u32[]{:S(2)}, u32[]{:S(2)}) collective-permute-start(bf16[264,128]{1,0:T(8,128)(2,1)S(1)} %get-tuple-element.44), channel_id=1, source_target_pairs={{0,4},{4,0},{8,12},{12,8},{1,5},{5,1},{9,13},{13,9},{2,6},{6,2},{1... | collective-permute-start | bytes 202760 | tf_op jit(solution)/shard_map/ppermute | solution.py:290
  27.6 1.1 %collective-permute-start.10 = (bf16[264,128]{1,0:T(8,128)(2,1)S(1)}, bf16[264,128]{1,0:T(8,128)(2,1)S(1)}, u32[]{:S(2)}, u32[]{:S(2)}) collective-permute-start(bf16[264,128]{1,0:T(8,128)(2,1)S(1)} %get-tuple-element.41), channel_id=1, source_target_pairs={{0,12},{4,8},{8,4},{12,0},{1,13},{5,9},{9,5},{13,1},{2,14},{6,10},... | collective-permute-start | bytes 202760 | tf_op jit(solution)/shard_map/ppermute | solution.py:290
  28.7 1.5 %collective-permute-start.14 = (bf16[1,264,128]{2,1,0:T(8,128)(2,1)S(1)}, bf16[1,264,128]{2,1,0:T(8,128)(2,1)S(1)}, u32[]{:S(2)}, u32[]{:S(2)}) collective-permute-start(bf16[1,264,128]{2,1,0:T(8,128)(2,1)S(1)} %bitcast.11), channel_id=1, source_target_pairs={{0,2},{2,0},{1,3},{3,1},{4,6},{6,4},{5,7},{7,5},{8,10},{10,8},{9,1... | collective-permute-start | bytes 202760 | tf_op jit(solution)/shard_map/ppermute | solution.py:282
  30.2 0.0 collective-permute-done.12.refs_1_
  30.2 0.9 %collective-permute-start.15 = (bf16[1,264,128]{2,1,0:T(8,128)(2,1)S(1)}, bf16[1,264,128]{2,1,0:T(8,128)(2,1)S(1)}, u32[]{:S(2)}, u32[]{:S(2)}) collective-permute-start(bf16[1,264,128]{2,1,0:T(8,128)(2,1)S(1)} %bitcast.12), channel_id=1, source_target_pairs={{0,2},{2,0},{1,3},{3,1},{4,6},{6,4},{5,7},{7,5},{8,10},{10,8},{9,1... | collective-permute-start | bytes 202760 | tf_op jit(solution)/shard_map/ppermute | solution.py:282
  31.2 0.0 collective-permute-done.13.refs_2_
  31.2 1.3 %collective-permute-start.16 = (bf16[1,264,128]{2,1,0:T(8,128)(2,1)S(1)}, bf16[1,264,128]{2,1,0:T(8,128)(2,1)S(1)}, u32[]{:S(2)}, u32[]{:S(2)}) collective-permute-start(bf16[1,264,128]{2,1,0:T(8,128)(2,1)S(1)} %bitcast.13), channel_id=1, source_target_pairs={{0,2},{2,0},{1,3},{3,1},{4,6},{6,4},{5,7},{7,5},{8,10},{10,8},{9,1... | collective-permute-start | bytes 202760 | tf_op jit(solution)/shard_map/ppermute | solution.py:282
  32.5 1.4 %collective-permute-done.10.refs_3_ = bf16[264,128]{1,0:T(8,128)(2,1)S(1)} collective-permute-done((bf16[264,128]{1,0:T(8,128)(2,1)S(1)}, bf16[264,128]{1,0:T(8,128)(2,1)S(1)}, u32[]{:S(2)}, u32[]{:S(2)}) %collective-permute-start.10) | collective-permute-done | bytes 67616 | tf_op jit(solution)/shard_map/ppermute | solution.py:290
  33.9 1.5 %collective-permute-start.11 = (bf16[1,264,128]{2,1,0:T(8,128)(2,1)S(1)}, bf16[1,264,128]{2,1,0:T(8,128)(2,1)S(1)}, u32[]{:S(2)}, u32[]{:S(2)}) collective-permute-start(bf16[1,264,128]{2,1,0:T(8,128)(2,1)S(1)} %bitcast.14), channel_id=1, source_target_pairs={{0,2},{2,0},{1,3},{3,1},{4,6},{6,4},{5,7},{7,5},{8,10},{10,8},{9,1... | collective-permute-start | bytes 202760 | tf_op jit(solution)/shard_map/ppermute | solution.py:282
  35.4 0.0 collective-permute-done.14.refs_4_
  35.4 0.0 collective-permute-done.15.refs_5_
  35.4 0.5 %collective-permute-done.16.refs_6_ = bf16[1,264,128]{2,1,0:T(8,128)(2,1)S(1)} collective-permute-done((bf16[1,264,128]{2,1,0:T(8,128)(2,1)S(1)}, bf16[1,264,128]{2,1,0:T(8,128)(2,1)S(1)}, u32[]{:S(2)}, u32[]{:S(2)}) %collective-permute-start.16) | collective-permute-done | bytes 67616 | tf_op jit(solution)/shard_map/ppermute | solution.py:282
  35.9 0.5 %combine_second_early.1 = (f32[4,128,256]{2,1,0:T(8,128)S(1)}, f32[8,128]{1,0:T(8,128)S(1)}) custom-call(bf16[264,128]{1,0:T(8,128)(2,1)S(1)} %get-tuple-element.42.refs_0_, bf16[264,128]{1,0:T(8,128)(2,1)S(1)} %collective-permute-done.12.refs_1_, bf16[264,128]{1,0:T(8,128)(2,1)S(1)} %collective-permute-done.13.refs_2_, ...), custom_call_target="tpu_custom_call" | custom-call | flops 1000000000 | tf_op jit(solution)/shard_map/combine_second_early/pallas_call | solution.py:418
  36.4 1.8 %collective-permute-done.11.refs_0_ = bf16[1,264,128]{2,1,0:T(8,128)(2,1)S(1)} collective-permute-done((bf16[1,264,128]{2,1,0:T(8,128)(2,1)S(1)}, bf16[1,264,128]{2,1,0:T(8,128)(2,1)S(1)}, u32[]{:S(2)}, u32[]{:S(2)}) %collective-permute-start.11) | collective-permute-done | bytes 67616 | tf_op jit(solution)/shard_map/ppermute | solution.py:282
  38.2 0.8 %combine_second.1 = bf16[4,128,256]{2,1,0:T(8,128)(2,1)} custom-call(bf16[1,264,128]{2,1,0:T(8,128)(2,1)S(1)} %collective-permute-done.11.refs_0_, s32[8,128]{1,0:T(8,128)S(1)} %get-tuple-element.28.refs_4_.refs_1_, f32[4,128,256]{2,1,0:T(8,128)S(1)} %get-tuple-element.46.refs_2_, f32[8,128]{1,0:T(8,128)S(1)} %get-tuple-element.47.refs_3_), custom_call_target="tpu_custom_call" | custom-call | tf_op jit(solution)/shard_map/combine_second/pallas_call | solution.py:418
  (1 shorter events, 0.0 us)
Async XLA Ops:
  0.6 2.5 %copy-start = (bf16[8,256,256]{2,1,0:T(8,128)(2,1)S(1)}, bf16[8,256,256]{2,1,0:T(8,128)(2,1)}, u32[]{:S(2)}) copy-start(bf16[8,256,256]{2,1,0:T(8,128)(2,1)} %refs_2_.3) | copy-start | bytes 3145732
  0.6 2.5 %collective-permute-start = (bf16[4,128,256]{2,1,0:T(8,128)(2,1)}, bf16[4,128,256]{2,1,0:T(8,128)(2,1)S(1)}, u32[]{:S(2)}, u32[]{:S(2)}) collective-permute-start(bf16[4,128,256]{2,1,0:T(8,128)(2,1)} %psi_hbm.1), channel_id=1, source_target_pairs={{1,0},{0,1},{3,2},{2,3},{5,4},{4,5},{7,6},{6,7},{9,8},{8,9},{11,10... | collective-permute-start | bytes 786440 | tf_op jit(solution)/shard_map/ppermute | solution.py:449
  1.2 1.9 %collective-permute-start.1 = (f32[4,128]{1,0:T(4,128)}, f32[4,128]{1,0:T(4,128)S(1)}, u32[]{:S(2)}, u32[]{:S(2)}) collective-permute-start(f32[4,128]{1,0:T(4,128)} %energy_hbm.1), channel_id=1, source_target_pairs={{1,0},{0,1},{3,2},{2,3},{5,4},{4,5},{7,6},{6,7},{9,8},{8,9},{11,10... | collective-permute-start | bytes 6152 | tf_op jit(solution)/shard_map/ppermute | solution.py:449
  4.7 8.5 %collective-permute-start.5 = (bf16[264,128]{1,0:T(8,128)(2,1)S(1)}, bf16[264,128]{1,0:T(8,128)(2,1)S(1)}, u32[]{:S(2)}, u32[]{:S(2)}) collective-permute-start(bf16[264,128]{1,0:T(8,128)(2,1)S(1)} %get-tuple-element.33), channel_id=1, source_target_pairs={{0,4},{4,8},{8,12},{12,0},{1,5},{5,9},{9,13},{13,1},{2,6},{6,10},{... | collective-permute-start | bytes 202760 | tf_op jit(solution)/shard_map/ppermute | solution.py:290
  7.8 7.4 %collective-permute-start.2 = (bf16[264,128]{1,0:T(8,128)(2,1)S(1)}, bf16[264,128]{1,0:T(8,128)(2,1)S(1)}, u32[]{:S(2)}, u32[]{:S(2)}) collective-permute-start(bf16[264,128]{1,0:T(8,128)(2,1)S(1)} %get-tuple-element.30), channel_id=1, source_target_pairs={{0,8},{4,12},{8,0},{12,4},{1,9},{5,13},{9,1},{13,5},{2,10},{6,14},... | collective-permute-start | bytes 202760 | tf_op jit(solution)/shard_map/ppermute | solution.py:290
  10.4 5.0 %collective-permute-start.3 = (bf16[264,128]{1,0:T(8,128)(2,1)S(1)}, bf16[264,128]{1,0:T(8,128)(2,1)S(1)}, u32[]{:S(2)}, u32[]{:S(2)}) collective-permute-start(bf16[264,128]{1,0:T(8,128)(2,1)S(1)} %get-tuple-element.31), channel_id=1, source_target_pairs={{0,12},{4,0},{8,4},{12,8},{1,13},{5,1},{9,5},{13,9},{2,14},{6,2},{... | collective-permute-start | bytes 202760 | tf_op jit(solution)/shard_map/ppermute | solution.py:290
  11.7 5.3 %collective-permute-start.6 = (bf16[1,264,128]{2,1,0:T(8,128)(2,1)S(1)}, bf16[1,264,128]{2,1,0:T(8,128)(2,1)S(1)}, u32[]{:S(2)}, u32[]{:S(2)}) collective-permute-start(bf16[1,264,128]{2,1,0:T(8,128)(2,1)S(1)} %bitcast.15), channel_id=1, source_target_pairs={{0,2},{2,0},{1,3},{3,1},{4,6},{6,4},{5,7},{7,5},{8,10},{10,8},{9,1... | collective-permute-start | bytes 202760 | tf_op jit(solution)/shard_map/ppermute | solution.py:282
  13.2 4.3 %collective-permute-start.7 = (bf16[1,264,128]{2,1,0:T(8,128)(2,1)S(1)}, bf16[1,264,128]{2,1,0:T(8,128)(2,1)S(1)}, u32[]{:S(2)}, u32[]{:S(2)}) collective-permute-start(bf16[1,264,128]{2,1,0:T(8,128)(2,1)S(1)} %bitcast.16), channel_id=1, source_target_pairs={{0,2},{2,0},{1,3},{3,1},{4,6},{6,4},{5,7},{7,5},{8,10},{10,8},{9,1... | collective-permute-start | bytes 202760 | tf_op jit(solution)/shard_map/ppermute | solution.py:282
  15.4 5.2 %collective-permute-start.4 = (bf16[2,264,128]{2,1,0:T(8,128)(2,1)S(1)}, bf16[2,264,128]{2,1,0:T(8,128)(2,1)S(1)}, u32[]{:S(2)}, u32[]{:S(2)}) collective-permute-start(bf16[2,264,128]{2,1,0:T(8,128)(2,1)S(1)} %pad_maximum_fusion), channel_id=1, source_target_pairs={{0,2},{2,0},{1,3},{3,1},{4,6},{6,4},{5,7},{7,5},{8,10},{10,8},{9,1... | collective-permute-start | bytes 405512 | tf_op jit(solution)/shard_map/ppermute | solution.py:282
  21.1 1.6 %collective-permute-start.9 = (bf16[272,256]{1,0:T(8,128)(2,1)S(1)}, bf16[272,256]{1,0:T(8,128)(2,1)S(1)}, u32[]{:S(2)}, u32[]{:S(2)}) collective-permute-start(bf16[272,256]{1,0:T(8,128)(2,1)S(1)} %get-tuple-element.39.refs_5_.refs_8_), channel_id=1, source_target_pairs={{1,0},{0,1},{3,2},{2,3},{5,4},{4,5},{7,6},{6,7},{9,8},{8,9},{11,10... | collective-permute-start | bytes 417800 | tf_op jit(solution)/shard_map/ppermute | solution.py:449
  21.2 1.5 %collective-permute-start.8 = (bf16[256,256]{1,0:T(8,128)(2,1)S(1)}, bf16[256,256]{1,0:T(8,128)(2,1)S(1)}, u32[]{:S(2)}, u32[]{:S(2)}) collective-permute-start(bf16[256,256]{1,0:T(8,128)(2,1)S(1)} %get-tuple-element.38.refs_4_.refs_7_), channel_id=1, source_target_pairs={{1,0},{0,1},{3,2},{2,3},{5,4},{4,5},{7,6},{6,7},{9,8},{8,9},{11,10... | collective-permute-start | bytes 393224 | tf_op jit(solution)/shard_map/ppermute | solution.py:449
  24.3 6.0 %collective-permute-start.12 = (bf16[264,128]{1,0:T(8,128)(2,1)S(1)}, bf16[264,128]{1,0:T(8,128)(2,1)S(1)}, u32[]{:S(2)}, u32[]{:S(2)}) collective-permute-start(bf16[264,128]{1,0:T(8,128)(2,1)S(1)} %get-tuple-element.43), channel_id=1, source_target_pairs={{0,8},{4,12},{8,0},{12,4},{1,9},{5,13},{9,1},{13,5},{2,10},{6,14},... | collective-permute-start | bytes 202760 | tf_op jit(solution)/shard_map/ppermute | solution.py:290
  25.3 5.9 %collective-permute-start.13 = (bf16[264,128]{1,0:T(8,128)(2,1)S(1)}, bf16[264,128]{1,0:T(8,128)(2,1)S(1)}, u32[]{:S(2)}, u32[]{:S(2)}) collective-permute-start(bf16[264,128]{1,0:T(8,128)(2,1)S(1)} %get-tuple-element.44), channel_id=1, source_target_pairs={{0,4},{4,0},{8,12},{12,8},{1,5},{5,1},{9,13},{13,9},{2,6},{6,2},{1... | collective-permute-start | bytes 202760 | tf_op jit(solution)/shard_map/ppermute | solution.py:290
  27.6 6.3 %collective-permute-start.10 = (bf16[264,128]{1,0:T(8,128)(2,1)S(1)}, bf16[264,128]{1,0:T(8,128)(2,1)S(1)}, u32[]{:S(2)}, u32[]{:S(2)}) collective-permute-start(bf16[264,128]{1,0:T(8,128)(2,1)S(1)} %get-tuple-element.41), channel_id=1, source_target_pairs={{0,12},{4,8},{8,4},{12,0},{1,13},{5,9},{9,5},{13,1},{2,14},{6,10},... | collective-permute-start | bytes 202760 | tf_op jit(solution)/shard_map/ppermute | solution.py:290
  28.7 6.7 %collective-permute-start.14 = (bf16[1,264,128]{2,1,0:T(8,128)(2,1)S(1)}, bf16[1,264,128]{2,1,0:T(8,128)(2,1)S(1)}, u32[]{:S(2)}, u32[]{:S(2)}) collective-permute-start(bf16[1,264,128]{2,1,0:T(8,128)(2,1)S(1)} %bitcast.11), channel_id=1, source_target_pairs={{0,2},{2,0},{1,3},{3,1},{4,6},{6,4},{5,7},{7,5},{8,10},{10,8},{9,1... | collective-permute-start | bytes 202760 | tf_op jit(solution)/shard_map/ppermute | solution.py:282
  30.2 5.2 %collective-permute-start.15 = (bf16[1,264,128]{2,1,0:T(8,128)(2,1)S(1)}, bf16[1,264,128]{2,1,0:T(8,128)(2,1)S(1)}, u32[]{:S(2)}, u32[]{:S(2)}) collective-permute-start(bf16[1,264,128]{2,1,0:T(8,128)(2,1)S(1)} %bitcast.12), channel_id=1, source_target_pairs={{0,2},{2,0},{1,3},{3,1},{4,6},{6,4},{5,7},{7,5},{8,10},{10,8},{9,1... | collective-permute-start | bytes 202760 | tf_op jit(solution)/shard_map/ppermute | solution.py:282
  31.2 4.7 %collective-permute-start.16 = (bf16[1,264,128]{2,1,0:T(8,128)(2,1)S(1)}, bf16[1,264,128]{2,1,0:T(8,128)(2,1)S(1)}, u32[]{:S(2)}, u32[]{:S(2)}) collective-permute-start(bf16[1,264,128]{2,1,0:T(8,128)(2,1)S(1)} %bitcast.13), channel_id=1, source_target_pairs={{0,2},{2,0},{1,3},{3,1},{4,6},{6,4},{5,7},{7,5},{8,10},{10,8},{9,1... | collective-permute-start | bytes 202760 | tf_op jit(solution)/shard_map/ppermute | solution.py:282
  33.9 4.3 %collective-permute-start.11 = (bf16[1,264,128]{2,1,0:T(8,128)(2,1)S(1)}, bf16[1,264,128]{2,1,0:T(8,128)(2,1)S(1)}, u32[]{:S(2)}, u32[]{:S(2)}) collective-permute-start(bf16[1,264,128]{2,1,0:T(8,128)(2,1)S(1)} %bitcast.14), channel_id=1, source_target_pairs={{0,2},{2,0},{1,3},{3,1},{4,6},{6,4},{5,7},{7,5},{8,10},{10,8},{9,1... | collective-permute-start | bytes 202760 | tf_op jit(solution)/shard_map/ppermute | solution.py:282

commit v5 on v3

--- a/solution.py
+++ b/solution.py
@@ -217,11 +217,13 @@
             owner = sec ^ d
         else:
             owner = remainder(sec + d, sec_count)
-        packet = jnp.zeros((half, width), F32)
-        for i in range(cap):
-            pair = entry_ref[owner, i]
-            term = jnp.minimum(quotient(pair, sec_dev), terms - 1)
-            packet += jnp.dot(inner_ref[pair], right_ref[term], preferred_element_type=F32)
+        listed = [entry_ref[owner, i] for i in range(cap)]
+        picked = [jnp.minimum(quotient(pair, sec_dev), terms - 1) for pair in listed]
+        packet = jnp.dot(
+            jnp.concatenate([inner_ref[pair] for pair in listed], axis=1),
+            jnp.concatenate([right_ref[term] for term in picked], axis=0),
+            preferred_element_type=F32,
+        )
         out = out_refs[d] if split else out_refs[0].at[d]
         for column in range(width // LANES):
             out[column * half:(column + 1) * half, :] = packet[
@@ -425,7 +427,7 @@
     steps = list(range(1, sec_count))
     first_plan = (False, steps, [[0]] + [[k] for k in steps[:-2]] + [steps[-2:]])
     second_groups = [[0]] + [[k] for k in steps[1:2] + steps[:1] + steps[2:]]
-    second_plan = (can_pair, steps[1:] + steps[:1], [[0], steps[1:2], steps[2:] + steps[:1]])
+    second_plan = (can_pair, steps[1:2] + steps[:1] + steps[2:], second_groups)
     params = pltpu.CompilerParams(vmem_limit_bytes=VMEM_BYTES)
     vec_shape = (sec_dev, half, width)
     vec_bf16 = jax.ShapeDtypeStruct(vec_shape, BF16)

time: 39.7 us -> 39.1 us (0.985)
  waiting for transfers between devices: 11.2 us -> 10 us
  starting transfers between devices: 20.5 us -> 21 us
    ppermute x6 -> x7, waiting for transfers between devices: 6.52 us -> 5.6 us  [exchange(): lax.ppermute(packet, 'op', turn)]
    ppermute x6 -> x7, starting transfers between devices: 8.38 us -> 8.93 us  [exchange(): lax.ppermute(packet, 'op', turn)]
  transfers between devices with their start and end apart: 15 -> 16, of which waited for: 9 -> 9; matrix products, arithmetic and copies ran while one was open for 0% -> 0% of each run, Pallas kernels for 7% -> 7%
where the time goes in v5:
time: 39.1 us; the launch traced here: 38.9 us
  starting transfers between devices  21 us (54%)
  waiting for transfers between devices  10 us (26%)
  Pallas kernels  7.12 us (18%)
  between operations  0.72 us (2%)
    ppermute x6, starting transfers between devices, exchange(): arrived[step] = lax.ppermute(packets[step], 'sec', turn)  11.4 us
    ppermute x7, starting transfers between devices, exchange(): lax.ppermute(packet, 'op', turn)  8.93 us
    ppermute x7, waiting for transfers between devices, exchange(): lax.ppermute(packet, 'op', turn)  5.6 us
    pallas_call x2, Pallas kernels, sigma_packets(): pl.pallas_call(functools.partial(product_kernel, is_first, split, paired,...  3.16 us
    ppermute x6, waiting for transfers between devices, exchange(): arrived[step] = lax.ppermute(packets[step], 'sec', turn)  2.9 us
    pallas_call x4, Pallas kernels, call(): pl.pallas_call(kernel, out_shape=outs, in_specs=[whole(pltpu.VMEM)] * len...  2.12 us
    pallas_call x1, Pallas kernels, body(): pl.pallas_call(load_kernel, out_shape=[vec_bf16, jax.ShapeDtypeStruct(lef...  1.84 us
    ppermute x3, waiting for transfers between devices, from_others(): arrays.append(lax.ppermute(array, 'rep', turn))  1.54 us
  transfers between devices with their start and end apart: 16, of which 9 were waited for; matrix products, arithmetic and copies ran while one was open for 0% of the time, Pallas kernels for 7%

profile of v5, /device:TPU:0, one launch (start us, length us, event | category | flops | bytes accessed | tf_op | source)
XLA Modules:
  0.0 38.9 jit_solution(2956454471540624053)
XLA Ops:
  0.6 0.0 copy-start
  0.6 0.5 %collective-permute-start = (bf16[4,128,256]{2,1,0:T(8,128)(2,1)}, bf16[4,128,256]{2,1,0:T(8,128)(2,1)S(1)}, u32[]{:S(2)}, u32[]{:S(2)}) collective-permute-start(bf16[4,128,256]{2,1,0:T(8,128)(2,1)} %psi_hbm.1), channel_id=1, source_target_pairs={{1,0},{0,1},{3,2},{2,3},{5,4},{4,5},{7,6},{6,7},{9,8},{8,9},{11,10... | collective-permute-start | bytes 786440 | tf_op jit(solution)/shard_map/ppermute | solution.py:439
  1.2 0.1 collective-permute-start.1
  1.2 1.8 %load.1 = (bf16[4,128,256]{2,1,0:T(8,128)(2,1)S(1)}, bf16[8,4,128,256]{3,2,1,0:T(8,128)(2,1)S(1)}, s32[4,128]{1,0:T(4,128)S(1)}, s32[8,128]{1,0:T(8,128)S(1)}, f...) custom-call(bf16[4,128,256]{2,1,0:T(8,128)(2,1)} %psi_hbm.1, bf16[8,4,128,256]{3,2,1,0:T(8,128)(2,1)} %left_hbm.1, ...), custom_call_target="tpu_custom_call" | custom-call | tf_op jit(solution)/shard_map/load/pallas_call | solution.py:444
  3.1 0.0 collective-permute-done.1.refs_7_
  3.1 0.0 collective-permute-done.refs_6_
  3.1 0.0 copy-done
  3.1 1.6 %products_first.1 = (bf16[264,128]{1,0:T(8,128)(2,1)S(1)}, bf16[264,128]{1,0:T(8,128)(2,1)S(1)}, bf16[264,128]{1,0:T(8,128)(2,1)S(1)}, bf16[264,128]{1,0:T(8,128)(2,1)S(1)}) custom-call(s32[4,128]{1,0:T(4,128)S(1)} %get-tuple-element.24.refs_0_, bf16[8,4,128,256]{3,2,1,0:T(8,128)(2,1)S(1)} %get-tuple-element.25.refs_1_, bf16[8,256,256]{2,1,0:T(8,128)(2,1)S(1)} %copy-done, ...), custom_call_target="tpu_custom_call" | custom-call | flops 1073741824 | bytes 3145728 | tf_op jit(solution)/shard_map/products_first/pallas_call | solution.py:251
  4.7 3.1 %collective-permute-start.5 = (bf16[264,128]{1,0:T(8,128)(2,1)S(1)}, bf16[264,128]{1,0:T(8,128)(2,1)S(1)}, u32[]{:S(2)}, u32[]{:S(2)}) collective-permute-start(bf16[264,128]{1,0:T(8,128)(2,1)S(1)} %get-tuple-element.32), channel_id=1, source_target_pairs={{0,4},{4,8},{8,12},{12,0},{1,5},{5,9},{9,13},{13,1},{2,6},{6,10},{... | collective-permute-start | bytes 202760 | tf_op jit(solution)/shard_map/ppermute | solution.py:285
  7.8 2.6 %collective-permute-start.2 = (bf16[264,128]{1,0:T(8,128)(2,1)S(1)}, bf16[264,128]{1,0:T(8,128)(2,1)S(1)}, u32[]{:S(2)}, u32[]{:S(2)}) collective-permute-start(bf16[264,128]{1,0:T(8,128)(2,1)S(1)} %get-tuple-element.29), channel_id=1, source_target_pairs={{0,8},{4,12},{8,0},{12,4},{1,9},{5,13},{9,1},{13,5},{2,10},{6,14},... | collective-permute-start | bytes 202760 | tf_op jit(solution)/shard_map/ppermute | solution.py:285
  10.4 1.3 %collective-permute-start.3 = (bf16[264,128]{1,0:T(8,128)(2,1)S(1)}, bf16[264,128]{1,0:T(8,128)(2,1)S(1)}, u32[]{:S(2)}, u32[]{:S(2)}) collective-permute-start(bf16[264,128]{1,0:T(8,128)(2,1)S(1)} %get-tuple-element.30), channel_id=1, source_target_pairs={{0,12},{4,0},{8,4},{12,8},{1,13},{5,1},{9,5},{13,9},{2,14},{6,2},{... | collective-permute-start | bytes 202760 | tf_op jit(solution)/shard_map/ppermute | solution.py:285
  11.7 1.5 %collective-permute-start.6 = (bf16[1,264,128]{2,1,0:T(8,128)(2,1)S(1)}, bf16[1,264,128]{2,1,0:T(8,128)(2,1)S(1)}, u32[]{:S(2)}, u32[]{:S(2)}) collective-permute-start(bf16[1,264,128]{2,1,0:T(8,128)(2,1)S(1)} %bitcast.13), channel_id=1, source_target_pairs={{0,2},{2,0},{1,3},{3,1},{4,6},{6,4},{5,7},{7,5},{8,10},{10,8},{9,1... | collective-permute-start | bytes 202760 | tf_op jit(solution)/shard_map/ppermute | solution.py:277
  13.2 0.0 collective-permute-done.5.refs_1_
  13.2 0.8 %collective-permute-start.7 = (bf16[1,264,128]{2,1,0:T(8,128)(2,1)S(1)}, bf16[1,264,128]{2,1,0:T(8,128)(2,1)S(1)}, u32[]{:S(2)}, u32[]{:S(2)}) collective-permute-start(bf16[1,264,128]{2,1,0:T(8,128)(2,1)S(1)} %bitcast.16), channel_id=1, source_target_pairs={{0,2},{2,0},{1,3},{3,1},{4,6},{6,4},{5,7},{7,5},{8,10},{10,8},{9,1... | collective-permute-start | bytes 202760 | tf_op jit(solution)/shard_map/ppermute | solution.py:277
  14.1 1.1 %collective-permute-done.2.refs_2_ = bf16[264,128]{1,0:T(8,128)(2,1)S(1)} collective-permute-done((bf16[264,128]{1,0:T(8,128)(2,1)S(1)}, bf16[264,128]{1,0:T(8,128)(2,1)S(1)}, u32[]{:S(2)}, u32[]{:S(2)}) %collective-permute-start.2) | collective-permute-done | bytes 67616 | tf_op jit(solution)/shard_map/ppermute | solution.py:285
  15.2 0.2 collective-permute-done.3.refs_3_
  15.4 1.6 %collective-permute-start.4 = (bf16[2,264,128]{2,1,0:T(8,128)(2,1)S(1)}, bf16[2,264,128]{2,1,0:T(8,128)(2,1)S(1)}, u32[]{:S(2)}, u32[]{:S(2)}) collective-permute-start(bf16[2,264,128]{2,1,0:T(8,128)(2,1)S(1)} %pad_maximum_fusion), channel_id=1, source_target_pairs={{0,2},{2,0},{1,3},{3,1},{4,6},{6,4},{5,7},{7,5},{8,10},{10,8},{9,1... | collective-permute-start | bytes 405512 | tf_op jit(solution)/shard_map/ppermute | solution.py:277
  17.0 0.0 collective-permute-done.6.refs_4_
  17.0 0.5 %collective-permute-done.7.refs_5_ = bf16[1,264,128]{2,1,0:T(8,128)(2,1)S(1)} collective-permute-done((bf16[1,264,128]{2,1,0:T(8,128)(2,1)S(1)}, bf16[1,264,128]{2,1,0:T(8,128)(2,1)S(1)}, u32[]{:S(2)}, u32[]{:S(2)}) %collective-permute-start.7) | collective-permute-done | bytes 67616 | tf_op jit(solution)/shard_map/ppermute | solution.py:277
  17.5 0.4 combine_first_early.1
  17.9 2.8 %collective-permute-done.4.refs_0_ = bf16[2,264,128]{2,1,0:T(8,128)(2,1)S(1)} collective-permute-done((bf16[2,264,128]{2,1,0:T(8,128)(2,1)S(1)}, bf16[2,264,128]{2,1,0:T(8,128)(2,1)S(1)}, u32[]{:S(2)}, u32[]{:S(2)}) %collective-permute-start.4) | collective-permute-done | bytes 135200 | tf_op jit(solution)/shard_map/ppermute | solution.py:277
  20.7 0.4 %combine_first.1 = (bf16[4,128,256]{2,1,0:T(8,128)(2,1)S(1)}, f32[4,128,256]{2,1,0:T(8,128)S(1)}, bf16[528,256]{1,0:T(8,128)(2,1)S(1)}) custom-call(bf16[2,264,128]{2,1,0:T(8,128)(2,1)S(1)} %collective-permute-done.4.refs_0_, s32[8,128]{1,0:T(8,128)S(1)} %get-tuple-element.27.refs_4_.refs_1_, ...), custom_call_target="tpu_custom_call" | custom-call | tf_op jit(solution)/shard_map/combine_first/pallas_call | solution.py:408
  21.1 0.1 collective-permute-start.8
  21.2 1.5 %collective-permute-done.8.refs_5_ = bf16[528,256]{1,0:T(8,128)(2,1)S(1)} collective-permute-done((bf16[528,256]{1,0:T(8,128)(2,1)S(1)}, bf16[528,256]{1,0:T(8,128)(2,1)S(1)}, u32[]{:S(2)}, u32[]{:S(2)}) %collective-permute-start.8) | collective-permute-done | bytes 270368 | tf_op jit(solution)/shard_map/ppermute | solution.py:439
  22.7 1.6 %products_second.1 = (bf16[264,128]{1,0:T(8,128)(2,1)S(1)}, bf16[264,128]{1,0:T(8,128)(2,1)S(1)}, bf16[264,128]{1,0:T(8,128)(2,1)S(1)}, bf16[264,128]{1,0:T(8,128)(2,1)S(1)}, bf16[4,128,256]{2,1,0:T(8,128)(2,1)}) custom-call(s32[4,128]{1,0:T(4,128)S(1)} %get-tuple-element.24.refs_0_, bf16[8,4,128,256]{3,2,1,0:T(8,128)(2,1)S(1)} %get-tuple-element.25.refs_1_, ...), custom_call_target="tpu_custom_call" | custom-call | flops 1073741824 | bytes 3145728 | tf_op jit(solution)/shard_map/products_second/pallas_call | solution.py:251
  24.3 1.1 %collective-permute-start.11 = (bf16[264,128]{1,0:T(8,128)(2,1)S(1)}, bf16[264,128]{1,0:T(8,128)(2,1)S(1)}, u32[]{:S(2)}, u32[]{:S(2)}) collective-permute-start(bf16[264,128]{1,0:T(8,128)(2,1)S(1)} %get-tuple-element.41), channel_id=1, source_target_pairs={{0,8},{4,12},{8,0},{12,4},{1,9},{5,13},{9,1},{13,5},{2,10},{6,14},... | collective-permute-start | bytes 202760 | tf_op jit(solution)/shard_map/ppermute | solution.py:285
  25.3 2.3 %collective-permute-start.12 = (bf16[264,128]{1,0:T(8,128)(2,1)S(1)}, bf16[264,128]{1,0:T(8,128)(2,1)S(1)}, u32[]{:S(2)}, u32[]{:S(2)}) collective-permute-start(bf16[264,128]{1,0:T(8,128)(2,1)S(1)} %get-tuple-element.42), channel_id=1, source_target_pairs={{0,4},{4,0},{8,12},{12,8},{1,5},{5,1},{9,13},{13,9},{2,6},{6,2},{1... | collective-permute-start | bytes 202760 | tf_op jit(solution)/shard_map/ppermute | solution.py:285
  27.6 1.1 %collective-permute-start.9 = (bf16[264,128]{1,0:T(8,128)(2,1)S(1)}, bf16[264,128]{1,0:T(8,128)(2,1)S(1)}, u32[]{:S(2)}, u32[]{:S(2)}) collective-permute-start(bf16[264,128]{1,0:T(8,128)(2,1)S(1)} %get-tuple-element.39), channel_id=1, source_target_pairs={{0,12},{4,8},{8,4},{12,0},{1,13},{5,9},{9,5},{13,1},{2,14},{6,10},... | collective-permute-start | bytes 202760 | tf_op jit(solution)/shard_map/ppermute | solution.py:285
  28.7 1.5 %collective-permute-start.13 = (bf16[1,264,128]{2,1,0:T(8,128)(2,1)S(1)}, bf16[1,264,128]{2,1,0:T(8,128)(2,1)S(1)}, u32[]{:S(2)}, u32[]{:S(2)}) collective-permute-start(bf16[1,264,128]{2,1,0:T(8,128)(2,1)S(1)} %bitcast.11), channel_id=1, source_target_pairs={{0,2},{2,0},{1,3},{3,1},{4,6},{6,4},{5,7},{7,5},{8,10},{10,8},{9,1... | collective-permute-start | bytes 202760 | tf_op jit(solution)/shard_map/ppermute | solution.py:277
  30.2 0.1 collective-permute-done.11.refs_1_
  30.3 1.5 %collective-permute-start.14 = (bf16[1,264,128]{2,1,0:T(8,128)(2,1)S(1)}, bf16[1,264,128]{2,1,0:T(8,128)(2,1)S(1)}, u32[]{:S(2)}, u32[]{:S(2)}) collective-permute-start(bf16[1,264,128]{2,1,0:T(8,128)(2,1)S(1)} %bitcast.12), channel_id=1, source_target_pairs={{0,2},{2,0},{1,3},{3,1},{4,6},{6,4},{5,7},{7,5},{8,10},{10,8},{9,1... | collective-permute-start | bytes 202760 | tf_op jit(solution)/shard_map/ppermute | solution.py:277
  31.8 0.0 collective-permute-done.12.refs_2_
  31.8 0.5 %collective-permute-start.15 = (bf16[1,264,128]{2,1,0:T(8,128)(2,1)S(1)}, bf16[1,264,128]{2,1,0:T(8,128)(2,1)S(1)}, u32[]{:S(2)}, u32[]{:S(2)}) collective-permute-start(bf16[1,264,128]{2,1,0:T(8,128)(2,1)S(1)} %bitcast.14), channel_id=1, source_target_pairs={{0,2},{2,0},{1,3},{3,1},{4,6},{6,4},{5,7},{7,5},{8,10},{10,8},{9,1... | collective-permute-start | bytes 202760 | tf_op jit(solution)/shard_map/ppermute | solution.py:277
  32.3 1.5 %collective-permute-done.9.refs_3_ = bf16[264,128]{1,0:T(8,128)(2,1)S(1)} collective-permute-done((bf16[264,128]{1,0:T(8,128)(2,1)S(1)}, bf16[264,128]{1,0:T(8,128)(2,1)S(1)}, u32[]{:S(2)}, u32[]{:S(2)}) %collective-permute-start.9) | collective-permute-done | bytes 67616 | tf_op jit(solution)/shard_map/ppermute | solution.py:285
  33.8 1.5 %collective-permute-start.10 = (bf16[1,264,128]{2,1,0:T(8,128)(2,1)S(1)}, bf16[1,264,128]{2,1,0:T(8,128)(2,1)S(1)}, u32[]{:S(2)}, u32[]{:S(2)}) collective-permute-start(bf16[1,264,128]{2,1,0:T(8,128)(2,1)S(1)} %bitcast.15), channel_id=1, source_target_pairs={{0,2},{2,0},{1,3},{3,1},{4,6},{6,4},{5,7},{7,5},{8,10},{10,8},{9,1... | collective-permute-start | bytes 202760 | tf_op jit(solution)/shard_map/ppermute | solution.py:277
  35.3 0.0 collective-permute-done.13.refs_4_
  35.3 0.0 collective-permute-done.14.refs_5_
  35.3 1.5 %collective-permute-done.15.refs_6_ = bf16[1,264,128]{2,1,0:T(8,128)(2,1)S(1)} collective-permute-done((bf16[1,264,128]{2,1,0:T(8,128)(2,1)S(1)}, bf16[1,264,128]{2,1,0:T(8,128)(2,1)S(1)}, u32[]{:S(2)}, u32[]{:S(2)}) %collective-permute-start.15) | collective-permute-done | bytes 67616 | tf_op jit(solution)/shard_map/ppermute | solution.py:277
  36.8 0.5 %combine_second_early.1 = (f32[4,128,256]{2,1,0:T(8,128)S(1)}, f32[8,128]{1,0:T(8,128)S(1)}) custom-call(bf16[264,128]{1,0:T(8,128)(2,1)S(1)} %get-tuple-element.40.refs_0_, bf16[264,128]{1,0:T(8,128)(2,1)S(1)} %collective-permute-done.11.refs_1_, bf16[264,128]{1,0:T(8,128)(2,1)S(1)} %collective-permute-done.12.refs_2_, ...), custom_call_target="tpu_custom_call" | custom-call | flops 1000000000 | tf_op jit(solution)/shard_map/combine_second_early/pallas_call | solution.py:408
  37.3 0.8 %collective-permute-done.10.refs_0_ = bf16[1,264,128]{2,1,0:T(8,128)(2,1)S(1)} collective-permute-done((bf16[1,264,128]{2,1,0:T(8,128)(2,1)S(1)}, bf16[1,264,128]{2,1,0:T(8,128)(2,1)S(1)}, u32[]{:S(2)}, u32[]{:S(2)}) %collective-permute-start.10) | collective-permute-done | bytes 67616 | tf_op jit(solution)/shard_map/ppermute | solution.py:277
  38.1 0.8 %combine_second.1 = bf16[4,128,256]{2,1,0:T(8,128)(2,1)} custom-call(bf16[1,264,128]{2,1,0:T(8,128)(2,1)S(1)} %collective-permute-done.10.refs_0_, s32[8,128]{1,0:T(8,128)S(1)} %get-tuple-element.27.refs_4_.refs_1_, f32[4,128,256]{2,1,0:T(8,128)S(1)} %get-tuple-element.44.refs_2_, f32[8,128]{1,0:T(8,128)S(1)} %get-tuple-element.45.refs_3_), custom_call_target="tpu_custom_call" | custom-call | tf_op jit(solution)/shard_map/combine_second/pallas_call | solution.py:408
  (1 shorter events, 0.0 us)
Async XLA Ops:
  0.6 2.5 %copy-start = (bf16[8,256,256]{2,1,0:T(8,128)(2,1)S(1)}, bf16[8,256,256]{2,1,0:T(8,128)(2,1)}, u32[]{:S(2)}) copy-start(bf16[8,256,256]{2,1,0:T(8,128)(2,1)} %refs_2_.3) | copy-start | bytes 3145732
  0.6 2.5 %collective-permute-start = (bf16[4,128,256]{2,1,0:T(8,128)(2,1)}, bf16[4,128,256]{2,1,0:T(8,128)(2,1)S(1)}, u32[]{:S(2)}, u32[]{:S(2)}) collective-permute-start(bf16[4,128,256]{2,1,0:T(8,128)(2,1)} %psi_hbm.1), channel_id=1, source_target_pairs={{1,0},{0,1},{3,2},{2,3},{5,4},{4,5},{7,6},{6,7},{9,8},{8,9},{11,10... | collective-permute-start | bytes 786440 | tf_op jit(solution)/shard_map/ppermute | solution.py:439
  1.2 1.9 %collective-permute-start.1 = (f32[4,128]{1,0:T(4,128)}, f32[4,128]{1,0:T(4,128)S(1)}, u32[]{:S(2)}, u32[]{:S(2)}) collective-permute-start(f32[4,128]{1,0:T(4,128)} %energy_hbm.1), channel_id=1, source_target_pairs={{1,0},{0,1},{3,2},{2,3},{5,4},{4,5},{7,6},{6,7},{9,8},{8,9},{11,10... | collective-permute-start | bytes 6152 | tf_op jit(solution)/shard_map/ppermute | solution.py:439
  4.7 8.5 %collective-permute-start.5 = (bf16[264,128]{1,0:T(8,128)(2,1)S(1)}, bf16[264,128]{1,0:T(8,128)(2,1)S(1)}, u32[]{:S(2)}, u32[]{:S(2)}) collective-permute-start(bf16[264,128]{1,0:T(8,128)(2,1)S(1)} %get-tuple-element.32), channel_id=1, source_target_pairs={{0,4},{4,8},{8,12},{12,0},{1,5},{5,9},{9,13},{13,1},{2,6},{6,10},{... | collective-permute-start | bytes 202760 | tf_op jit(solution)/shard_map/ppermute | solution.py:285
  7.8 7.4 %collective-permute-start.2 = (bf16[264,128]{1,0:T(8,128)(2,1)S(1)}, bf16[264,128]{1,0:T(8,128)(2,1)S(1)}, u32[]{:S(2)}, u32[]{:S(2)}) collective-permute-start(bf16[264,128]{1,0:T(8,128)(2,1)S(1)} %get-tuple-element.29), channel_id=1, source_target_pairs={{0,8},{4,12},{8,0},{12,4},{1,9},{5,13},{9,1},{13,5},{2,10},{6,14},... | collective-permute-start | bytes 202760 | tf_op jit(solution)/shard_map/ppermute | solution.py:285
  10.4 5.0 %collective-permute-start.3 = (bf16[264,128]{1,0:T(8,128)(2,1)S(1)}, bf16[264,128]{1,0:T(8,128)(2,1)S(1)}, u32[]{:S(2)}, u32[]{:S(2)}) collective-permute-start(bf16[264,128]{1,0:T(8,128)(2,1)S(1)} %get-tuple-element.30), channel_id=1, source_target_pairs={{0,12},{4,0},{8,4},{12,8},{1,13},{5,1},{9,5},{13,9},{2,14},{6,2},{... | collective-permute-start | bytes 202760 | tf_op jit(solution)/shard_map/ppermute | solution.py:285
  11.7 5.3 %collective-permute-start.6 = (bf16[1,264,128]{2,1,0:T(8,128)(2,1)S(1)}, bf16[1,264,128]{2,1,0:T(8,128)(2,1)S(1)}, u32[]{:S(2)}, u32[]{:S(2)}) collective-permute-start(bf16[1,264,128]{2,1,0:T(8,128)(2,1)S(1)} %bitcast.13), channel_id=1, source_target_pairs={{0,2},{2,0},{1,3},{3,1},{4,6},{6,4},{5,7},{7,5},{8,10},{10,8},{9,1... | collective-permute-start | bytes 202760 | tf_op jit(solution)/shard_map/ppermute | solution.py:277
  13.2 4.3 %collective-permute-start.7 = (bf16[1,264,128]{2,1,0:T(8,128)(2,1)S(1)}, bf16[1,264,128]{2,1,0:T(8,128)(2,1)S(1)}, u32[]{:S(2)}, u32[]{:S(2)}) collective-permute-start(bf16[1,264,128]{2,1,0:T(8,128)(2,1)S(1)} %bitcast.16), channel_id=1, source_target_pairs={{0,2},{2,0},{1,3},{3,1},{4,6},{6,4},{5,7},{7,5},{8,10},{10,8},{9,1... | collective-permute-start | bytes 202760 | tf_op jit(solution)/shard_map/ppermute | solution.py:277
  15.4 5.2 %collective-permute-start.4 = (bf16[2,264,128]{2,1,0:T(8,128)(2,1)S(1)}, bf16[2,264,128]{2,1,0:T(8,128)(2,1)S(1)}, u32[]{:S(2)}, u32[]{:S(2)}) collective-permute-start(bf16[2,264,128]{2,1,0:T(8,128)(2,1)S(1)} %pad_maximum_fusion), channel_id=1, source_target_pairs={{0,2},{2,0},{1,3},{3,1},{4,6},{6,4},{5,7},{7,5},{8,10},{10,8},{9,1... | collective-permute-start | bytes 405512 | tf_op jit(solution)/shard_map/ppermute | solution.py:277
  21.1 1.6 %collective-permute-start.8 = (bf16[528,256]{1,0:T(8,128)(2,1)S(1)}, bf16[528,256]{1,0:T(8,128)(2,1)S(1)}, u32[]{:S(2)}, u32[]{:S(2)}) collective-permute-start(bf16[528,256]{1,0:T(8,128)(2,1)S(1)} %get-tuple-element.37.refs_4_.refs_7_), channel_id=1, source_target_pairs={{1,0},{0,1},{3,2},{2,3},{5,4},{4,5},{7,6},{6,7},{9,8},{8,9},{11,10... | collective-permute-start | bytes 811016 | tf_op jit(solution)/shard_map/ppermute | solution.py:439
  24.3 6.0 %collective-permute-start.11 = (bf16[264,128]{1,0:T(8,128)(2,1)S(1)}, bf16[264,128]{1,0:T(8,128)(2,1)S(1)}, u32[]{:S(2)}, u32[]{:S(2)}) collective-permute-start(bf16[264,128]{1,0:T(8,128)(2,1)S(1)} %get-tuple-element.41), channel_id=1, source_target_pairs={{0,8},{4,12},{8,0},{12,4},{1,9},{5,13},{9,1},{13,5},{2,10},{6,14},... | collective-permute-start | bytes 202760 | tf_op jit(solution)/shard_map/ppermute | solution.py:285
  25.3 6.5 %collective-permute-start.12 = (bf16[264,128]{1,0:T(8,128)(2,1)S(1)}, bf16[264,128]{1,0:T(8,128)(2,1)S(1)}, u32[]{:S(2)}, u32[]{:S(2)}) collective-permute-start(bf16[264,128]{1,0:T(8,128)(2,1)S(1)} %get-tuple-element.42), channel_id=1, source_target_pairs={{0,4},{4,0},{8,12},{12,8},{1,5},{5,1},{9,13},{13,9},{2,6},{6,2},{1... | collective-permute-start | bytes 202760 | tf_op jit(solution)/shard_map/ppermute | solution.py:285
  27.6 6.2 %collective-permute-start.9 = (bf16[264,128]{1,0:T(8,128)(2,1)S(1)}, bf16[264,128]{1,0:T(8,128)(2,1)S(1)}, u32[]{:S(2)}, u32[]{:S(2)}) collective-permute-start(bf16[264,128]{1,0:T(8,128)(2,1)S(1)} %get-tuple-element.39), channel_id=1, source_target_pairs={{0,12},{4,8},{8,4},{12,0},{1,13},{5,9},{9,5},{13,1},{2,14},{6,10},... | collective-permute-start | bytes 202760 | tf_op jit(solution)/shard_map/ppermute | solution.py:285
  28.7 6.6 %collective-permute-start.13 = (bf16[1,264,128]{2,1,0:T(8,128)(2,1)S(1)}, bf16[1,264,128]{2,1,0:T(8,128)(2,1)S(1)}, u32[]{:S(2)}, u32[]{:S(2)}) collective-permute-start(bf16[1,264,128]{2,1,0:T(8,128)(2,1)S(1)} %bitcast.11), channel_id=1, source_target_pairs={{0,2},{2,0},{1,3},{3,1},{4,6},{6,4},{5,7},{7,5},{8,10},{10,8},{9,1... | collective-permute-start | bytes 202760 | tf_op jit(solution)/shard_map/ppermute | solution.py:277
  30.3 5.0 %collective-permute-start.14 = (bf16[1,264,128]{2,1,0:T(8,128)(2,1)S(1)}, bf16[1,264,128]{2,1,0:T(8,128)(2,1)S(1)}, u32[]{:S(2)}, u32[]{:S(2)}) collective-permute-start(bf16[1,264,128]{2,1,0:T(8,128)(2,1)S(1)} %bitcast.12), channel_id=1, source_target_pairs={{0,2},{2,0},{1,3},{3,1},{4,6},{6,4},{5,7},{7,5},{8,10},{10,8},{9,1... | collective-permute-start | bytes 202760 | tf_op jit(solution)/shard_map/ppermute | solution.py:277
  31.8 4.9 %collective-permute-start.15 = (bf16[1,264,128]{2,1,0:T(8,128)(2,1)S(1)}, bf16[1,264,128]{2,1,0:T(8,128)(2,1)S(1)}, u32[]{:S(2)}, u32[]{:S(2)}) collective-permute-start(bf16[1,264,128]{2,1,0:T(8,128)(2,1)S(1)} %bitcast.14), channel_id=1, source_target_pairs={{0,2},{2,0},{1,3},{3,1},{4,6},{6,4},{5,7},{7,5},{8,10},{10,8},{9,1... | collective-permute-start | bytes 202760 | tf_op jit(solution)/shard_map/ppermute | solution.py:277
  33.8 4.3 %collective-permute-start.10 = (bf16[1,264,128]{2,1,0:T(8,128)(2,1)S(1)}, bf16[1,264,128]{2,1,0:T(8,128)(2,1)S(1)}, u32[]{:S(2)}, u32[]{:S(2)}) collective-permute-start(bf16[1,264,128]{2,1,0:T(8,128)(2,1)S(1)} %bitcast.15), channel_id=1, source_target_pairs={{0,2},{2,0},{1,3},{3,1},{4,6},{6,4},{5,7},{7,5},{8,10},{10,8},{9,1... | collective-permute-start | bytes 202760 | tf_op jit(solution)/shard_map/ppermute | solution.py:277

commit v6 on v3

--- a/solution.py
+++ b/solution.py
@@ -425,7 +425,7 @@
     steps = list(range(1, sec_count))
     first_plan = (False, steps, [[0]] + [[k] for k in steps[:-2]] + [steps[-2:]])
     second_groups = [[0]] + [[k] for k in steps[1:2] + steps[:1] + steps[2:]]
-    second_plan = (can_pair, steps[1:] + steps[:1], [[0], steps[1:2], steps[2:] + steps[:1]])
+    second_plan = (False, steps, [[0]] + [[k] for k in steps[:-2]] + [steps[-2:]])
     params = pltpu.CompilerParams(vmem_limit_bytes=VMEM_BYTES)
     vec_shape = (sec_dev, half, width)
     vec_bf16 = jax.ShapeDtypeStruct(vec_shape, BF16)

time: 39.7 us -> 39.8 us (level)
  transfers between devices with their start and end apart: 15 -> 15, of which waited for: 9 -> 10; matrix products, arithmetic and copies ran while one was open for 0% -> 0% of each run, Pallas kernels for 7% -> 7%
where the time goes in v6:
time: 39.8 us; the launch traced here: 39.7 us
  starting transfers between devices  20.6 us (52%)
  waiting for transfers between devices  11.2 us (28%)
  Pallas kernels  7.13 us (18%)
  between operations  0.72 us (2%)
    ppermute x6, starting transfers between devices, exchange(): arrived[step] = lax.ppermute(packets[step], 'sec', turn)  11.5 us
    ppermute x6, starting transfers between devices, exchange(): lax.ppermute(packet, 'op', turn)  8.41 us
    ppermute x6, waiting for transfers between devices, exchange(): lax.ppermute(packet, 'op', turn)  6.73 us
    pallas_call x2, Pallas kernels, sigma_packets(): pl.pallas_call(functools.partial(product_kernel, is_first, split, paired,...  3.16 us
    ppermute x6, waiting for transfers between devices, exchange(): arrived[step] = lax.ppermute(packets[step], 'sec', turn)  2.96 us
    pallas_call x4, Pallas kernels, call(): pl.pallas_call(kernel, out_shape=outs, in_specs=[whole(pltpu.VMEM)] * len...  2.12 us
    pallas_call x1, Pallas kernels, body(): pl.pallas_call(load_kernel, out_shape=[vec_bf16, jax.ShapeDtypeStruct(lef...  1.84 us
    ppermute x3, waiting for transfers between devices, from_others(): arrays.append(lax.ppermute(array, 'rep', turn))  1.54 us
  transfers between devices with their start and end apart: 15, of which 10 were waited for; matrix products, arithmetic and copies ran while one was open for 0% of the time, Pallas kernels for 7%

profile of v6, /device:TPU:0, one launch (start us, length us, event | category | flops | bytes accessed | tf_op | source)
XLA Modules:
  0.0 39.7 jit_solution(5592607682401938055)
XLA Ops:
  0.6 0.0 copy-start
  0.6 0.5 %collective-permute-start = (bf16[4,128,256]{2,1,0:T(8,128)(2,1)}, bf16[4,128,256]{2,1,0:T(8,128)(2,1)S(1)}, u32[]{:S(2)}, u32[]{:S(2)}) collective-permute-start(bf16[4,128,256]{2,1,0:T(8,128)(2,1)} %psi_hbm.1), channel_id=1, source_target_pairs={{1,0},{0,1},{3,2},{2,3},{5,4},{4,5},{7,6},{6,7},{9,8},{8,9},{11,10... | collective-permute-start | bytes 786440 | tf_op jit(solution)/shard_map/ppermute | solution.py:437
  1.2 0.1 collective-permute-start.1
  1.2 1.8 %load.1 = (bf16[4,128,256]{2,1,0:T(8,128)(2,1)S(1)}, bf16[8,4,128,256]{3,2,1,0:T(8,128)(2,1)S(1)}, s32[4,128]{1,0:T(4,128)S(1)}, s32[8,128]{1,0:T(8,128)S(1)}, f...) custom-call(bf16[4,128,256]{2,1,0:T(8,128)(2,1)} %psi_hbm.1, bf16[8,4,128,256]{3,2,1,0:T(8,128)(2,1)} %left_hbm.1, ...), custom_call_target="tpu_custom_call" | custom-call | tf_op jit(solution)/shard_map/load/pallas_call | solution.py:442
  3.1 0.0 collective-permute-done.1.refs_7_
  3.1 0.0 collective-permute-done.refs_6_
  3.1 0.0 copy-done
  3.1 1.6 %products_first.1 = (bf16[264,128]{1,0:T(8,128)(2,1)S(1)}, bf16[264,128]{1,0:T(8,128)(2,1)S(1)}, bf16[264,128]{1,0:T(8,128)(2,1)S(1)}, bf16[264,128]{1,0:T(8,128)(2,1)S(1)}) custom-call(s32[4,128]{1,0:T(4,128)S(1)} %get-tuple-element.24.refs_0_, bf16[8,4,128,256]{3,2,1,0:T(8,128)(2,1)S(1)} %get-tuple-element.25.refs_1_, bf16[8,256,256]{2,1,0:T(8,128)(2,1)S(1)} %copy-done, ...), custom_call_target="tpu_custom_call" | custom-call | flops 1073741824 | bytes 3145728 | tf_op jit(solution)/shard_map/products_first/pallas_call | solution.py:249
  4.7 3.1 %collective-permute-start.5 = (bf16[264,128]{1,0:T(8,128)(2,1)S(1)}, bf16[264,128]{1,0:T(8,128)(2,1)S(1)}, u32[]{:S(2)}, u32[]{:S(2)}) collective-permute-start(bf16[264,128]{1,0:T(8,128)(2,1)S(1)} %get-tuple-element.32), channel_id=1, source_target_pairs={{0,4},{4,8},{8,12},{12,0},{1,5},{5,9},{9,13},{13,1},{2,6},{6,10},{... | collective-permute-start | bytes 202760 | tf_op jit(solution)/shard_map/ppermute | solution.py:283
  7.8 2.6 %collective-permute-start.2 = (bf16[264,128]{1,0:T(8,128)(2,1)S(1)}, bf16[264,128]{1,0:T(8,128)(2,1)S(1)}, u32[]{:S(2)}, u32[]{:S(2)}) collective-permute-start(bf16[264,128]{1,0:T(8,128)(2,1)S(1)} %get-tuple-element.29), channel_id=1, source_target_pairs={{0,8},{4,12},{8,0},{12,4},{1,9},{5,13},{9,1},{13,5},{2,10},{6,14},... | collective-permute-start | bytes 202760 | tf_op jit(solution)/shard_map/ppermute | solution.py:283
  10.4 1.4 %collective-permute-start.3 = (bf16[264,128]{1,0:T(8,128)(2,1)S(1)}, bf16[264,128]{1,0:T(8,128)(2,1)S(1)}, u32[]{:S(2)}, u32[]{:S(2)}) collective-permute-start(bf16[264,128]{1,0:T(8,128)(2,1)S(1)} %get-tuple-element.30), channel_id=1, source_target_pairs={{0,12},{4,0},{8,4},{12,8},{1,13},{5,1},{9,5},{13,9},{2,14},{6,2},{... | collective-permute-start | bytes 202760 | tf_op jit(solution)/shard_map/ppermute | solution.py:283
  11.7 1.5 %collective-permute-start.6 = (bf16[1,264,128]{2,1,0:T(8,128)(2,1)S(1)}, bf16[1,264,128]{2,1,0:T(8,128)(2,1)S(1)}, u32[]{:S(2)}, u32[]{:S(2)}) collective-permute-start(bf16[1,264,128]{2,1,0:T(8,128)(2,1)S(1)} %bitcast.14), channel_id=1, source_target_pairs={{0,2},{2,0},{1,3},{3,1},{4,6},{6,4},{5,7},{7,5},{8,10},{10,8},{9,1... | collective-permute-start | bytes 202760 | tf_op jit(solution)/shard_map/ppermute | solution.py:275
  13.2 0.0 collective-permute-done.5.refs_1_
  13.2 0.8 %collective-permute-start.7 = (bf16[1,264,128]{2,1,0:T(8,128)(2,1)S(1)}, bf16[1,264,128]{2,1,0:T(8,128)(2,1)S(1)}, u32[]{:S(2)}, u32[]{:S(2)}) collective-permute-start(bf16[1,264,128]{2,1,0:T(8,128)(2,1)S(1)} %bitcast.16), channel_id=1, source_target_pairs={{0,2},{2,0},{1,3},{3,1},{4,6},{6,4},{5,7},{7,5},{8,10},{10,8},{9,1... | collective-permute-start | bytes 202760 | tf_op jit(solution)/shard_map/ppermute | solution.py:275
  14.1 1.1 %collective-permute-done.2.refs_2_ = bf16[264,128]{1,0:T(8,128)(2,1)S(1)} collective-permute-done((bf16[264,128]{1,0:T(8,128)(2,1)S(1)}, bf16[264,128]{1,0:T(8,128)(2,1)S(1)}, u32[]{:S(2)}, u32[]{:S(2)}) %collective-permute-start.2) | collective-permute-done | bytes 67616 | tf_op jit(solution)/shard_map/ppermute | solution.py:283
  15.2 0.2 collective-permute-done.3.refs_3_
  15.4 1.6 %collective-permute-start.4 = (bf16[2,264,128]{2,1,0:T(8,128)(2,1)S(1)}, bf16[2,264,128]{2,1,0:T(8,128)(2,1)S(1)}, u32[]{:S(2)}, u32[]{:S(2)}) collective-permute-start(bf16[2,264,128]{2,1,0:T(8,128)(2,1)S(1)} %pad_maximum_fusion), channel_id=1, source_target_pairs={{0,2},{2,0},{1,3},{3,1},{4,6},{6,4},{5,7},{7,5},{8,10},{10,8},{9,1... | collective-permute-start | bytes 405512 | tf_op jit(solution)/shard_map/ppermute | solution.py:275
  17.0 0.0 collective-permute-done.6.refs_4_
  17.0 0.5 %collective-permute-done.7.refs_5_ = bf16[1,264,128]{2,1,0:T(8,128)(2,1)S(1)} collective-permute-done((bf16[1,264,128]{2,1,0:T(8,128)(2,1)S(1)}, bf16[1,264,128]{2,1,0:T(8,128)(2,1)S(1)}, u32[]{:S(2)}, u32[]{:S(2)}) %collective-permute-start.7) | collective-permute-done | bytes 67616 | tf_op jit(solution)/shard_map/ppermute | solution.py:275
  17.5 0.4 combine_first_early.1
  17.9 2.8 %collective-permute-done.4.refs_0_ = bf16[2,264,128]{2,1,0:T(8,128)(2,1)S(1)} collective-permute-done((bf16[2,264,128]{2,1,0:T(8,128)(2,1)S(1)}, bf16[2,264,128]{2,1,0:T(8,128)(2,1)S(1)}, u32[]{:S(2)}, u32[]{:S(2)}) %collective-permute-start.4) | collective-permute-done | bytes 135200 | tf_op jit(solution)/shard_map/ppermute | solution.py:275
  20.7 0.4 %combine_first.1 = (bf16[4,128,256]{2,1,0:T(8,128)(2,1)S(1)}, f32[4,128,256]{2,1,0:T(8,128)S(1)}, bf16[528,256]{1,0:T(8,128)(2,1)S(1)}) custom-call(bf16[2,264,128]{2,1,0:T(8,128)(2,1)S(1)} %collective-permute-done.4.refs_0_, s32[8,128]{1,0:T(8,128)S(1)} %get-tuple-element.27.refs_4_.refs_1_, ...), custom_call_target="tpu_custom_call" | custom-call | tf_op jit(solution)/shard_map/combine_first/pallas_call | solution.py:406
  21.1 0.1 collective-permute-start.8
  21.2 1.5 %collective-permute-done.8.refs_5_ = bf16[528,256]{1,0:T(8,128)(2,1)S(1)} collective-permute-done((bf16[528,256]{1,0:T(8,128)(2,1)S(1)}, bf16[528,256]{1,0:T(8,128)(2,1)S(1)}, u32[]{:S(2)}, u32[]{:S(2)}) %collective-permute-start.8) | collective-permute-done | bytes 270368 | tf_op jit(solution)/shard_map/ppermute | solution.py:437
  22.7 1.6 %products_second.1 = (bf16[264,128]{1,0:T(8,128)(2,1)S(1)}, bf16[264,128]{1,0:T(8,128)(2,1)S(1)}, bf16[264,128]{1,0:T(8,128)(2,1)S(1)}, bf16[264,128]{1,0:T(8,128)(2,1)S(1)}, bf16[4,128,256]{2,1,0:T(8,128)(2,1)}) custom-call(s32[4,128]{1,0:T(4,128)S(1)} %get-tuple-element.24.refs_0_, bf16[8,4,128,256]{3,2,1,0:T(8,128)(2,1)S(1)} %get-tuple-element.25.refs_1_, ...), custom_call_target="tpu_custom_call" | custom-call | flops 1073741824 | bytes 3145728 | tf_op jit(solution)/shard_map/products_second/pallas_call | solution.py:249
  24.3 2.1 %collective-permute-start.12 = (bf16[264,128]{1,0:T(8,128)(2,1)S(1)}, bf16[264,128]{1,0:T(8,128)(2,1)S(1)}, u32[]{:S(2)}, u32[]{:S(2)}) collective-permute-start(bf16[264,128]{1,0:T(8,128)(2,1)S(1)} %get-tuple-element.42), channel_id=1, source_target_pairs={{0,4},{4,8},{8,12},{12,0},{1,5},{5,9},{9,13},{13,1},{2,6},{6,10},{... | collective-permute-start | bytes 202760 | tf_op jit(solution)/shard_map/ppermute | solution.py:283
  26.3 1.3 %collective-permute-start.9 = (bf16[264,128]{1,0:T(8,128)(2,1)S(1)}, bf16[264,128]{1,0:T(8,128)(2,1)S(1)}, u32[]{:S(2)}, u32[]{:S(2)}) collective-permute-start(bf16[264,128]{1,0:T(8,128)(2,1)S(1)} %get-tuple-element.39), channel_id=1, source_target_pairs={{0,8},{4,12},{8,0},{12,4},{1,9},{5,13},{9,1},{13,5},{2,10},{6,14},... | collective-permute-start | bytes 202760 | tf_op jit(solution)/shard_map/ppermute | solution.py:283
  27.6 1.1 %collective-permute-start.10 = (bf16[264,128]{1,0:T(8,128)(2,1)S(1)}, bf16[264,128]{1,0:T(8,128)(2,1)S(1)}, u32[]{:S(2)}, u32[]{:S(2)}) collective-permute-start(bf16[264,128]{1,0:T(8,128)(2,1)S(1)} %get-tuple-element.40), channel_id=1, source_target_pairs={{0,12},{4,0},{8,4},{12,8},{1,13},{5,1},{9,5},{13,9},{2,14},{6,2},{... | collective-permute-start | bytes 202760 | tf_op jit(solution)/shard_map/ppermute | solution.py:283
  28.8 1.5 %collective-permute-start.13 = (bf16[1,264,128]{2,1,0:T(8,128)(2,1)S(1)}, bf16[1,264,128]{2,1,0:T(8,128)(2,1)S(1)}, u32[]{:S(2)}, u32[]{:S(2)}) collective-permute-start(bf16[1,264,128]{2,1,0:T(8,128)(2,1)S(1)} %bitcast.13), channel_id=1, source_target_pairs={{0,2},{2,0},{1,3},{3,1},{4,6},{6,4},{5,7},{7,5},{8,10},{10,8},{9,1... | collective-permute-start | bytes 202760 | tf_op jit(solution)/shard_map/ppermute | solution.py:275
  30.2 0.9 %collective-permute-done.12.refs_1_ = bf16[264,128]{1,0:T(8,128)(2,1)S(1)} collective-permute-done((bf16[264,128]{1,0:T(8,128)(2,1)S(1)}, bf16[264,128]{1,0:T(8,128)(2,1)S(1)}, u32[]{:S(2)}, u32[]{:S(2)}) %collective-permute-start.12) | collective-permute-done | bytes 67616 | tf_op jit(solution)/shard_map/ppermute | solution.py:283
  31.1 1.5 %collective-permute-start.14 = (bf16[1,264,128]{2,1,0:T(8,128)(2,1)S(1)}, bf16[1,264,128]{2,1,0:T(8,128)(2,1)S(1)}, u32[]{:S(2)}, u32[]{:S(2)}) collective-permute-start(bf16[1,264,128]{2,1,0:T(8,128)(2,1)S(1)} %bitcast.15), channel_id=1, source_target_pairs={{0,2},{2,0},{1,3},{3,1},{4,6},{6,4},{5,7},{7,5},{8,10},{10,8},{9,1... | collective-permute-start | bytes 202760 | tf_op jit(solution)/shard_map/ppermute | solution.py:275
  32.6 0.7 %collective-permute-done.9.refs_2_ = bf16[264,128]{1,0:T(8,128)(2,1)S(1)} collective-permute-done((bf16[264,128]{1,0:T(8,128)(2,1)S(1)}, bf16[264,128]{1,0:T(8,128)(2,1)S(1)}, u32[]{:S(2)}, u32[]{:S(2)}) %collective-permute-start.9) | collective-permute-done | bytes 67616 | tf_op jit(solution)/shard_map/ppermute | solution.py:283
  33.3 0.1 collective-permute-done.10.refs_3_
  33.4 1.5 %collective-permute-start.11 = (bf16[2,264,128]{2,1,0:T(8,128)(2,1)S(1)}, bf16[2,264,128]{2,1,0:T(8,128)(2,1)S(1)}, u32[]{:S(2)}, u32[]{:S(2)}) collective-permute-start(bf16[2,264,128]{2,1,0:T(8,128)(2,1)S(1)} %pad_maximum_fusion.1), channel_id=1, source_target_pairs={{0,2},{2,0},{1,3},{3,1},{4,6},{6,4},{5,7},{7,5},{8,10},{10,8},{9,1... | collective-permute-start | bytes 405512 | tf_op jit(solution)/shard_map/ppermute | solution.py:275
  34.9 0.0 collective-permute-done.13.refs_4_
  34.9 0.5 %collective-permute-done.14.refs_5_ = bf16[1,264,128]{2,1,0:T(8,128)(2,1)S(1)} collective-permute-done((bf16[1,264,128]{2,1,0:T(8,128)(2,1)S(1)}, bf16[1,264,128]{2,1,0:T(8,128)(2,1)S(1)}, u32[]{:S(2)}, u32[]{:S(2)}) %collective-permute-start.14) | collective-permute-done | bytes 67616 | tf_op jit(solution)/shard_map/ppermute | solution.py:275
  35.4 0.4 %combine_second_early.1 = (f32[4,128,256]{2,1,0:T(8,128)S(1)}, f32[8,128]{1,0:T(8,128)S(1)}) custom-call(bf16[264,128]{1,0:T(8,128)(2,1)S(1)} %get-tuple-element.41.refs_0_, bf16[264,128]{1,0:T(8,128)(2,1)S(1)} %collective-permute-done.12.refs_1_, bf16[264,128]{1,0:T(8,128)(2,1)S(1)} %collective-permute-done.9.refs_2_, ...), custom_call_target="tpu_custom_call" | custom-call | flops 1000000000 | tf_op jit(solution)/shard_map/combine_second_early/pallas_call | solution.py:406
  35.8 2.9 %collective-permute-done.11.refs_0_ = bf16[2,264,128]{2,1,0:T(8,128)(2,1)S(1)} collective-permute-done((bf16[2,264,128]{2,1,0:T(8,128)(2,1)S(1)}, bf16[2,264,128]{2,1,0:T(8,128)(2,1)S(1)}, u32[]{:S(2)}, u32[]{:S(2)}) %collective-permute-start.11) | collective-permute-done | bytes 135200 | tf_op jit(solution)/shard_map/ppermute | solution.py:275
  38.8 0.9 %combine_second.1 = bf16[4,128,256]{2,1,0:T(8,128)(2,1)} custom-call(bf16[2,264,128]{2,1,0:T(8,128)(2,1)S(1)} %collective-permute-done.11.refs_0_, s32[8,128]{1,0:T(8,128)S(1)} %get-tuple-element.27.refs_4_.refs_1_, f32[4,128,256]{2,1,0:T(8,128)S(1)} %get-tuple-element.44.refs_2_, f32[8,128]{1,0:T(8,128)S(1)} %get-tuple-element.45.refs_3_), custom_call_target="tpu_custom_call" | custom-call | tf_op jit(solution)/shard_map/combine_second/pallas_call | solution.py:406
  (2 shorter events, 0.0 us)
Async XLA Ops:
  0.6 2.5 %copy-start = (bf16[8,256,256]{2,1,0:T(8,128)(2,1)S(1)}, bf16[8,256,256]{2,1,0:T(8,128)(2,1)}, u32[]{:S(2)}) copy-start(bf16[8,256,256]{2,1,0:T(8,128)(2,1)} %refs_2_.3) | copy-start | bytes 3145732
  0.6 2.5 %collective-permute-start = (bf16[4,128,256]{2,1,0:T(8,128)(2,1)}, bf16[4,128,256]{2,1,0:T(8,128)(2,1)S(1)}, u32[]{:S(2)}, u32[]{:S(2)}) collective-permute-start(bf16[4,128,256]{2,1,0:T(8,128)(2,1)} %psi_hbm.1), channel_id=1, source_target_pairs={{1,0},{0,1},{3,2},{2,3},{5,4},{4,5},{7,6},{6,7},{9,8},{8,9},{11,10... | collective-permute-start | bytes 786440 | tf_op jit(solution)/shard_map/ppermute | solution.py:437
  1.2 1.9 %collective-permute-start.1 = (f32[4,128]{1,0:T(4,128)}, f32[4,128]{1,0:T(4,128)S(1)}, u32[]{:S(2)}, u32[]{:S(2)}) collective-permute-start(f32[4,128]{1,0:T(4,128)} %energy_hbm.1), channel_id=1, source_target_pairs={{1,0},{0,1},{3,2},{2,3},{5,4},{4,5},{7,6},{6,7},{9,8},{8,9},{11,10... | collective-permute-start | bytes 6152 | tf_op jit(solution)/shard_map/ppermute | solution.py:437
  4.7 8.5 %collective-permute-start.5 = (bf16[264,128]{1,0:T(8,128)(2,1)S(1)}, bf16[264,128]{1,0:T(8,128)(2,1)S(1)}, u32[]{:S(2)}, u32[]{:S(2)}) collective-permute-start(bf16[264,128]{1,0:T(8,128)(2,1)S(1)} %get-tuple-element.32), channel_id=1, source_target_pairs={{0,4},{4,8},{8,12},{12,0},{1,5},{5,9},{9,13},{13,1},{2,6},{6,10},{... | collective-permute-start | bytes 202760 | tf_op jit(solution)/shard_map/ppermute | solution.py:283
  7.8 7.4 %collective-permute-start.2 = (bf16[264,128]{1,0:T(8,128)(2,1)S(1)}, bf16[264,128]{1,0:T(8,128)(2,1)S(1)}, u32[]{:S(2)}, u32[]{:S(2)}) collective-permute-start(bf16[264,128]{1,0:T(8,128)(2,1)S(1)} %get-tuple-element.29), channel_id=1, source_target_pairs={{0,8},{4,12},{8,0},{12,4},{1,9},{5,13},{9,1},{13,5},{2,10},{6,14},... | collective-permute-start | bytes 202760 | tf_op jit(solution)/shard_map/ppermute | solution.py:283
  10.4 5.0 %collective-permute-start.3 = (bf16[264,128]{1,0:T(8,128)(2,1)S(1)}, bf16[264,128]{1,0:T(8,128)(2,1)S(1)}, u32[]{:S(2)}, u32[]{:S(2)}) collective-permute-start(bf16[264,128]{1,0:T(8,128)(2,1)S(1)} %get-tuple-element.30), channel_id=1, source_target_pairs={{0,12},{4,0},{8,4},{12,8},{1,13},{5,1},{9,5},{13,9},{2,14},{6,2},{... | collective-permute-start | bytes 202760 | tf_op jit(solution)/shard_map/ppermute | solution.py:283
  11.7 5.3 %collective-permute-start.6 = (bf16[1,264,128]{2,1,0:T(8,128)(2,1)S(1)}, bf16[1,264,128]{2,1,0:T(8,128)(2,1)S(1)}, u32[]{:S(2)}, u32[]{:S(2)}) collective-permute-start(bf16[1,264,128]{2,1,0:T(8,128)(2,1)S(1)} %bitcast.14), channel_id=1, source_target_pairs={{0,2},{2,0},{1,3},{3,1},{4,6},{6,4},{5,7},{7,5},{8,10},{10,8},{9,1... | collective-permute-start | bytes 202760 | tf_op jit(solution)/shard_map/ppermute | solution.py:275
  13.2 4.3 %collective-permute-start.7 = (bf16[1,264,128]{2,1,0:T(8,128)(2,1)S(1)}, bf16[1,264,128]{2,1,0:T(8,128)(2,1)S(1)}, u32[]{:S(2)}, u32[]{:S(2)}) collective-permute-start(bf16[1,264,128]{2,1,0:T(8,128)(2,1)S(1)} %bitcast.16), channel_id=1, source_target_pairs={{0,2},{2,0},{1,3},{3,1},{4,6},{6,4},{5,7},{7,5},{8,10},{10,8},{9,1... | collective-permute-start | bytes 202760 | tf_op jit(solution)/shard_map/ppermute | solution.py:275
  15.4 5.3 %collective-permute-start.4 = (bf16[2,264,128]{2,1,0:T(8,128)(2,1)S(1)}, bf16[2,264,128]{2,1,0:T(8,128)(2,1)S(1)}, u32[]{:S(2)}, u32[]{:S(2)}) collective-permute-start(bf16[2,264,128]{2,1,0:T(8,128)(2,1)S(1)} %pad_maximum_fusion), channel_id=1, source_target_pairs={{0,2},{2,0},{1,3},{3,1},{4,6},{6,4},{5,7},{7,5},{8,10},{10,8},{9,1... | collective-permute-start | bytes 405512 | tf_op jit(solution)/shard_map/ppermute | solution.py:275
  21.1 1.6 %collective-permute-start.8 = (bf16[528,256]{1,0:T(8,128)(2,1)S(1)}, bf16[528,256]{1,0:T(8,128)(2,1)S(1)}, u32[]{:S(2)}, u32[]{:S(2)}) collective-permute-start(bf16[528,256]{1,0:T(8,128)(2,1)S(1)} %get-tuple-element.37.refs_4_.refs_6_), channel_id=1, source_target_pairs={{1,0},{0,1},{3,2},{2,3},{5,4},{4,5},{7,6},{6,7},{9,8},{8,9},{11,10... | collective-permute-start | bytes 811016 | tf_op jit(solution)/shard_map/ppermute | solution.py:437
  24.3 6.8 %collective-permute-start.12 = (bf16[264,128]{1,0:T(8,128)(2,1)S(1)}, bf16[264,128]{1,0:T(8,128)(2,1)S(1)}, u32[]{:S(2)}, u32[]{:S(2)}) collective-permute-start(bf16[264,128]{1,0:T(8,128)(2,1)S(1)} %get-tuple-element.42), channel_id=1, source_target_pairs={{0,4},{4,8},{8,12},{12,0},{1,5},{5,9},{9,13},{13,1},{2,6},{6,10},{... | collective-permute-start | bytes 202760 | tf_op jit(solution)/shard_map/ppermute | solution.py:283
  26.3 7.0 %collective-permute-start.9 = (bf16[264,128]{1,0:T(8,128)(2,1)S(1)}, bf16[264,128]{1,0:T(8,128)(2,1)S(1)}, u32[]{:S(2)}, u32[]{:S(2)}) collective-permute-start(bf16[264,128]{1,0:T(8,128)(2,1)S(1)} %get-tuple-element.39), channel_id=1, source_target_pairs={{0,8},{4,12},{8,0},{12,4},{1,9},{5,13},{9,1},{13,5},{2,10},{6,14},... | collective-permute-start | bytes 202760 | tf_op jit(solution)/shard_map/ppermute | solution.py:283
  27.6 5.7 %collective-permute-start.10 = (bf16[264,128]{1,0:T(8,128)(2,1)S(1)}, bf16[264,128]{1,0:T(8,128)(2,1)S(1)}, u32[]{:S(2)}, u32[]{:S(2)}) collective-permute-start(bf16[264,128]{1,0:T(8,128)(2,1)S(1)} %get-tuple-element.40), channel_id=1, source_target_pairs={{0,12},{4,0},{8,4},{12,8},{1,13},{5,1},{9,5},{13,9},{2,14},{6,2},{... | collective-permute-start | bytes 202760 | tf_op jit(solution)/shard_map/ppermute | solution.py:283
  28.8 6.2 %collective-permute-start.13 = (bf16[1,264,128]{2,1,0:T(8,128)(2,1)S(1)}, bf16[1,264,128]{2,1,0:T(8,128)(2,1)S(1)}, u32[]{:S(2)}, u32[]{:S(2)}) collective-permute-start(bf16[1,264,128]{2,1,0:T(8,128)(2,1)S(1)} %bitcast.13), channel_id=1, source_target_pairs={{0,2},{2,0},{1,3},{3,1},{4,6},{6,4},{5,7},{7,5},{8,10},{10,8},{9,1... | collective-permute-start | bytes 202760 | tf_op jit(solution)/shard_map/ppermute | solution.py:275
  31.1 4.3 %collective-permute-start.14 = (bf16[1,264,128]{2,1,0:T(8,128)(2,1)S(1)}, bf16[1,264,128]{2,1,0:T(8,128)(2,1)S(1)}, u32[]{:S(2)}, u32[]{:S(2)}) collective-permute-start(bf16[1,264,128]{2,1,0:T(8,128)(2,1)S(1)} %bitcast.15), channel_id=1, source_target_pairs={{0,2},{2,0},{1,3},{3,1},{4,6},{6,4},{5,7},{7,5},{8,10},{10,8},{9,1... | collective-permute-start | bytes 202760 | tf_op jit(solution)/shard_map/ppermute | solution.py:275
  33.4 5.4 %collective-permute-start.11 = (bf16[2,264,128]{2,1,0:T(8,128)(2,1)S(1)}, bf16[2,264,128]{2,1,0:T(8,128)(2,1)S(1)}, u32[]{:S(2)}, u32[]{:S(2)}) collective-permute-start(bf16[2,264,128]{2,1,0:T(8,128)(2,1)S(1)} %pad_maximum_fusion.1), channel_id=1, source_target_pairs={{0,2},{2,0},{1,3},{3,1},{4,6},{6,4},{5,7},{7,5},{8,10},{10,8},{9,1... | collective-permute-start | bytes 405512 | tf_op jit(solution)/shard_map/ppermute | solution.py:275

commit v7 on v6

--- a/solution.py
+++ b/solution.py
@@ -11,6 +11,7 @@
 HEAD = 8
 PARTS = 3
 EARLY_FLOPS = 10**9
+SLOT_ROW = 2
 MORE_ROWS = 16
 LANES = 128
 VMEM_BYTES = 24 * 1024 * 1024
@@ -266,7 +267,7 @@
     )(*operands)
 
 
-def exchange(packets, split, paired, order, groups):
+def exchange(packets, split, paired, order, groups, bare=0):
     sec_count = lax.axis_size("sec")
     op_count = lax.axis_size("op")
     op_turns = [
@@ -281,7 +282,9 @@
         reach = (lambda i: i ^ step) if paired else (lambda i: (i + step) % sec_count)
         turn = [(i, reach(i)) for i in range(sec_count)]
         arrived[step] = lax.ppermute(packets[step], "sec", turn)
-    crossed = [over_op(jnp.stack([arrived[step] for step in group])) for group in groups]
+    crossed = [
+        over_op(jnp.stack([arrived[step][:bare or None] for step in group])) for group in groups
+    ]
     return [arrived[step] for step in [0, *order]] + sum(crossed[:-1], []), crossed[-1]
 
 
@@ -293,13 +296,15 @@
     ]
 
 
-def add_packets(packet_refs, split, half, base_ref):
+def add_packets(packet_refs, split, half, base_ref, slots=()):
     sec_dev, _, width = base_ref.shape
     own = lax.axis_size("sec") if split else 1
     body_rows = width // LANES * half
     if split:
         packet_refs = views(packet_refs)
-        heads = [ref[body_rows:].astype(F32) for ref in packet_refs]
+        with_head = packet_refs[:len(packet_refs) - len(slots)]
+        heads = [ref[body_rows:].astype(F32) for ref in with_head]
+        heads += slots
         for column in range(width // LANES):
             lanes = slice(column * LANES, (column + 1) * LANES)
             for s in range(sec_dev):
@@ -326,14 +331,15 @@
     return head_sum
 
 
-def late_sum(packet_refs, s, half, width):
+def late_sum(packet_refs, s, half, width, slots=()):
     body_rows = width // LANES * half
     value = jnp.zeros((half, width), F32)
-    for ref in views(packet_refs):
+    for i, ref in enumerate(views(packet_refs)):
         body = jnp.concatenate(
             [ref[c * half:(c + 1) * half].astype(F32) for c in range(width // LANES)], axis=1
         )
-        slot = spread(ref[body_rows:].astype(F32)[0:1], width)
+        slot = slots[i] if slots else ref[body_rows:].astype(F32)[0:1]
+        slot = spread(slot, width)
         value += jnp.where(slot == s, body, 0.0)
     return value
 
@@ -348,12 +354,35 @@
     norm = head_scalar(head_sum, 0)
     scalar_ref[0:1] = norm
     scalar_ref[1:2] = head_scalar(head_sum, 1) / norm
+    if split:
+        crossed = views(packet_refs)[lax.axis_size("sec"):]
+        for i, ref in enumerate(crossed):
+            scalar_ref[SLOT_ROW + i:SLOT_ROW + i + 1] = crossed_slot(ref, half, width)
+
+
+def crossed_slot(ref, half, width):
+    return ref[width // LANES * half:].astype(F32)[0:1]
+
+
+def known_slots(slot_ref, steps):
+    sec_count = lax.axis_size("sec")
+    sec = lax.axis_index("sec")
+    rows = [remainder(sec - (sec ^ step) + sec_count, sec_count) for step in steps]
+    return [slot_ref[pl.ds(row, 1), :] for row in rows]
 
 
 def first_kernel(count, *refs):
     packet_refs = refs[:count]
-    limit_ref, start_ref, base_ref, scalar_ref, first_ref, one_ref, vec_ref = refs[count:]
+    limit_ref, start_ref, base_ref, scalar_ref, first_ref, one_ref, vec_ref, slot_ref = refs[count:]
     sec_dev, half, width = start_ref.shape
+    late = views(packet_refs)
+    early_count = lax.axis_size("sec") - len(late)
+    slot_ref[...] = jnp.zeros_like(slot_ref)
+    if late:
+        slot_ref[0:early_count] = scalar_ref[SLOT_ROW:SLOT_ROW + early_count]
+        for i, ref in enumerate(late):
+            row = early_count + i
+            slot_ref[row:row + 1] = crossed_slot(ref, half, width)
     shift = spread(scalar_ref[1:2], width)
     first_row = lax.axis_index("rep") * half
     cross = jnp.zeros((8, width), F32)
@@ -372,14 +401,14 @@
     vec_ref[sec_dev * half:] = header(jnp.int32(0), scalars, (MORE_ROWS, width))
 
 
-def second_early_kernel(split, count, entries, *refs):
+def second_early_kernel(split, count, entries, steps, *refs):
     packet_refs = refs[:count]
-    vec_ref, energy_ref, one_ref, scalar_ref, base_ref, scale_ref = refs[count:]
+    slot_ref, vec_ref, energy_ref, one_ref, scalar_ref, base_ref, scale_ref = refs[count:]
     sec_dev, half, width = one_ref.shape
     for s in range(sec_dev):
         vector = vec_ref[s * half:(s + 1) * half].astype(F32)
         base_ref[s] = spread(energy_ref[s], width) * vector
-    head_sum = add_packets(packet_refs, split, half, base_ref)
+    head_sum = add_packets(packet_refs, split, half, base_ref, known_slots(slot_ref, steps))
     cross = head_scalar(head_sum, 0)
     square = head_scalar(head_sum, 1)
     excess = cross / scalar_ref[0:1]
@@ -390,15 +419,16 @@
         base_ref[s] = base_ref[s] - spread(excess, width) * one_ref[s]
 
 
-def second_kernel(count, *refs):
+def second_kernel(count, steps, *refs):
     packet_refs = refs[:count]
-    limit_ref, base_ref, scale_ref, second_ref = refs[count:]
+    slot_ref, limit_ref, base_ref, scale_ref, second_ref = refs[count:]
     sec_dev, half, width = base_ref.shape
     scale = spread(scale_ref[0:1], width)
+    slots = known_slots(slot_ref, steps)
     first_row = lax.axis_index("rep") * half
     for s in range(sec_dev):
         mask = live(limit_ref, s, first_row, (half, width))
-        value = scale * (base_ref[s] + late_sum(packet_refs, s, half, width))
+        value = scale * (base_ref[s] + late_sum(packet_refs, s, half, width, slots))
         second_ref[s] = jnp.where(mask, value, 0.0).astype(BF16)
 
 
@@ -425,7 +455,8 @@
     steps = list(range(1, sec_count))
     first_plan = (False, steps, [[0]] + [[k] for k in steps[:-2]] + [steps[-2:]])
     second_groups = [[0]] + [[k] for k in steps[1:2] + steps[:1] + steps[2:]]
-    second_plan = (False, steps, [[0]] + [[k] for k in steps[:-2]] + [steps[-2:]])
+    second_plan = (can_pair, steps[1:2] + steps[:1] + steps[2:], second_groups)
+    known = split and can_pair and op_count == 2 and sec_count <= 4
     params = pltpu.CompilerParams(vmem_limit_bytes=VMEM_BYTES)
     vec_shape = (sec_dev, half, width)
     vec_bf16 = jax.ShapeDtypeStruct(vec_shape, BF16)
@@ -480,12 +511,13 @@
         functools.partial(first_early_kernel, split, len(early)), "combine_first_early",
         [block_f32, row_f32], *early, start, levels, flops=EARLY_FLOPS,
     )
-    first, sigma_one, vector = call(
+    first, sigma_one, vector, slots = call(
         functools.partial(first_kernel, len(late)), "combine_first",
         [
             pltpu.VMEM(vec_shape, BF16),
             block_f32,
             jax.ShapeDtypeStruct((sec_dev * half + MORE_ROWS, width), BF16),
+            row_f32,
         ],
         *late, limits, start, base, scalars,
     )
@@ -494,15 +526,20 @@
         False, split, second_plan[0], rep_count, lists, left_env, right_env,
         [first, vector, *from_others(vector)],
     )
-    early, late = exchange(packets, split, *second_plan)
+    bare = width // LANES * half if known else 0
+    early, late = exchange(packets, split, *second_plan, bare)
+    crossed = sum(second_plan[2], []) if known else []
+    late_steps = second_plan[2][-1] if known else []
     base, scale = call(
-        functools.partial(second_early_kernel, split, len(early), entries),
-        "combine_second_early", [block_f32, row_f32], *early, vector, levels, sigma_one, scalars,
+        functools.partial(
+            second_early_kernel, split, len(early), entries, crossed[:len(crossed) - len(late_steps)]
+        ),
+        "combine_second_early", [block_f32, row_f32], *early, slots, vector, levels, sigma_one, scalars,
         flops=EARLY_FLOPS,
     )
     (second_out,) = call(
-        functools.partial(second_kernel, len(late)), "combine_second", [vec_bf16],
-        *late, limits, base, scale,
+        functools.partial(second_kernel, len(late), late_steps), "combine_second", [vec_bf16],
+        *late, slots, limits, base, scale,
     )
     return (first_out, second_out)
 

time: 39.8 us -> 40.5 us (1.018)
    ppermute x6, waiting for transfers between devices: 2.96 us -> 4.15 us  [exchange(): arrived[step] = lax.ppermute(packets[step], 'sec', turn)]
    ppermute x6 -> x7, waiting for transfers between devices: 6.73 us -> 5.78 us  [exchange(): lax.ppermute(packet, 'op', turn)]
    ppermute x6 -> x7, starting transfers between devices: 8.41 us -> 8.91 us  [exchange(): lax.ppermute(packet, 'op', turn)]
  transfers between devices with their start and end apart: 15 -> 16, of which waited for: 10 -> 9; matrix products, arithmetic and copies ran while one was open for 0% -> 0% of each run, Pallas kernels for 7% -> 7%
where the time goes in v7:
time: 40.5 us; the launch traced here: 40.4 us
  starting transfers between devices  21 us (52%)
  waiting for transfers between devices  11.5 us (28%)
  Pallas kernels  7.15 us (18%)
  between operations  0.72 us (2%)
    ppermute x6, starting transfers between devices, exchange(): arrived[step] = lax.ppermute(packets[step], 'sec', turn)  11.4 us
    ppermute x7, starting transfers between devices, exchange(): lax.ppermute(packet, 'op', turn)  8.91 us
    ppermute x7, waiting for transfers between devices, exchange(): lax.ppermute(packet, 'op', turn)  5.78 us
    ppermute x6, waiting for transfers between devices, exchange(): arrived[step] = lax.ppermute(packets[step], 'sec', turn)  4.15 us
    pallas_call x2, Pallas kernels, sigma_packets(): pl.pallas_call(functools.partial(product_kernel, is_first, split, paired,...  3.17 us
    pallas_call x4, Pallas kernels, call(): pl.pallas_call(kernel, out_shape=outs, in_specs=[whole(pltpu.VMEM)] * len...  2.13 us
    pallas_call x1, Pallas kernels, body(): pl.pallas_call(load_kernel, out_shape=[vec_bf16, jax.ShapeDtypeStruct(lef...  1.84 us
    ppermute x3, waiting for transfers between devices, from_others(): arrays.append(lax.ppermute(array, 'rep', turn))  1.54 us
  transfers between devices with their start and end apart: 16, of which 9 were waited for; matrix products, arithmetic and copies ran while one was open for 0% of the time, Pallas kernels for 7%

profile of v7, /device:TPU:0, one launch (start us, length us, event | category | flops | bytes accessed | tf_op | source)
XLA Modules:
  0.0 40.4 jit_solution(7376206329845789803)
XLA Ops:
  0.6 0.0 copy-start
  0.6 0.5 %collective-permute-start = (bf16[4,128,256]{2,1,0:T(8,128)(2,1)}, bf16[4,128,256]{2,1,0:T(8,128)(2,1)S(1)}, u32[]{:S(2)}, u32[]{:S(2)}) collective-permute-start(bf16[4,128,256]{2,1,0:T(8,128)(2,1)} %psi_hbm.1), channel_id=1, source_target_pairs={{1,0},{0,1},{3,2},{2,3},{5,4},{4,5},{7,6},{6,7},{9,8},{8,9},{11,10... | collective-permute-start | bytes 786440 | tf_op jit(solution)/shard_map/ppermute | solution.py:468
  1.2 0.1 collective-permute-start.1
  1.2 1.8 %load.1 = (bf16[4,128,256]{2,1,0:T(8,128)(2,1)S(1)}, bf16[8,4,128,256]{3,2,1,0:T(8,128)(2,1)S(1)}, s32[4,128]{1,0:T(4,128)S(1)}, s32[8,128]{1,0:T(8,128)S(1)}, f...) custom-call(bf16[4,128,256]{2,1,0:T(8,128)(2,1)} %psi_hbm.1, bf16[8,4,128,256]{3,2,1,0:T(8,128)(2,1)} %left_hbm.1, ...), custom_call_target="tpu_custom_call" | custom-call | tf_op jit(solution)/shard_map/load/pallas_call | solution.py:473
  3.1 0.0 collective-permute-done.1.refs_7_
  3.1 0.0 collective-permute-done.refs_6_
  3.1 0.0 copy-done
  3.1 1.6 %products_first.1 = (bf16[264,128]{1,0:T(8,128)(2,1)S(1)}, bf16[264,128]{1,0:T(8,128)(2,1)S(1)}, bf16[264,128]{1,0:T(8,128)(2,1)S(1)}, bf16[264,128]{1,0:T(8,128)(2,1)S(1)}) custom-call(s32[4,128]{1,0:T(4,128)S(1)} %get-tuple-element.25.refs_0_, bf16[8,4,128,256]{3,2,1,0:T(8,128)(2,1)S(1)} %get-tuple-element.26.refs_1_, bf16[8,256,256]{2,1,0:T(8,128)(2,1)S(1)} %copy-done, ...), custom_call_target="tpu_custom_call" | custom-call | flops 1073741824 | bytes 3145728 | tf_op jit(solution)/shard_map/products_first/pallas_call | solution.py:250
  4.7 3.1 %collective-permute-start.5 = (bf16[264,128]{1,0:T(8,128)(2,1)S(1)}, bf16[264,128]{1,0:T(8,128)(2,1)S(1)}, u32[]{:S(2)}, u32[]{:S(2)}) collective-permute-start(bf16[264,128]{1,0:T(8,128)(2,1)S(1)} %get-tuple-element.33), channel_id=1, source_target_pairs={{0,4},{4,8},{8,12},{12,0},{1,5},{5,9},{9,13},{13,1},{2,6},{6,10},{... | collective-permute-start | bytes 202760 | tf_op jit(solution)/shard_map/ppermute | solution.py:284
  7.8 2.6 %collective-permute-start.2 = (bf16[264,128]{1,0:T(8,128)(2,1)S(1)}, bf16[264,128]{1,0:T(8,128)(2,1)S(1)}, u32[]{:S(2)}, u32[]{:S(2)}) collective-permute-start(bf16[264,128]{1,0:T(8,128)(2,1)S(1)} %get-tuple-element.30), channel_id=1, source_target_pairs={{0,8},{4,12},{8,0},{12,4},{1,9},{5,13},{9,1},{13,5},{2,10},{6,14},... | collective-permute-start | bytes 202760 | tf_op jit(solution)/shard_map/ppermute | solution.py:284
  10.4 1.3 %collective-permute-start.3 = (bf16[264,128]{1,0:T(8,128)(2,1)S(1)}, bf16[264,128]{1,0:T(8,128)(2,1)S(1)}, u32[]{:S(2)}, u32[]{:S(2)}) collective-permute-start(bf16[264,128]{1,0:T(8,128)(2,1)S(1)} %get-tuple-element.31), channel_id=1, source_target_pairs={{0,12},{4,0},{8,4},{12,8},{1,13},{5,1},{9,5},{13,9},{2,14},{6,2},{... | collective-permute-start | bytes 202760 | tf_op jit(solution)/shard_map/ppermute | solution.py:284
  11.7 1.5 %collective-permute-start.6 = (bf16[1,264,128]{2,1,0:T(8,128)(2,1)S(1)}, bf16[1,264,128]{2,1,0:T(8,128)(2,1)S(1)}, u32[]{:S(2)}, u32[]{:S(2)}) collective-permute-start(bf16[1,264,128]{2,1,0:T(8,128)(2,1)S(1)} %bitcast.15), channel_id=1, source_target_pairs={{0,2},{2,0},{1,3},{3,1},{4,6},{6,4},{5,7},{7,5},{8,10},{10,8},{9,1... | collective-permute-start | bytes 202760 | tf_op jit(solution)/shard_map/ppermute | solution.py:276
  13.2 0.0 collective-permute-done.5.refs_1_
  13.2 0.8 %collective-permute-start.7 = (bf16[1,264,128]{2,1,0:T(8,128)(2,1)S(1)}, bf16[1,264,128]{2,1,0:T(8,128)(2,1)S(1)}, u32[]{:S(2)}, u32[]{:S(2)}) collective-permute-start(bf16[1,264,128]{2,1,0:T(8,128)(2,1)S(1)} %bitcast.16), channel_id=1, source_target_pairs={{0,2},{2,0},{1,3},{3,1},{4,6},{6,4},{5,7},{7,5},{8,10},{10,8},{9,1... | collective-permute-start | bytes 202760 | tf_op jit(solution)/shard_map/ppermute | solution.py:276
  14.1 1.1 %collective-permute-done.2.refs_2_ = bf16[264,128]{1,0:T(8,128)(2,1)S(1)} collective-permute-done((bf16[264,128]{1,0:T(8,128)(2,1)S(1)}, bf16[264,128]{1,0:T(8,128)(2,1)S(1)}, u32[]{:S(2)}, u32[]{:S(2)}) %collective-permute-start.2) | collective-permute-done | bytes 67616 | tf_op jit(solution)/shard_map/ppermute | solution.py:284
  15.2 0.2 collective-permute-done.3.refs_3_
  15.4 1.5 %collective-permute-start.4 = (bf16[2,264,128]{2,1,0:T(8,128)(2,1)S(1)}, bf16[2,264,128]{2,1,0:T(8,128)(2,1)S(1)}, u32[]{:S(2)}, u32[]{:S(2)}) collective-permute-start(bf16[2,264,128]{2,1,0:T(8,128)(2,1)S(1)} %pad_maximum_fusion), channel_id=1, source_target_pairs={{0,2},{2,0},{1,3},{3,1},{4,6},{6,4},{5,7},{7,5},{8,10},{10,8},{9,1... | collective-permute-start | bytes 405512 | tf_op jit(solution)/shard_map/ppermute | solution.py:276
  17.0 0.0 collective-permute-done.6.refs_4_
  17.0 0.5 %collective-permute-done.7.refs_5_ = bf16[1,264,128]{2,1,0:T(8,128)(2,1)S(1)} collective-permute-done((bf16[1,264,128]{2,1,0:T(8,128)(2,1)S(1)}, bf16[1,264,128]{2,1,0:T(8,128)(2,1)S(1)}, u32[]{:S(2)}, u32[]{:S(2)}) %collective-permute-start.7) | collective-permute-done | bytes 67616 | tf_op jit(solution)/shard_map/ppermute | solution.py:276
  17.5 0.4 combine_first_early.1
  17.9 2.8 %collective-permute-done.4.refs_0_ = bf16[2,264,128]{2,1,0:T(8,128)(2,1)S(1)} collective-permute-done((bf16[2,264,128]{2,1,0:T(8,128)(2,1)S(1)}, bf16[2,264,128]{2,1,0:T(8,128)(2,1)S(1)}, u32[]{:S(2)}, u32[]{:S(2)}) %collective-permute-start.4) | collective-permute-done | bytes 135200 | tf_op jit(solution)/shard_map/ppermute | solution.py:276
  20.7 0.4 %combine_first.1 = (bf16[4,128,256]{2,1,0:T(8,128)(2,1)S(1)}, f32[4,128,256]{2,1,0:T(8,128)S(1)}, bf16[528,256]{1,0:T(8,128)(2,1)S(1)}, f32[8,128]{1,0:T(8,128)S(1)}) custom-call(bf16[2,264,128]{2,1,0:T(8,128)(2,1)S(1)} %collective-permute-done.4.refs_0_, s32[8,128]{1,0:T(8,128)S(1)} %get-tuple-element.28.refs_4_.refs_1_.refs_2_, ...), custom_call_target="tpu_custom_call" | custom-call | tf_op jit(solution)/shard_map/combine_first/pallas_call | solution.py:436
  21.1 0.1 collective-permute-start.8
  21.2 1.5 %collective-permute-done.8.refs_5_ = bf16[528,256]{1,0:T(8,128)(2,1)S(1)} collective-permute-done((bf16[528,256]{1,0:T(8,128)(2,1)S(1)}, bf16[528,256]{1,0:T(8,128)(2,1)S(1)}, u32[]{:S(2)}, u32[]{:S(2)}) %collective-permute-start.8) | collective-permute-done | bytes 270368 | tf_op jit(solution)/shard_map/ppermute | solution.py:468
  22.7 1.6 %products_second.1 = (bf16[264,128]{1,0:T(8,128)(2,1)S(1)}, bf16[264,128]{1,0:T(8,128)(2,1)S(1)}, bf16[264,128]{1,0:T(8,128)(2,1)S(1)}, bf16[264,128]{1,0:T(8,128)(2,1)S(1)}, bf16[4,128,256]{2,1,0:T(8,128)(2,1)}) custom-call(s32[4,128]{1,0:T(4,128)S(1)} %get-tuple-element.25.refs_0_, bf16[8,4,128,256]{3,2,1,0:T(8,128)(2,1)S(1)} %get-tuple-element.26.refs_1_, ...), custom_call_target="tpu_custom_call" | custom-call | flops 1073741824 | bytes 3145728 | tf_op jit(solution)/shard_map/products_second/pallas_call | solution.py:250
  24.3 1.1 %collective-permute-start.11 = (bf16[264,128]{1,0:T(8,128)(2,1)S(1)}, bf16[264,128]{1,0:T(8,128)(2,1)S(1)}, u32[]{:S(2)}, u32[]{:S(2)}) collective-permute-start(bf16[264,128]{1,0:T(8,128)(2,1)S(1)} %get-tuple-element.43), channel_id=1, source_target_pairs={{0,8},{4,12},{8,0},{12,4},{1,9},{5,13},{9,1},{13,5},{2,10},{6,14},... | collective-permute-start | bytes 202760 | tf_op jit(solution)/shard_map/ppermute | solution.py:284
  25.3 1.5 %collective-permute-start.13 = (bf16[1,256,128]{2,1,0:T(8,128)(2,1)S(1)}, bf16[1,256,128]{2,1,0:T(8,128)(2,1)S(1)}, u32[]{:S(2)}, u32[]{:S(2)}) collective-permute-start(bf16[1,256,128]{2,1,0:T(8,128)(2,1)S(1)} %slice_bitcast_fusion.3), channel_id=1, source_target_pairs={{0,2},{2,0},{1,3},{3,1},{4,6},{6,4},{5,7},{7,5},{8,10},{10,8},{9,1... | collective-permute-start | bytes 196616 | tf_op jit(solution)/shard_map/ppermute | solution.py:276
  26.8 3.4 %collective-permute-start.9 = (bf16[264,128]{1,0:T(8,128)(2,1)S(1)}, bf16[264,128]{1,0:T(8,128)(2,1)S(1)}, u32[]{:S(2)}, u32[]{:S(2)}) collective-permute-start(bf16[264,128]{1,0:T(8,128)(2,1)S(1)} %get-tuple-element.40), channel_id=1, source_target_pairs={{0,12},{4,8},{8,4},{12,0},{1,13},{5,9},{9,5},{13,1},{2,14},{6,10},... | collective-permute-start | bytes 202760 | tf_op jit(solution)/shard_map/ppermute | solution.py:284
  30.2 0.0 collective-permute-start.12
  30.2 1.5 %collective-permute-done.11.refs_1_ = bf16[264,128]{1,0:T(8,128)(2,1)S(1)} collective-permute-done((bf16[264,128]{1,0:T(8,128)(2,1)S(1)}, bf16[264,128]{1,0:T(8,128)(2,1)S(1)}, u32[]{:S(2)}, u32[]{:S(2)}) %collective-permute-start.11) | collective-permute-done | bytes 67616 | tf_op jit(solution)/shard_map/ppermute | solution.py:284
  31.7 1.5 %collective-permute-start.14 = (bf16[1,256,128]{2,1,0:T(8,128)(2,1)S(1)}, bf16[1,256,128]{2,1,0:T(8,128)(2,1)S(1)}, u32[]{:S(2)}, u32[]{:S(2)}) collective-permute-start(bf16[1,256,128]{2,1,0:T(8,128)(2,1)S(1)} %slice_bitcast_fusion.1), channel_id=1, source_target_pairs={{0,2},{2,0},{1,3},{3,1},{4,6},{6,4},{5,7},{7,5},{8,10},{10,8},{9,1... | collective-permute-start | bytes 196616 | tf_op jit(solution)/shard_map/ppermute | solution.py:276
  33.2 1.3 %collective-permute-done.12.refs_2_ = bf16[264,128]{1,0:T(8,128)(2,1)S(1)} collective-permute-done((bf16[264,128]{1,0:T(8,128)(2,1)S(1)}, bf16[264,128]{1,0:T(8,128)(2,1)S(1)}, u32[]{:S(2)}, u32[]{:S(2)}) %collective-permute-start.12) | collective-permute-done | bytes 67616 | tf_op jit(solution)/shard_map/ppermute | solution.py:284
  34.5 0.7 %collective-permute-start.15 = (bf16[1,256,128]{2,1,0:T(8,128)(2,1)S(1)}, bf16[1,256,128]{2,1,0:T(8,128)(2,1)S(1)}, u32[]{:S(2)}, u32[]{:S(2)}) collective-permute-start(bf16[1,256,128]{2,1,0:T(8,128)(2,1)S(1)} %slice_bitcast_fusion), channel_id=1, source_target_pairs={{0,2},{2,0},{1,3},{3,1},{4,6},{6,4},{5,7},{7,5},{8,10},{10,8},{9,1... | collective-permute-start | bytes 196616 | tf_op jit(solution)/shard_map/ppermute | solution.py:276
  35.2 0.0 collective-permute-done.9.refs_3_
  35.2 1.4 %collective-permute-start.10 = (bf16[1,256,128]{2,1,0:T(8,128)(2,1)S(1)}, bf16[1,256,128]{2,1,0:T(8,128)(2,1)S(1)}, u32[]{:S(2)}, u32[]{:S(2)}) collective-permute-start(bf16[1,256,128]{2,1,0:T(8,128)(2,1)S(1)} %slice_bitcast_fusion.2), channel_id=1, source_target_pairs={{0,2},{2,0},{1,3},{3,1},{4,6},{6,4},{5,7},{7,5},{8,10},{10,8},{9,1... | collective-permute-start | bytes 196616 | tf_op jit(solution)/shard_map/ppermute | solution.py:276
  36.6 0.0 collective-permute-done.13.refs_4_
  36.6 0.0 collective-permute-done.14.refs_5_
  36.6 2.2 %collective-permute-done.15.refs_6_ = bf16[1,256,128]{2,1,0:T(8,128)(2,1)S(1)} collective-permute-done((bf16[1,256,128]{2,1,0:T(8,128)(2,1)S(1)}, bf16[1,256,128]{2,1,0:T(8,128)(2,1)S(1)}, u32[]{:S(2)}, u32[]{:S(2)}) %collective-permute-start.15) | collective-permute-done | bytes 65568 | tf_op jit(solution)/shard_map/ppermute | solution.py:276
  38.8 0.5 %combine_second_early.1 = (f32[4,128,256]{2,1,0:T(8,128)S(1)}, f32[8,128]{1,0:T(8,128)S(1)}) custom-call(bf16[264,128]{1,0:T(8,128)(2,1)S(1)} %get-tuple-element.42.refs_0_, bf16[264,128]{1,0:T(8,128)(2,1)S(1)} %collective-permute-done.11.refs_1_, bf16[264,128]{1,0:T(8,128)(2,1)S(1)} %collective-permute-done.12.refs_2_, ...), custom_call_target="tpu_custom_call" | custom-call | flops 1000000000 | tf_op jit(solution)/shard_map/combine_second_early/pallas_call | solution.py:436
  39.2 0.3 collective-permute-done.10.refs_0_
  39.5 0.8 %combine_second.1 = bf16[4,128,256]{2,1,0:T(8,128)(2,1)} custom-call(bf16[1,256,128]{2,1,0:T(8,128)(2,1)S(1)} %collective-permute-done.10.refs_0_, f32[8,128]{1,0:T(8,128)S(1)} %get-tuple-element.41.refs_7_.refs_1_, s32[8,128]{1,0:T(8,128)S(1)} %get-tuple-element.28.refs_4_.refs_1_.refs_2_, f32[4,128,256]{2,1,0:T(8,128)S(1)} %get-tuple-element.46.refs_3_, ...), custom_call_target="tpu_custom_call" | custom-call | tf_op jit(solution)/shard_map/combine_second/pallas_call | solution.py:436
  (5 shorter events, 0.0 us)
Async XLA Ops:
  0.6 2.5 %copy-start = (bf16[8,256,256]{2,1,0:T(8,128)(2,1)S(1)}, bf16[8,256,256]{2,1,0:T(8,128)(2,1)}, u32[]{:S(2)}) copy-start(bf16[8,256,256]{2,1,0:T(8,128)(2,1)} %refs_2_.3) | copy-start | bytes 3145732
  0.6 2.5 %collective-permute-start = (bf16[4,128,256]{2,1,0:T(8,128)(2,1)}, bf16[4,128,256]{2,1,0:T(8,128)(2,1)S(1)}, u32[]{:S(2)}, u32[]{:S(2)}) collective-permute-start(bf16[4,128,256]{2,1,0:T(8,128)(2,1)} %psi_hbm.1), channel_id=1, source_target_pairs={{1,0},{0,1},{3,2},{2,3},{5,4},{4,5},{7,6},{6,7},{9,8},{8,9},{11,10... | collective-permute-start | bytes 786440 | tf_op jit(solution)/shard_map/ppermute | solution.py:468
  1.2 1.9 %collective-permute-start.1 = (f32[4,128]{1,0:T(4,128)}, f32[4,128]{1,0:T(4,128)S(1)}, u32[]{:S(2)}, u32[]{:S(2)}) collective-permute-start(f32[4,128]{1,0:T(4,128)} %energy_hbm.1), channel_id=1, source_target_pairs={{1,0},{0,1},{3,2},{2,3},{5,4},{4,5},{7,6},{6,7},{9,8},{8,9},{11,10... | collective-permute-start | bytes 6152 | tf_op jit(solution)/shard_map/ppermute | solution.py:468
  4.7 8.5 %collective-permute-start.5 = (bf16[264,128]{1,0:T(8,128)(2,1)S(1)}, bf16[264,128]{1,0:T(8,128)(2,1)S(1)}, u32[]{:S(2)}, u32[]{:S(2)}) collective-permute-start(bf16[264,128]{1,0:T(8,128)(2,1)S(1)} %get-tuple-element.33), channel_id=1, source_target_pairs={{0,4},{4,8},{8,12},{12,0},{1,5},{5,9},{9,13},{13,1},{2,6},{6,10},{... | collective-permute-start | bytes 202760 | tf_op jit(solution)/shard_map/ppermute | solution.py:284
  7.8 7.4 %collective-permute-start.2 = (bf16[264,128]{1,0:T(8,128)(2,1)S(1)}, bf16[264,128]{1,0:T(8,128)(2,1)S(1)}, u32[]{:S(2)}, u32[]{:S(2)}) collective-permute-start(bf16[264,128]{1,0:T(8,128)(2,1)S(1)} %get-tuple-element.30), channel_id=1, source_target_pairs={{0,8},{4,12},{8,0},{12,4},{1,9},{5,13},{9,1},{13,5},{2,10},{6,14},... | collective-permute-start | bytes 202760 | tf_op jit(solution)/shard_map/ppermute | solution.py:284
  10.4 5.0 %collective-permute-start.3 = (bf16[264,128]{1,0:T(8,128)(2,1)S(1)}, bf16[264,128]{1,0:T(8,128)(2,1)S(1)}, u32[]{:S(2)}, u32[]{:S(2)}) collective-permute-start(bf16[264,128]{1,0:T(8,128)(2,1)S(1)} %get-tuple-element.31), channel_id=1, source_target_pairs={{0,12},{4,0},{8,4},{12,8},{1,13},{5,1},{9,5},{13,9},{2,14},{6,2},{... | collective-permute-start | bytes 202760 | tf_op jit(solution)/shard_map/ppermute | solution.py:284
  11.7 5.3 %collective-permute-start.6 = (bf16[1,264,128]{2,1,0:T(8,128)(2,1)S(1)}, bf16[1,264,128]{2,1,0:T(8,128)(2,1)S(1)}, u32[]{:S(2)}, u32[]{:S(2)}) collective-permute-start(bf16[1,264,128]{2,1,0:T(8,128)(2,1)S(1)} %bitcast.15), channel_id=1, source_target_pairs={{0,2},{2,0},{1,3},{3,1},{4,6},{6,4},{5,7},{7,5},{8,10},{10,8},{9,1... | collective-permute-start | bytes 202760 | tf_op jit(solution)/shard_map/ppermute | solution.py:276
  13.2 4.3 %collective-permute-start.7 = (bf16[1,264,128]{2,1,0:T(8,128)(2,1)S(1)}, bf16[1,264,128]{2,1,0:T(8,128)(2,1)S(1)}, u32[]{:S(2)}, u32[]{:S(2)}) collective-permute-start(bf16[1,264,128]{2,1,0:T(8,128)(2,1)S(1)} %bitcast.16), channel_id=1, source_target_pairs={{0,2},{2,0},{1,3},{3,1},{4,6},{6,4},{5,7},{7,5},{8,10},{10,8},{9,1... | collective-permute-start | bytes 202760 | tf_op jit(solution)/shard_map/ppermute | solution.py:276
  15.4 5.2 %collective-permute-start.4 = (bf16[2,264,128]{2,1,0:T(8,128)(2,1)S(1)}, bf16[2,264,128]{2,1,0:T(8,128)(2,1)S(1)}, u32[]{:S(2)}, u32[]{:S(2)}) collective-permute-start(bf16[2,264,128]{2,1,0:T(8,128)(2,1)S(1)} %pad_maximum_fusion), channel_id=1, source_target_pairs={{0,2},{2,0},{1,3},{3,1},{4,6},{6,4},{5,7},{7,5},{8,10},{10,8},{9,1... | collective-permute-start | bytes 405512 | tf_op jit(solution)/shard_map/ppermute | solution.py:276
  21.1 1.6 %collective-permute-start.8 = (bf16[528,256]{1,0:T(8,128)(2,1)S(1)}, bf16[528,256]{1,0:T(8,128)(2,1)S(1)}, u32[]{:S(2)}, u32[]{:S(2)}) collective-permute-start(bf16[528,256]{1,0:T(8,128)(2,1)S(1)} %get-tuple-element.38.refs_4_.refs_8_), channel_id=1, source_target_pairs={{1,0},{0,1},{3,2},{2,3},{5,4},{4,5},{7,6},{6,7},{9,8},{8,9},{11,10... | collective-permute-start | bytes 811016 | tf_op jit(solution)/shard_map/ppermute | solution.py:468
  24.3 7.4 %collective-permute-start.11 = (bf16[264,128]{1,0:T(8,128)(2,1)S(1)}, bf16[264,128]{1,0:T(8,128)(2,1)S(1)}, u32[]{:S(2)}, u32[]{:S(2)}) collective-permute-start(bf16[264,128]{1,0:T(8,128)(2,1)S(1)} %get-tuple-element.43), channel_id=1, source_target_pairs={{0,8},{4,12},{8,0},{12,4},{1,9},{5,13},{9,1},{13,5},{2,10},{6,14},... | collective-permute-start | bytes 202760 | tf_op jit(solution)/shard_map/ppermute | solution.py:284
  25.3 11.2 %collective-permute-start.13 = (bf16[1,256,128]{2,1,0:T(8,128)(2,1)S(1)}, bf16[1,256,128]{2,1,0:T(8,128)(2,1)S(1)}, u32[]{:S(2)}, u32[]{:S(2)}) collective-permute-start(bf16[1,256,128]{2,1,0:T(8,128)(2,1)S(1)} %slice_bitcast_fusion.3), channel_id=1, source_target_pairs={{0,2},{2,0},{1,3},{3,1},{4,6},{6,4},{5,7},{7,5},{8,10},{10,8},{9,1... | collective-permute-start | bytes 196616 | tf_op jit(solution)/shard_map/ppermute | solution.py:276
  26.8 8.4 %collective-permute-start.9 = (bf16[264,128]{1,0:T(8,128)(2,1)S(1)}, bf16[264,128]{1,0:T(8,128)(2,1)S(1)}, u32[]{:S(2)}, u32[]{:S(2)}) collective-permute-start(bf16[264,128]{1,0:T(8,128)(2,1)S(1)} %get-tuple-element.40), channel_id=1, source_target_pairs={{0,12},{4,8},{8,4},{12,0},{1,13},{5,9},{9,5},{13,1},{2,14},{6,10},... | collective-permute-start | bytes 202760 | tf_op jit(solution)/shard_map/ppermute | solution.py:284
  30.2 4.3 %collective-permute-start.12 = (bf16[264,128]{1,0:T(8,128)(2,1)S(1)}, bf16[264,128]{1,0:T(8,128)(2,1)S(1)}, u32[]{:S(2)}, u32[]{:S(2)}) collective-permute-start(bf16[264,128]{1,0:T(8,128)(2,1)S(1)} %get-tuple-element.44), channel_id=1, source_target_pairs={{0,4},{4,0},{8,12},{12,8},{1,5},{5,1},{9,13},{13,9},{2,6},{6,2},{1... | collective-permute-start | bytes 202760 | tf_op jit(solution)/shard_map/ppermute | solution.py:284
  31.7 4.9 %collective-permute-start.14 = (bf16[1,256,128]{2,1,0:T(8,128)(2,1)S(1)}, bf16[1,256,128]{2,1,0:T(8,128)(2,1)S(1)}, u32[]{:S(2)}, u32[]{:S(2)}) collective-permute-start(bf16[1,256,128]{2,1,0:T(8,128)(2,1)S(1)} %slice_bitcast_fusion.1), channel_id=1, source_target_pairs={{0,2},{2,0},{1,3},{3,1},{4,6},{6,4},{5,7},{7,5},{8,10},{10,8},{9,1... | collective-permute-start | bytes 196616 | tf_op jit(solution)/shard_map/ppermute | solution.py:276
  34.5 4.3 %collective-permute-start.15 = (bf16[1,256,128]{2,1,0:T(8,128)(2,1)S(1)}, bf16[1,256,128]{2,1,0:T(8,128)(2,1)S(1)}, u32[]{:S(2)}, u32[]{:S(2)}) collective-permute-start(bf16[1,256,128]{2,1,0:T(8,128)(2,1)S(1)} %slice_bitcast_fusion), channel_id=1, source_target_pairs={{0,2},{2,0},{1,3},{3,1},{4,6},{6,4},{5,7},{7,5},{8,10},{10,8},{9,1... | collective-permute-start | bytes 196616 | tf_op jit(solution)/shard_map/ppermute | solution.py:276
  35.2 4.3 %collective-permute-start.10 = (bf16[1,256,128]{2,1,0:T(8,128)(2,1)S(1)}, bf16[1,256,128]{2,1,0:T(8,128)(2,1)S(1)}, u32[]{:S(2)}, u32[]{:S(2)}) collective-permute-start(bf16[1,256,128]{2,1,0:T(8,128)(2,1)S(1)} %slice_bitcast_fusion.2), channel_id=1, source_target_pairs={{0,2},{2,0},{1,3},{3,1},{4,6},{6,4},{5,7},{7,5},{8,10},{10,8},{9,1... | collective-permute-start | bytes 196616 | tf_op jit(solution)/shard_map/ppermute | solution.py:276

commit v8 on v7

--- a/solution.py
+++ b/solution.py
@@ -282,9 +282,10 @@
         reach = (lambda i: i ^ step) if paired else (lambda i: (i + step) % sec_count)
         turn = [(i, reach(i)) for i in range(sec_count)]
         arrived[step] = lax.ppermute(packets[step], "sec", turn)
-    crossed = [
-        over_op(jnp.stack([arrived[step][:bare or None] for step in group])) for group in groups
-    ]
+    crossed = []
+    for group in groups:
+        rows = bare if bare and group != [0] else None
+        crossed.append(over_op(jnp.stack([arrived[step][:rows] for step in group])))
     return [arrived[step] for step in [0, *order]] + sum(crossed[:-1], []), crossed[-1]
 
 

time: 40.5 us -> 40.3 us (level)
    ppermute x6, waiting for transfers between devices: 4.15 us -> 3.14 us  [exchange(): arrived[step] = lax.ppermute(packets[step], 'sec', turn)]
    ppermute x7, waiting for transfers between devices: 5.78 us -> 6.53 us  [exchange(): lax.ppermute(packet, 'op', turn)]
  transfers between devices with their start and end apart: 16 -> 16, of which waited for: 9 -> 10; matrix products, arithmetic and copies ran while one was open for 0% -> 0% of each run, Pallas kernels for 7% -> 7%
where the time goes in v8:
time: 40.3 us; the launch traced here: 40.1 us
  starting transfers between devices  21 us (52%)
  waiting for transfers between devices  11.2 us (28%)
  Pallas kernels  7.14 us (18%)
  between operations  0.72 us (2%)
    ppermute x6, starting transfers between devices, exchange(): arrived[step] = lax.ppermute(packets[step], 'sec', turn)  11.4 us
    ppermute x7, starting transfers between devices, exchange(): lax.ppermute(packet, 'op', turn)  8.92 us
    ppermute x7, waiting for transfers between devices, exchange(): lax.ppermute(packet, 'op', turn)  6.53 us
    pallas_call x2, Pallas kernels, sigma_packets(): pl.pallas_call(functools.partial(product_kernel, is_first, split, paired,...  3.17 us
    ppermute x6, waiting for transfers between devices, exchange(): arrived[step] = lax.ppermute(packets[step], 'sec', turn)  3.14 us
    pallas_call x4, Pallas kernels, call(): pl.pallas_call(kernel, out_shape=outs, in_specs=[whole(pltpu.VMEM)] * len...  2.13 us
    pallas_call x1, Pallas kernels, body(): pl.pallas_call(load_kernel, out_shape=[vec_bf16, jax.ShapeDtypeStruct(lef...  1.84 us
    ppermute x3, waiting for transfers between devices, from_others(): arrays.append(lax.ppermute(array, 'rep', turn))  1.54 us
  transfers between devices with their start and end apart: 16, of which 10 were waited for; matrix products, arithmetic and copies ran while one was open for 0% of the time, Pallas kernels for 7%

profile of v8, /device:TPU:0, one launch (start us, length us, event | category | flops | bytes accessed | tf_op | source)
XLA Modules:
  0.0 40.1 jit_solution(11922595574480921036)
XLA Ops:
  0.6 0.0 copy-start
  0.6 0.5 %collective-permute-start = (bf16[4,128,256]{2,1,0:T(8,128)(2,1)}, bf16[4,128,256]{2,1,0:T(8,128)(2,1)S(1)}, u32[]{:S(2)}, u32[]{:S(2)}) collective-permute-start(bf16[4,128,256]{2,1,0:T(8,128)(2,1)} %psi_hbm.1), channel_id=1, source_target_pairs={{1,0},{0,1},{3,2},{2,3},{5,4},{4,5},{7,6},{6,7},{9,8},{8,9},{11,10... | collective-permute-start | bytes 786440 | tf_op jit(solution)/shard_map/ppermute | solution.py:469
  1.2 0.1 collective-permute-start.1
  1.2 1.8 %load.1 = (bf16[4,128,256]{2,1,0:T(8,128)(2,1)S(1)}, bf16[8,4,128,256]{3,2,1,0:T(8,128)(2,1)S(1)}, s32[4,128]{1,0:T(4,128)S(1)}, s32[8,128]{1,0:T(8,128)S(1)}, f...) custom-call(bf16[4,128,256]{2,1,0:T(8,128)(2,1)} %psi_hbm.1, bf16[8,4,128,256]{3,2,1,0:T(8,128)(2,1)} %left_hbm.1, ...), custom_call_target="tpu_custom_call" | custom-call | tf_op jit(solution)/shard_map/load/pallas_call | solution.py:474
  3.1 0.0 collective-permute-done.1.refs_7_
  3.1 0.0 collective-permute-done.refs_6_
  3.1 0.0 copy-done
  3.1 1.6 %products_first.1 = (bf16[264,128]{1,0:T(8,128)(2,1)S(1)}, bf16[264,128]{1,0:T(8,128)(2,1)S(1)}, bf16[264,128]{1,0:T(8,128)(2,1)S(1)}, bf16[264,128]{1,0:T(8,128)(2,1)S(1)}) custom-call(s32[4,128]{1,0:T(4,128)S(1)} %get-tuple-element.25.refs_0_, bf16[8,4,128,256]{3,2,1,0:T(8,128)(2,1)S(1)} %get-tuple-element.26.refs_1_, bf16[8,256,256]{2,1,0:T(8,128)(2,1)S(1)} %copy-done, ...), custom_call_target="tpu_custom_call" | custom-call | flops 1073741824 | bytes 3145728 | tf_op jit(solution)/shard_map/products_first/pallas_call | solution.py:250
  4.7 3.1 %collective-permute-start.5 = (bf16[264,128]{1,0:T(8,128)(2,1)S(1)}, bf16[264,128]{1,0:T(8,128)(2,1)S(1)}, u32[]{:S(2)}, u32[]{:S(2)}) collective-permute-start(bf16[264,128]{1,0:T(8,128)(2,1)S(1)} %get-tuple-element.33), channel_id=1, source_target_pairs={{0,4},{4,8},{8,12},{12,0},{1,5},{5,9},{9,13},{13,1},{2,6},{6,10},{... | collective-permute-start | bytes 202760 | tf_op jit(solution)/shard_map/ppermute | solution.py:284
  7.8 2.6 %collective-permute-start.2 = (bf16[264,128]{1,0:T(8,128)(2,1)S(1)}, bf16[264,128]{1,0:T(8,128)(2,1)S(1)}, u32[]{:S(2)}, u32[]{:S(2)}) collective-permute-start(bf16[264,128]{1,0:T(8,128)(2,1)S(1)} %get-tuple-element.30), channel_id=1, source_target_pairs={{0,8},{4,12},{8,0},{12,4},{1,9},{5,13},{9,1},{13,5},{2,10},{6,14},... | collective-permute-start | bytes 202760 | tf_op jit(solution)/shard_map/ppermute | solution.py:284
  10.4 1.3 %collective-permute-start.3 = (bf16[264,128]{1,0:T(8,128)(2,1)S(1)}, bf16[264,128]{1,0:T(8,128)(2,1)S(1)}, u32[]{:S(2)}, u32[]{:S(2)}) collective-permute-start(bf16[264,128]{1,0:T(8,128)(2,1)S(1)} %get-tuple-element.31), channel_id=1, source_target_pairs={{0,12},{4,0},{8,4},{12,8},{1,13},{5,1},{9,5},{13,9},{2,14},{6,2},{... | collective-permute-start | bytes 202760 | tf_op jit(solution)/shard_map/ppermute | solution.py:284
  11.7 1.5 %collective-permute-start.6 = (bf16[1,264,128]{2,1,0:T(8,128)(2,1)S(1)}, bf16[1,264,128]{2,1,0:T(8,128)(2,1)S(1)}, u32[]{:S(2)}, u32[]{:S(2)}) collective-permute-start(bf16[1,264,128]{2,1,0:T(8,128)(2,1)S(1)} %bitcast.15), channel_id=1, source_target_pairs={{0,2},{2,0},{1,3},{3,1},{4,6},{6,4},{5,7},{7,5},{8,10},{10,8},{9,1... | collective-permute-start | bytes 202760 | tf_op jit(solution)/shard_map/ppermute | solution.py:276
  13.2 0.0 collective-permute-done.5.refs_1_
  13.2 0.8 %collective-permute-start.7 = (bf16[1,264,128]{2,1,0:T(8,128)(2,1)S(1)}, bf16[1,264,128]{2,1,0:T(8,128)(2,1)S(1)}, u32[]{:S(2)}, u32[]{:S(2)}) collective-permute-start(bf16[1,264,128]{2,1,0:T(8,128)(2,1)S(1)} %bitcast.16), channel_id=1, source_target_pairs={{0,2},{2,0},{1,3},{3,1},{4,6},{6,4},{5,7},{7,5},{8,10},{10,8},{9,1... | collective-permute-start | bytes 202760 | tf_op jit(solution)/shard_map/ppermute | solution.py:276
  14.1 1.1 %collective-permute-done.2.refs_2_ = bf16[264,128]{1,0:T(8,128)(2,1)S(1)} collective-permute-done((bf16[264,128]{1,0:T(8,128)(2,1)S(1)}, bf16[264,128]{1,0:T(8,128)(2,1)S(1)}, u32[]{:S(2)}, u32[]{:S(2)}) %collective-permute-start.2) | collective-permute-done | bytes 67616 | tf_op jit(solution)/shard_map/ppermute | solution.py:284
  15.2 0.2 collective-permute-done.3.refs_3_
  15.4 1.5 %collective-permute-start.4 = (bf16[2,264,128]{2,1,0:T(8,128)(2,1)S(1)}, bf16[2,264,128]{2,1,0:T(8,128)(2,1)S(1)}, u32[]{:S(2)}, u32[]{:S(2)}) collective-permute-start(bf16[2,264,128]{2,1,0:T(8,128)(2,1)S(1)} %pad_maximum_fusion), channel_id=1, source_target_pairs={{0,2},{2,0},{1,3},{3,1},{4,6},{6,4},{5,7},{7,5},{8,10},{10,8},{9,1... | collective-permute-start | bytes 405512 | tf_op jit(solution)/shard_map/ppermute | solution.py:276
  17.0 0.0 collective-permute-done.6.refs_4_
  17.0 0.5 %collective-permute-done.7.refs_5_ = bf16[1,264,128]{2,1,0:T(8,128)(2,1)S(1)} collective-permute-done((bf16[1,264,128]{2,1,0:T(8,128)(2,1)S(1)}, bf16[1,264,128]{2,1,0:T(8,128)(2,1)S(1)}, u32[]{:S(2)}, u32[]{:S(2)}) %collective-permute-start.7) | collective-permute-done | bytes 67616 | tf_op jit(solution)/shard_map/ppermute | solution.py:276
  17.5 0.4 combine_first_early.1
  17.9 2.8 %collective-permute-done.4.refs_0_ = bf16[2,264,128]{2,1,0:T(8,128)(2,1)S(1)} collective-permute-done((bf16[2,264,128]{2,1,0:T(8,128)(2,1)S(1)}, bf16[2,264,128]{2,1,0:T(8,128)(2,1)S(1)}, u32[]{:S(2)}, u32[]{:S(2)}) %collective-permute-start.4) | collective-permute-done | bytes 135200 | tf_op jit(solution)/shard_map/ppermute | solution.py:276
  20.7 0.4 %combine_first.1 = (bf16[4,128,256]{2,1,0:T(8,128)(2,1)S(1)}, f32[4,128,256]{2,1,0:T(8,128)S(1)}, bf16[528,256]{1,0:T(8,128)(2,1)S(1)}, f32[8,128]{1,0:T(8,128)S(1)}) custom-call(bf16[2,264,128]{2,1,0:T(8,128)(2,1)S(1)} %collective-permute-done.4.refs_0_, s32[8,128]{1,0:T(8,128)S(1)} %get-tuple-element.28.refs_4_.refs_1_.refs_2_, ...), custom_call_target="tpu_custom_call" | custom-call | tf_op jit(solution)/shard_map/combine_first/pallas_call | solution.py:437
  21.1 0.1 collective-permute-start.8
  21.2 1.5 %collective-permute-done.8.refs_5_ = bf16[528,256]{1,0:T(8,128)(2,1)S(1)} collective-permute-done((bf16[528,256]{1,0:T(8,128)(2,1)S(1)}, bf16[528,256]{1,0:T(8,128)(2,1)S(1)}, u32[]{:S(2)}, u32[]{:S(2)}) %collective-permute-start.8) | collective-permute-done | bytes 270368 | tf_op jit(solution)/shard_map/ppermute | solution.py:469
  22.7 1.6 %products_second.1 = (bf16[264,128]{1,0:T(8,128)(2,1)S(1)}, bf16[264,128]{1,0:T(8,128)(2,1)S(1)}, bf16[264,128]{1,0:T(8,128)(2,1)S(1)}, bf16[264,128]{1,0:T(8,128)(2,1)S(1)}, bf16[4,128,256]{2,1,0:T(8,128)(2,1)}) custom-call(s32[4,128]{1,0:T(4,128)S(1)} %get-tuple-element.25.refs_0_, bf16[8,4,128,256]{3,2,1,0:T(8,128)(2,1)S(1)} %get-tuple-element.26.refs_1_, ...), custom_call_target="tpu_custom_call" | custom-call | flops 1073741824 | bytes 3145728 | tf_op jit(solution)/shard_map/products_second/pallas_call | solution.py:250
  24.3 1.1 %collective-permute-start.11 = (bf16[264,128]{1,0:T(8,128)(2,1)S(1)}, bf16[264,128]{1,0:T(8,128)(2,1)S(1)}, u32[]{:S(2)}, u32[]{:S(2)}) collective-permute-start(bf16[264,128]{1,0:T(8,128)(2,1)S(1)} %get-tuple-element.43), channel_id=1, source_target_pairs={{0,8},{4,12},{8,0},{12,4},{1,9},{5,13},{9,1},{13,5},{2,10},{6,14},... | collective-permute-start | bytes 202760 | tf_op jit(solution)/shard_map/ppermute | solution.py:284
  25.3 3.4 %collective-permute-start.9 = (bf16[264,128]{1,0:T(8,128)(2,1)S(1)}, bf16[264,128]{1,0:T(8,128)(2,1)S(1)}, u32[]{:S(2)}, u32[]{:S(2)}) collective-permute-start(bf16[264,128]{1,0:T(8,128)(2,1)S(1)} %get-tuple-element.40), channel_id=1, source_target_pairs={{0,12},{4,8},{8,4},{12,0},{1,13},{5,9},{9,5},{13,1},{2,14},{6,10},... | collective-permute-start | bytes 202760 | tf_op jit(solution)/shard_map/ppermute | solution.py:284
  28.7 0.0 collective-permute-start.12
  28.7 1.5 %collective-permute-start.13 = (bf16[1,264,128]{2,1,0:T(8,128)(2,1)S(1)}, bf16[1,264,128]{2,1,0:T(8,128)(2,1)S(1)}, u32[]{:S(2)}, u32[]{:S(2)}) collective-permute-start(bf16[1,264,128]{2,1,0:T(8,128)(2,1)S(1)} %bitcast.14), channel_id=1, source_target_pairs={{0,2},{2,0},{1,3},{3,1},{4,6},{6,4},{5,7},{7,5},{8,10},{10,8},{9,1... | collective-permute-start | bytes 202760 | tf_op jit(solution)/shard_map/ppermute | solution.py:276
  30.2 1.7 %collective-permute-done.11.refs_1_ = bf16[264,128]{1,0:T(8,128)(2,1)S(1)} collective-permute-done((bf16[264,128]{1,0:T(8,128)(2,1)S(1)}, bf16[264,128]{1,0:T(8,128)(2,1)S(1)}, u32[]{:S(2)}, u32[]{:S(2)}) %collective-permute-start.11) | collective-permute-done | bytes 67616 | tf_op jit(solution)/shard_map/ppermute | solution.py:284
  31.9 1.5 %collective-permute-start.14 = (bf16[1,256,128]{2,1,0:T(8,128)(2,1)S(1)}, bf16[1,256,128]{2,1,0:T(8,128)(2,1)S(1)}, u32[]{:S(2)}, u32[]{:S(2)}) collective-permute-start(bf16[1,256,128]{2,1,0:T(8,128)(2,1)S(1)} %slice_bitcast_fusion.1), channel_id=1, source_target_pairs={{0,2},{2,0},{1,3},{3,1},{4,6},{6,4},{5,7},{7,5},{8,10},{10,8},{9,1... | collective-permute-start | bytes 196616 | tf_op jit(solution)/shard_map/ppermute | solution.py:276
  33.4 0.1 collective-permute-done.12.refs_2_
  33.5 1.5 %collective-permute-start.15 = (bf16[1,256,128]{2,1,0:T(8,128)(2,1)S(1)}, bf16[1,256,128]{2,1,0:T(8,128)(2,1)S(1)}, u32[]{:S(2)}, u32[]{:S(2)}) collective-permute-start(bf16[1,256,128]{2,1,0:T(8,128)(2,1)S(1)} %slice_bitcast_fusion), channel_id=1, source_target_pairs={{0,2},{2,0},{1,3},{3,1},{4,6},{6,4},{5,7},{7,5},{8,10},{10,8},{9,1... | collective-permute-start | bytes 196616 | tf_op jit(solution)/shard_map/ppermute | solution.py:276
  34.9 0.0 collective-permute-done.9.refs_3_
  34.9 0.6 %collective-permute-start.10 = (bf16[1,256,128]{2,1,0:T(8,128)(2,1)S(1)}, bf16[1,256,128]{2,1,0:T(8,128)(2,1)S(1)}, u32[]{:S(2)}, u32[]{:S(2)}) collective-permute-start(bf16[1,256,128]{2,1,0:T(8,128)(2,1)S(1)} %slice_bitcast_fusion.2), channel_id=1, source_target_pairs={{0,2},{2,0},{1,3},{3,1},{4,6},{6,4},{5,7},{7,5},{8,10},{10,8},{9,1... | collective-permute-start | bytes 196616 | tf_op jit(solution)/shard_map/ppermute | solution.py:276
  35.6 0.0 collective-permute-done.13.refs_4_
  35.6 1.0 %collective-permute-done.14.refs_5_ = bf16[1,256,128]{2,1,0:T(8,128)(2,1)S(1)} collective-permute-done((bf16[1,256,128]{2,1,0:T(8,128)(2,1)S(1)}, bf16[1,256,128]{2,1,0:T(8,128)(2,1)S(1)}, u32[]{:S(2)}, u32[]{:S(2)}) %collective-permute-start.14) | collective-permute-done | bytes 65568 | tf_op jit(solution)/shard_map/ppermute | solution.py:276
  36.6 1.2 %collective-permute-done.15.refs_6_ = bf16[1,256,128]{2,1,0:T(8,128)(2,1)S(1)} collective-permute-done((bf16[1,256,128]{2,1,0:T(8,128)(2,1)S(1)}, bf16[1,256,128]{2,1,0:T(8,128)(2,1)S(1)}, u32[]{:S(2)}, u32[]{:S(2)}) %collective-permute-start.15) | collective-permute-done | bytes 65568 | tf_op jit(solution)/shard_map/ppermute | solution.py:276
  37.8 0.5 %combine_second_early.1 = (f32[4,128,256]{2,1,0:T(8,128)S(1)}, f32[8,128]{1,0:T(8,128)S(1)}) custom-call(bf16[264,128]{1,0:T(8,128)(2,1)S(1)} %get-tuple-element.42.refs_0_, bf16[264,128]{1,0:T(8,128)(2,1)S(1)} %collective-permute-done.11.refs_1_, bf16[264,128]{1,0:T(8,128)(2,1)S(1)} %collective-permute-done.12.refs_2_, ...), custom_call_target="tpu_custom_call" | custom-call | flops 1000000000 | tf_op jit(solution)/shard_map/combine_second_early/pallas_call | solution.py:437
  38.3 1.0 %collective-permute-done.10.refs_0_ = bf16[1,256,128]{2,1,0:T(8,128)(2,1)S(1)} collective-permute-done((bf16[1,256,128]{2,1,0:T(8,128)(2,1)S(1)}, bf16[1,256,128]{2,1,0:T(8,128)(2,1)S(1)}, u32[]{:S(2)}, u32[]{:S(2)}) %collective-permute-start.10) | collective-permute-done | bytes 65568 | tf_op jit(solution)/shard_map/ppermute | solution.py:276
  39.3 0.8 %combine_second.1 = bf16[4,128,256]{2,1,0:T(8,128)(2,1)} custom-call(bf16[1,256,128]{2,1,0:T(8,128)(2,1)S(1)} %collective-permute-done.10.refs_0_, f32[8,128]{1,0:T(8,128)S(1)} %get-tuple-element.41.refs_7_.refs_1_, s32[8,128]{1,0:T(8,128)S(1)} %get-tuple-element.28.refs_4_.refs_1_.refs_2_, f32[4,128,256]{2,1,0:T(8,128)S(1)} %get-tuple-element.46.refs_3_, ...), custom_call_target="tpu_custom_call" | custom-call | tf_op jit(solution)/shard_map/combine_second/pallas_call | solution.py:437
  (4 shorter events, 0.0 us)
Async XLA Ops:
  0.6 2.5 %copy-start = (bf16[8,256,256]{2,1,0:T(8,128)(2,1)S(1)}, bf16[8,256,256]{2,1,0:T(8,128)(2,1)}, u32[]{:S(2)}) copy-start(bf16[8,256,256]{2,1,0:T(8,128)(2,1)} %refs_2_.3) | copy-start | bytes 3145732
  0.6 2.5 %collective-permute-start = (bf16[4,128,256]{2,1,0:T(8,128)(2,1)}, bf16[4,128,256]{2,1,0:T(8,128)(2,1)S(1)}, u32[]{:S(2)}, u32[]{:S(2)}) collective-permute-start(bf16[4,128,256]{2,1,0:T(8,128)(2,1)} %psi_hbm.1), channel_id=1, source_target_pairs={{1,0},{0,1},{3,2},{2,3},{5,4},{4,5},{7,6},{6,7},{9,8},{8,9},{11,10... | collective-permute-start | bytes 786440 | tf_op jit(solution)/shard_map/ppermute | solution.py:469
  1.2 1.9 %collective-permute-start.1 = (f32[4,128]{1,0:T(4,128)}, f32[4,128]{1,0:T(4,128)S(1)}, u32[]{:S(2)}, u32[]{:S(2)}) collective-permute-start(f32[4,128]{1,0:T(4,128)} %energy_hbm.1), channel_id=1, source_target_pairs={{1,0},{0,1},{3,2},{2,3},{5,4},{4,5},{7,6},{6,7},{9,8},{8,9},{11,10... | collective-permute-start | bytes 6152 | tf_op jit(solution)/shard_map/ppermute | solution.py:469
  4.7 8.5 %collective-permute-start.5 = (bf16[264,128]{1,0:T(8,128)(2,1)S(1)}, bf16[264,128]{1,0:T(8,128)(2,1)S(1)}, u32[]{:S(2)}, u32[]{:S(2)}) collective-permute-start(bf16[264,128]{1,0:T(8,128)(2,1)S(1)} %get-tuple-element.33), channel_id=1, source_target_pairs={{0,4},{4,8},{8,12},{12,0},{1,5},{5,9},{9,13},{13,1},{2,6},{6,10},{... | collective-permute-start | bytes 202760 | tf_op jit(solution)/shard_map/ppermute | solution.py:284
  7.8 7.4 %collective-permute-start.2 = (bf16[264,128]{1,0:T(8,128)(2,1)S(1)}, bf16[264,128]{1,0:T(8,128)(2,1)S(1)}, u32[]{:S(2)}, u32[]{:S(2)}) collective-permute-start(bf16[264,128]{1,0:T(8,128)(2,1)S(1)} %get-tuple-element.30), channel_id=1, source_target_pairs={{0,8},{4,12},{8,0},{12,4},{1,9},{5,13},{9,1},{13,5},{2,10},{6,14},... | collective-permute-start | bytes 202760 | tf_op jit(solution)/shard_map/ppermute | solution.py:284
  10.4 5.0 %collective-permute-start.3 = (bf16[264,128]{1,0:T(8,128)(2,1)S(1)}, bf16[264,128]{1,0:T(8,128)(2,1)S(1)}, u32[]{:S(2)}, u32[]{:S(2)}) collective-permute-start(bf16[264,128]{1,0:T(8,128)(2,1)S(1)} %get-tuple-element.31), channel_id=1, source_target_pairs={{0,12},{4,0},{8,4},{12,8},{1,13},{5,1},{9,5},{13,9},{2,14},{6,2},{... | collective-permute-start | bytes 202760 | tf_op jit(solution)/shard_map/ppermute | solution.py:284
  11.7 5.3 %collective-permute-start.6 = (bf16[1,264,128]{2,1,0:T(8,128)(2,1)S(1)}, bf16[1,264,128]{2,1,0:T(8,128)(2,1)S(1)}, u32[]{:S(2)}, u32[]{:S(2)}) collective-permute-start(bf16[1,264,128]{2,1,0:T(8,128)(2,1)S(1)} %bitcast.15), channel_id=1, source_target_pairs={{0,2},{2,0},{1,3},{3,1},{4,6},{6,4},{5,7},{7,5},{8,10},{10,8},{9,1... | collective-permute-start | bytes 202760 | tf_op jit(solution)/shard_map/ppermute | solution.py:276
  13.2 4.3 %collective-permute-start.7 = (bf16[1,264,128]{2,1,0:T(8,128)(2,1)S(1)}, bf16[1,264,128]{2,1,0:T(8,128)(2,1)S(1)}, u32[]{:S(2)}, u32[]{:S(2)}) collective-permute-start(bf16[1,264,128]{2,1,0:T(8,128)(2,1)S(1)} %bitcast.16), channel_id=1, source_target_pairs={{0,2},{2,0},{1,3},{3,1},{4,6},{6,4},{5,7},{7,5},{8,10},{10,8},{9,1... | collective-permute-start | bytes 202760 | tf_op jit(solution)/shard_map/ppermute | solution.py:276
  15.4 5.2 %collective-permute-start.4 = (bf16[2,264,128]{2,1,0:T(8,128)(2,1)S(1)}, bf16[2,264,128]{2,1,0:T(8,128)(2,1)S(1)}, u32[]{:S(2)}, u32[]{:S(2)}) collective-permute-start(bf16[2,264,128]{2,1,0:T(8,128)(2,1)S(1)} %pad_maximum_fusion), channel_id=1, source_target_pairs={{0,2},{2,0},{1,3},{3,1},{4,6},{6,4},{5,7},{7,5},{8,10},{10,8},{9,1... | collective-permute-start | bytes 405512 | tf_op jit(solution)/shard_map/ppermute | solution.py:276
  21.1 1.6 %collective-permute-start.8 = (bf16[528,256]{1,0:T(8,128)(2,1)S(1)}, bf16[528,256]{1,0:T(8,128)(2,1)S(1)}, u32[]{:S(2)}, u32[]{:S(2)}) collective-permute-start(bf16[528,256]{1,0:T(8,128)(2,1)S(1)} %get-tuple-element.38.refs_4_.refs_8_), channel_id=1, source_target_pairs={{1,0},{0,1},{3,2},{2,3},{5,4},{4,5},{7,6},{6,7},{9,8},{8,9},{11,10... | collective-permute-start | bytes 811016 | tf_op jit(solution)/shard_map/ppermute | solution.py:469
  24.3 7.6 %collective-permute-start.11 = (bf16[264,128]{1,0:T(8,128)(2,1)S(1)}, bf16[264,128]{1,0:T(8,128)(2,1)S(1)}, u32[]{:S(2)}, u32[]{:S(2)}) collective-permute-start(bf16[264,128]{1,0:T(8,128)(2,1)S(1)} %get-tuple-element.43), channel_id=1, source_target_pairs={{0,8},{4,12},{8,0},{12,4},{1,9},{5,13},{9,1},{13,5},{2,10},{6,14},... | collective-permute-start | bytes 202760 | tf_op jit(solution)/shard_map/ppermute | solution.py:284
  25.3 9.6 %collective-permute-start.9 = (bf16[264,128]{1,0:T(8,128)(2,1)S(1)}, bf16[264,128]{1,0:T(8,128)(2,1)S(1)}, u32[]{:S(2)}, u32[]{:S(2)}) collective-permute-start(bf16[264,128]{1,0:T(8,128)(2,1)S(1)} %get-tuple-element.40), channel_id=1, source_target_pairs={{0,12},{4,8},{8,4},{12,0},{1,13},{5,9},{9,5},{13,1},{2,14},{6,10},... | collective-permute-start | bytes 202760 | tf_op jit(solution)/shard_map/ppermute | solution.py:284
  28.7 4.7 %collective-permute-start.12 = (bf16[264,128]{1,0:T(8,128)(2,1)S(1)}, bf16[264,128]{1,0:T(8,128)(2,1)S(1)}, u32[]{:S(2)}, u32[]{:S(2)}) collective-permute-start(bf16[264,128]{1,0:T(8,128)(2,1)S(1)} %get-tuple-element.44), channel_id=1, source_target_pairs={{0,4},{4,0},{8,12},{12,8},{1,5},{5,1},{9,13},{13,9},{2,6},{6,2},{1... | collective-permute-start | bytes 202760 | tf_op jit(solution)/shard_map/ppermute | solution.py:284
  28.7 6.9 %collective-permute-start.13 = (bf16[1,264,128]{2,1,0:T(8,128)(2,1)S(1)}, bf16[1,264,128]{2,1,0:T(8,128)(2,1)S(1)}, u32[]{:S(2)}, u32[]{:S(2)}) collective-permute-start(bf16[1,264,128]{2,1,0:T(8,128)(2,1)S(1)} %bitcast.14), channel_id=1, source_target_pairs={{0,2},{2,0},{1,3},{3,1},{4,6},{6,4},{5,7},{7,5},{8,10},{10,8},{9,1... | collective-permute-start | bytes 202760 | tf_op jit(solution)/shard_map/ppermute | solution.py:276
  31.9 4.7 %collective-permute-start.14 = (bf16[1,256,128]{2,1,0:T(8,128)(2,1)S(1)}, bf16[1,256,128]{2,1,0:T(8,128)(2,1)S(1)}, u32[]{:S(2)}, u32[]{:S(2)}) collective-permute-start(bf16[1,256,128]{2,1,0:T(8,128)(2,1)S(1)} %slice_bitcast_fusion.1), channel_id=1, source_target_pairs={{0,2},{2,0},{1,3},{3,1},{4,6},{6,4},{5,7},{7,5},{8,10},{10,8},{9,1... | collective-permute-start | bytes 196616 | tf_op jit(solution)/shard_map/ppermute | solution.py:276
  33.5 4.3 %collective-permute-start.15 = (bf16[1,256,128]{2,1,0:T(8,128)(2,1)S(1)}, bf16[1,256,128]{2,1,0:T(8,128)(2,1)S(1)}, u32[]{:S(2)}, u32[]{:S(2)}) collective-permute-start(bf16[1,256,128]{2,1,0:T(8,128)(2,1)S(1)} %slice_bitcast_fusion), channel_id=1, source_target_pairs={{0,2},{2,0},{1,3},{3,1},{4,6},{6,4},{5,7},{7,5},{8,10},{10,8},{9,1... | collective-permute-start | bytes 196616 | tf_op jit(solution)/shard_map/ppermute | solution.py:276
  34.9 4.3 %collective-permute-start.10 = (bf16[1,256,128]{2,1,0:T(8,128)(2,1)S(1)}, bf16[1,256,128]{2,1,0:T(8,128)(2,1)S(1)}, u32[]{:S(2)}, u32[]{:S(2)}) collective-permute-start(bf16[1,256,128]{2,1,0:T(8,128)(2,1)S(1)} %slice_bitcast_fusion.2), channel_id=1, source_target_pairs={{0,2},{2,0},{1,3},{3,1},{4,6},{6,4},{5,7},{7,5},{8,10},{10,8},{9,1... | collective-permute-start | bytes 196616 | tf_op jit(solution)/shard_map/ppermute | solution.py:276
